TPU v7x, 128 devices: a whole 4x4x4 slice. The times are simulated.
128 devices in a mesh: fsdp: 8 (over x_hi, z), tp: 8 (over y, core), grp: 2 (over x_lo).
Axes of the slice: x: 4 (x_hi: 2, x_lo: 2; x = x_hi * 2 + x_lo), y: 4, z: 4, core: 2. Of those that a mesh axis runs over, the one named last changes fastest.
Arguments:
- noisy_latents: bfloat16 [16, 256, 64], P(('fsdp', 'grp')), may hold values from -20 to 20
- student_step: int32 [16], replicated, may hold values from 1 to 4
- teacher_step: int32 [16], replicated, may hold values from 1 to 1000
- teacher_noise: bfloat16 [16, 256, 64], P(('fsdp', 'grp')), may hold values from -6 to 6
- layer_pick: int32 [16, 2], P(('fsdp', 'grp')), may hold values from 0 to 1
- in_proj_s: bfloat16 [64, 2432], P(None, 'tp'), may hold values from -3 to 3
- in_proj_t: bfloat16 [64, 2432], P(None, 'tp'), may hold values from -3 to 3
- out_proj: bfloat16 [64, 2432], P(None, 'tp'), may hold values from -0.125 to 0.125
- s_mod: bfloat16 [2432, 7296], P(('fsdp', 'grp'), 'tp'), may hold values from -0.25 to 0.25
- s_w1: bfloat16 [2432, 9728], P(('fsdp', 'grp'), 'tp'), may hold values from -0.125 to 0.125
- s_w2: bfloat16 [9728, 2432], P('tp', ('fsdp', 'grp')), may hold values from -0.0625 to 0.0625
- t_mod: bfloat16 [2, 2432, 7296], P(None, ('fsdp', 'grp'), 'tp'), may hold values from -0.125 to 0.125
- t_w1: bfloat16 [2, 2432, 9728], P(None, None, 'tp'), may hold values from -0.125 to 0.125
- t_w2: bfloat16 [2, 9728, 2432], P(None, 'tp'), may hold values from -0.0625 to 0.0625
- d_w1: bfloat16 [2432, 2432], P(('fsdp', 'grp'), 'tp'), may hold values from -0.125 to 0.125
- d_w2: float32 [2, 2432], P(None, 'tp'), may hold values from -0.6 to 0.6
Outputs:
- latents: bfloat16 [16, 256, 64], P(('fsdp', 'grp'))
- disc_scores: float32 [16, 2, 256], P(('fsdp', 'grp'))
- latent_grad: float32 [16, 256, 64], P(('fsdp', 'grp'))
All inputs are finite; a program needn't handle non-finite values.
Results may differ from a plain program's by a relative error of at most 0.03.
Values may be sent and summed in bfloat16 or wider, within the bound.
No kernel may reach another device: no remote copies, remote signals or barrier semaphores. Data moves between devices by JAX's collectives and lax.ppermute only.
A program may use at most 128 MiB of HBM per device.

v0:
```python
import functools
import math

import jax
import jax.numpy as jnp
from jax import lax
from jax.experimental import pallas as pl
from jax.experimental.pallas import tpu as pltpu
from jax.sharding import Mesh
from jax.sharding import PartitionSpec as P

HIGH = lax.Precision.HIGHEST
SAMPLE = ("fsdp", "grp")
TP = ("y", "core")
STEPS = 4
LAYERS = 2
BF = jnp.bfloat16
F32 = jnp.float32


def embed_block(times, width, block, start):
    half = width // 2
    column = start + jnp.arange(block)
    steps = jnp.where(column < half, column, column - half).astype(F32)
    freq = jnp.exp(-math.log(10000.0) * steps / half)
    angle = times[:, None] * freq[None, :]
    return jnp.where((column < half)[None, :], jnp.cos(angle), jnp.sin(angle))


def normalize(values):
    mean = jnp.mean(values, axis=-1, keepdims=True)
    centered = values - mean
    inverse = lax.rsqrt(jnp.mean(centered * centered, axis=-1, keepdims=True) + 1e-06)
    return (centered * inverse, inverse)


def ln_back(grad, normed, inverse):
    mean_grad = jnp.mean(grad, axis=-1, keepdims=True)
    mean_cross = jnp.mean(grad * normed, axis=-1, keepdims=True)
    return inverse * (grad - mean_grad - normed * mean_cross)


def gelu_both(values):
    inner = 0.7978845608 * (values + 0.044715 * values * values * values)
    tangent = jnp.tanh(inner)
    halved = 0.5 * (1.0 + tangent)
    slope = halved + 0.5 * values * (1.0 - tangent * tangent) * 0.7978845608 * (
        1.0 + 3.0 * 0.044715 * values * values
    )
    return values * halved, slope


def dot(left, right):
    return jnp.dot(left, right, preferred_element_type=F32)


def dot_back(left, right):
    return lax.dot_general(left, right, (((1,), (1,)), ((), ())), preferred_element_type=F32)


def dot_across(left, right):
    return lax.dot_general(left, right, (((0,), (0,)), ((), ())), preferred_element_type=F32)


def split(values):
    high = values.astype(BF)
    return high, (values - high.astype(F32)).astype(BF)


def sibling(values):
    return lax.ppermute(values, "core", [(0, 1), (1, 0)])


def swap_y(values):
    return lax.all_to_all(values, "y", 0, 0)


class Stream:
    def __init__(self, plan, sems):
        self.copies = [
            pltpu.make_async_copy(source, target, sems.at[index])
            for index, (source, target) in enumerate(plan)
        ]
        for copy in self.copies:
            copy.start()
        self.at = 0

    def next(self):
        self.copies[self.at].wait()
        self.at += 1


def matrices(layer, sources, target):
    return [(source.at[layer], target.at[side]) for side, source in enumerate(sources)]


def turned(values):
    extent = values.shape[1]
    row = lax.broadcasted_iota(jnp.int32, (extent, extent), 0)
    col = lax.broadcasted_iota(jnp.int32, (extent, extent), 1)
    return dot_back((row == col).astype(BF), values)


def product_kernel(at_ref, packed_ref, w1_ref, w2_ref, out_ref, bias_ref):
    blocks, columns, _ = packed_ref.shape
    rows, hidden = w1_ref.shape
    cells = out_ref.shape[0] // STEPS
    pick_row = lax.broadcasted_iota(jnp.int32, (rows, columns), 0)
    pick_col = lax.broadcasted_iota(jnp.int32, (rows, columns), 1)
    mine = (pick_col == pick_row + rows * at_ref[1]).astype(BF)
    total = jnp.zeros((columns, cells), F32)
    for block in range(blocks):
        total = total + packed_ref[block, :, :cells].astype(F32)
    mean = jnp.sum(total, axis=0, keepdims=True) / (blocks * columns)
    local = dot(mine, packed_ref[at_ref[0]])
    high, low = split(local[:, :cells] - mean)
    out_rows = local[:, 2 * cells : 3 * cells].astype(BF)

    def modulation(index):
        block = dot(mine, packed_ref[at_ref[2 * index + 2]]).astype(BF)[:, 3 * cells :]
        row = lax.broadcasted_iota(jnp.int32, (block.shape[1], 8), 0)
        kind = lax.broadcasted_iota(jnp.int32, (block.shape[1], 8), 1)
        want = (row == 3 * (kind + LAYERS) + at_ref[2 * index + 3]) & (kind < STEPS)
        return dot(block, want.astype(BF)).astype(BF)

    shift, scale, gate = modulation(0), modulation(1), modulation(2)
    cell_row = lax.broadcasted_iota(jnp.int32, (cells, cells * STEPS), 0)
    cell_col = lax.broadcasted_iota(jnp.int32, (cells, cells * STEPS), 1)
    by_cell = (cell_col // STEPS == cell_row).astype(BF)
    step_row = lax.broadcasted_iota(jnp.int32, (8, cells * STEPS), 0)
    step_col = lax.broadcasted_iota(jnp.int32, (8, cells * STEPS), 1)
    by_step = (step_col % STEPS == step_row).astype(BF)
    left_in = (dot(high, by_cell) + dot(low, by_cell)) * (1.0 + dot(scale, by_step))
    left_out = dot(out_rows, by_cell) * dot(gate, by_step)
    gap = -hidden % 128
    out_ref[:, :hidden] = dot_across(left_in.astype(BF), w1_ref[...]).astype(BF)
    out_ref[:, hidden : hidden + gap] = jnp.zeros((cells * STEPS, gap), BF)
    out_ref[:, hidden + gap :] = dot_across(left_out.astype(BF), w2_ref[...]).astype(BF)
    bias_ref[...] = dot_across(shift, w1_ref[...]).astype(BF)


def select_kernel(parts_ref, pick_ref, pick_bias_ref, bias_ref, out_ref):
    hidden = bias_ref.shape[1]
    total = parts_ref[0].astype(F32)
    for source in range(1, parts_ref.shape[0]):
        total = total + parts_ref[source].astype(F32)
    chosen = dot(pick_ref[...], total.astype(BF))
    out_ref[...] = chosen.astype(BF)
    out_ref[:, :hidden] = (chosen[:, :hidden] + dot(pick_bias_ref[...], bias_ref[...])).astype(BF)


def student_kernel(x_ref, inverse_ref, mat_ref, out_ref):
    cells = x_ref.shape[1]
    lanes, wide = mat_ref.shape
    hidden = wide // 2 - (wide // 2) % 64
    gap = wide - 2 * hidden
    group = lanes * 4 // cells
    row = lax.broadcasted_iota(jnp.int32, (cells, lanes), 0)
    col = lax.broadcasted_iota(jnp.int32, (cells, lanes), 1)
    spread = (col == group * (row // 4) + row % 4).astype(BF)
    bias_col = lax.broadcasted_iota(jnp.int32, (8, lanes), 1)
    bias = dot((bias_col % group == 4).astype(BF), mat_ref[:, :hidden])[:1]
    x = dot(x_ref[...], spread).astype(BF)
    z = inverse_ref[...] * dot(x, mat_ref[:, :hidden]) + bias
    active = gelu_both(z)[0].astype(BF)
    high, low = split(dot_back(active, mat_ref[:, hidden + gap :]))
    out_ref[...] = dot_back(high, spread) + dot_back(low, spread)


def first_product_kernel(proj_ref, scale_ref, shift_ref, up, out_ref, up_ref, sems):
    cells = proj_ref.shape[1]
    stream = Stream(matrices(0, (up,), up_ref), sems)
    proj = turned(proj_ref[...])
    centered = proj - jnp.mean(proj, axis=1, keepdims=True)
    left = (centered * (1.0 + scale_ref[...])).astype(BF)
    shift = jnp.broadcast_to(shift_ref[...], (16, shift_ref.shape[1])).astype(BF)
    left = jnp.concatenate([left, shift], axis=0)
    stream.next()
    out_ref[...] = dot_back(left, up_ref[0])[: cells + 8]


def first_forward_kernel(
    x_ref, proj_ref, mat_own, mat_sib, own, sib, y_out, slope_out, g_ref, back_ref, w_ref, y_ref, slope_ref, sems
):
    cells = x_ref.shape[1]
    stream = Stream(matrices(0, (own, sib), w_ref), sems)
    x = x_ref[...]
    g_0 = dot_back(x, proj_ref[...]).astype(BF)
    g_ref[...] = g_0
    normed, inverse = normalize(g_0.astype(F32))
    back_ref[:, :cells] = dot(normed.astype(BF), proj_ref[...])
    back_ref[:, cells:] = jnp.broadcast_to(inverse, (x.shape[0], cells))
    twice = jnp.concatenate([x, x], axis=1)
    actives = []
    for side, mat_ref in enumerate((mat_own, mat_sib)):
        high, low = split(mat_ref[:cells])
        z = inverse * dot(twice, jnp.concatenate([high, low], axis=0)) + mat_ref[cells : cells + 1]
        active, slope = gelu_both(z)
        slope_ref[side] = slope.astype(BF)
        actives.append(active.astype(BF))
    keep = pltpu.make_async_copy(slope_ref, slope_out, sems.at[2])
    keep.start()
    stream.next()
    y = dot(actives[0], w_ref[0])
    stream.next()
    y_ref[...] = (y + dot(actives[1], w_ref[1])).astype(BF)
    send = pltpu.make_async_copy(y_ref, y_out, sems.at[3])
    send.start()
    keep.wait()
    send.wait()


def resident_kernel(plan, *refs):
    sources, out_refs, sems = refs[: 2 * len(plan)], refs[2 * len(plan) : -1], refs[-1]
    copies = []
    for index, layer in enumerate(plan):
        copies += matrices(layer, sources[2 * index : 2 * index + 2], out_refs[index])
    stream = Stream(copies, sems)
    for _ in copies:
        stream.next()


def forward_kernel(
    g_ref, scale_ref, shift_ref, up_ref, down_ref, y_out, slope_out, y_ref, slope_ref, sems
):
    normed, _ = normalize(g_ref[...].astype(F32))
    u = (normed * (1.0 + scale_ref[...]) + shift_ref[...]).astype(BF)
    actives = []
    for side in range(2):
        active, slope = gelu_both(dot_back(u, up_ref[side]))
        slope_ref[side] = slope.astype(BF)
        actives.append(active.astype(BF))
    keep = pltpu.make_async_copy(slope_ref, slope_out, sems.at[0])
    keep.start()
    y_ref[...] = (dot(actives[0], down_ref[0]) + dot(actives[1], down_ref[1])).astype(BF)
    send = pltpu.make_async_copy(y_ref, y_out, sems.at[1])
    send.start()
    keep.wait()
    send.wait()


def backward_kernel(
    dy_ref, scale_ref, up_ref, down_ref, slope, head, out, slope_ref, head_ref, out_ref, sems
):
    stream = Stream([(slope, slope_ref), (head, head_ref)], sems)
    dy = dy_ref[...]
    da = dot_back(dy, down_ref[0])
    stream.next()
    dz_own = (da * slope_ref[0].astype(F32)).astype(BF)
    dz_sib = (dot_back(dy, down_ref[1]) * slope_ref[1].astype(F32)).astype(BF)
    du = dot(dz_own, up_ref[0]) + dot(dz_sib, up_ref[1])
    stream.next()
    out_ref[...] = (du * (1.0 + scale_ref[...]) + head_ref[...].astype(F32)).astype(BF)
    send = pltpu.make_async_copy(out_ref, out, sems.at[2])
    send.start()
    send.wait()


def first_backward_kernel(
    at_ref, rest_ref, dy_ref, x_ref, back_ref, score_ref, direct_ref, mat_own, mat_sib, down_ref, slope,
    out_ref, slope_ref, sems
):
    cells = x_ref.shape[1]
    stream = Stream([(slope, slope_ref)], sems)
    dy = dy_ref[...]
    total = None
    for side, mat_ref in enumerate((mat_own, mat_sib)):
        high, low = split(mat_ref[:cells])
        da = dot_back(dy, down_ref[side])
        if side == 0:
            stream.next()
        dz = (da * slope_ref[side].astype(F32)).astype(BF)
        part = dot_back(dz, high) + dot_back(dz, low)
        total = part if total is None else total + part
    inverse = back_ref[:, cells : cells + 1]
    cross = inverse * jnp.sum(x_ref[...].astype(F32) * total, axis=1, keepdims=True) / dy.shape[1]
    rest = rest_ref[0]
    out_ref[:, :cells] = rest * (inverse * (total - back_ref[:, :cells] * cross))
    out_ref[:, cells:] = score_ref[:, :cells]
    rows = direct_ref.shape[0]
    mine = pl.ds(pl.multiple_of(at_ref[0] * rows, rows), rows)
    out_ref[mine, :cells] += rest * direct_ref[...]


def modulation_kernel(cond_s_ref, cond_t_ref, s_ref, t_ref, out_ref):
    samples = cond_t_ref.shape[0]

    def product(cond, weight):
        extent = cond.shape[0]
        high, rest = split(cond)
        rest = cond - high.astype(F32)
        middle, low = split(rest)
        parts = dot(jnp.concatenate([high, middle, low], axis=0), weight)
        return (parts[:extent] + (parts[extent : 2 * extent] + parts[2 * extent :])).astype(BF)

    def place(extent, first, every):
        row = lax.broadcasted_iota(jnp.int32, (samples * 8, extent), 0)
        col = lax.broadcasted_iota(jnp.int32, (samples * 8, extent), 1)
        if every:
            return (row % 8 == first + col).astype(BF)
        return ((row // 8 == col) & (row % 8 == first)).astype(BF)

    total = dot(place(16, LAYERS, True), product(cond_s_ref[...], s_ref[...]))
    for layer in range(LAYERS):
        part = product(cond_t_ref[...], t_ref[layer])
        total = total + dot(place(samples, layer, False), part)
    out_ref[...] = total.astype(BF)


def sum_parts(parts_ref):
    total = parts_ref[0].astype(F32)
    for source in range(1, parts_ref.shape[0]):
        total = total + parts_ref[source].astype(F32)
    return total


def share(values, all_ref):
    for target in range(all_ref.shape[0]):
        all_ref[target] = values


def first_middle_kernel(at_ref, parts_ref, g_ref, gate_ref, mine_ref, all_ref):
    rows = mine_ref.shape[0]
    before = g_ref[pl.ds(pl.multiple_of(at_ref[0] * rows, rows), rows), :].astype(F32)
    after = (before + gate_ref[...] * sum_parts(parts_ref)).astype(BF)
    mine_ref[...] = after
    share(after, all_ref)


def last_middle_kernel(parts_ref, g_ref, gate_ref, mine_ref, all_ref):
    after = (g_ref[...].astype(F32) + gate_ref[...] * sum_parts(parts_ref)).astype(BF)
    mine_ref[...] = after
    share(after, all_ref)


def last_back_kernel(parts_ref, g_ref, gate_ref, grad_ref, all_ref):
    normed, inverse = normalize(g_ref[...].astype(F32))
    grad = ln_back(sum_parts(parts_ref), normed, inverse)
    grad_ref[...] = grad
    share((gate_ref[...] * grad).astype(BF), all_ref)


def first_back_kernel(parts_ref, g_ref, old_ref, gate_ref, proj_ref, direct_ref, all_ref):
    normed, inverse = normalize(g_ref[...].astype(F32))
    grad = old_ref[...] + ln_back(sum_parts(parts_ref), normed, inverse)
    direct_ref[...] = dot(grad.astype(BF), proj_ref[...])
    share((gate_ref[...] * grad).astype(BF), all_ref)


def head_kernel(g_ref, use_ref, own, sib, back_out, score_ref, weight_ref, back_ref, sems):
    stream = Stream([(own, weight_ref.at[0]), (sib, weight_ref.at[1])], sems)
    normed, _ = normalize(g_ref[...].astype(F32))
    quantised = normed.astype(BF)
    back = None
    scores = None
    for side in range(2):
        stream.next()
        weight = weight_ref[side]
        e = dot(quantised, weight)
        sigm = 1.0 / (1.0 + jnp.exp(-e))
        active = e * sigm
        outs = use_ref[side]
        slope = sigm * (1.0 + e * (1.0 - sigm))
        part = dot_back((-(outs[0:1] + outs[1:2]) * slope).astype(BF), weight)
        back = part if back is None else back + part
        part = [jnp.sum(active * outs[head : head + 1], axis=1, keepdims=True) for head in range(2)]
        scores = part if scores is None else [old + new for old, new in zip(scores, part)]
    back_ref[...] = back.astype(BF)
    send = pltpu.make_async_copy(back_ref, back_out, sems.at[2])
    send.start()
    lane = lax.broadcasted_iota(jnp.int32, score_ref.shape, 1)
    score_ref[...] = jnp.where(lane == 0, scores[0], 0.0) + jnp.where(lane == 1, scores[1], 0.0)
    send.wait()


WHOLE = pl.BlockSpec(memory_space=pltpu.VMEM)
FAR = pl.BlockSpec(memory_space=pltpu.HBM)


def here(kernel, name, out_shape, operands, scalars=0, far=0, far_out=(), scratch=(), limit=20):
    many = isinstance(out_shape, tuple)
    near = len(operands) - scalars - far
    specs = tuple(
        FAR if index in far_out else WHOLE for index in range(len(out_shape) if many else 1)
    )
    return pl.pallas_call(
        kernel,
        name=name,
        out_shape=out_shape,
        in_specs=[pl.BlockSpec(memory_space=pltpu.SMEM)] * scalars + [WHOLE] * near + [FAR] * far,
        out_specs=specs if many else specs[0],
        scratch_shapes=list(scratch),
        compiler_params=pltpu.CompilerParams(vmem_limit_bytes=limit * 2**20),
    )(*operands)


def resident(plan, sources):
    shapes = tuple(
        pltpu.VMEM((2,) + sources[2 * index].shape[1:], sources[2 * index].dtype)
        for index in range(len(plan))
    )
    return pl.pallas_call(
        functools.partial(resident_kernel, plan),
        name="resident",
        out_shape=shapes,
        in_specs=[FAR] * len(sources),
        out_specs=(WHOLE,) * len(plan),
        scratch_shapes=[pltpu.SemaphoreType.DMA((len(sources),))],
        compiler_params=pltpu.CompilerParams(vmem_limit_bytes=4 * 2**20),
    )(*sources)


def array(shape, dtype):
    return jax.ShapeDtypeStruct(shape, dtype)


def body(
    noisy_latents,
    student_step,
    teacher_step,
    teacher_noise,
    layer_pick,
    in_proj_s,
    in_proj_t,
    out_proj,
    s_mod,
    s_w1,
    s_w2,
    t_mod,
    t_w1,
    t_w2,
    d_w1,
    d_w2,
):
    cells = in_proj_s.shape[0]
    width = in_proj_s.shape[1] * 8
    samples = student_step.shape[0]
    layers = t_w1.shape[0]
    heads = d_w2.shape[0]
    seq = noisy_latents.shape[1]
    half = seq // 2
    quarter = half // 4
    rows = s_mod.shape[0]
    hidden = s_w1.shape[1]
    columns = in_proj_s.shape[1]
    sample = lax.axis_index(SAMPLE)
    at_y = lax.axis_index("y")
    at_core = lax.axis_index("core")
    start = sample * rows

    sig_all_t = teacher_step.astype(F32) * 0.001
    sig_steps = (1 + jnp.arange(STEPS)).astype(F32) * 0.25
    cond_s = jax.nn.silu(embed_block(1000.0 * sig_steps, width, rows, start))
    cond_t = jax.nn.silu(embed_block(1000.0 * sig_all_t, width, rows, start))
    mod_part = here(
        modulation_kernel,
        "modulation",
        array((samples * 8, s_mod.shape[1]), BF),
        (jnp.pad(cond_s, ((0, 16 - STEPS), (0, 0))), cond_t, s_mod, t_mod),
    ).reshape(samples, 8, s_mod.shape[1])
    mods = jnp.sum(lax.all_to_all(mod_part, SAMPLE, 0, 0).astype(F32), axis=0)
    kinds = layers + STEPS
    mods = mods[:kinds].reshape(kinds * 3, columns).astype(BF)
    packed = jnp.concatenate([in_proj_s, in_proj_t, out_proj, mods], axis=0).T
    gathered = lax.all_gather(packed, TP, axis=0, tiled=False)

    block = lax.axis_index(SAMPLE) * rows // columns
    places = [block, sample * rows // rows % (columns // rows)]
    for offset in (0, 8, 16):
        places += [(block + offset) // 3, (block + offset) % 3]
    gap = -hidden % 128
    both_wide = 2 * hidden + gap
    parts, part_bias = here(
        product_kernel,
        "product",
        (
            jax.ShapeDtypeStruct((cells * STEPS, both_wide), BF),
            jax.ShapeDtypeStruct((8, hidden), BF),
        ),
        (jnp.stack(places).astype(jnp.int32), gathered, s_w1, s_w2.T),
        scalars=1,
    )
    piece = cells * STEPS // samples
    chunk = cells // samples
    t_w1 = jnp.swapaxes(t_w1, 1, 2)
    parts, gathered, t_w1, t_w2 = lax.optimization_barrier((parts, gathered, t_w1, t_w2))
    received = lax.all_to_all(parts.reshape(samples, piece, both_wide), SAMPLE, 0, 0)

    mods = gathered[:, :, 3 * cells :].astype(F32).reshape(8, columns, kinds, 3)
    mod_teacher = mods[:, :, :layers].transpose(2, 0, 3, 1).reshape(layers, 1, 3 * width)
    packed = gathered.reshape(width, -1)
    proj_s, proj_t, proj_out = (packed[:, at * cells : (at + 1) * cells] for at in range(3))
    shifts = [mod_teacher[l, :, :width] for l in range(layers)]
    scales = [mod_teacher[l, :, width : 2 * width] for l in range(layers)]
    gates = [mod_teacher[l, :, 2 * width :] for l in range(layers)]
    first_own = here(
        first_product_kernel,
        "first_product",
        array((cells + 8, hidden), F32),
        (proj_t, scales[0], shifts[0], t_w1),
        far=1,
        scratch=(pltpu.VMEM((1, hidden, width), BF), pltpu.SemaphoreType.DMA((1,))),
    )
    latent_in = noisy_latents[0]
    h0 = dot_back(latent_in, proj_s).astype(BF)
    _, inverse_s = normalize(h0.astype(F32))
    received, first_own, inverse_s = lax.optimization_barrier((received, first_own, inverse_s))

    w2_sib = sibling(t_w2)
    w1_sib = sibling(t_w1)

    at_row = jnp.arange(samples * 8)
    step_at = jnp.repeat(student_step - 1, 8)
    pick = (
        ((at_row % 8 * STEPS + step_at)[:, None] == jnp.arange(piece)[None])
        & (at_row % 8 < chunk)[:, None]
    ).astype(BF)
    pick_bias = ((step_at[:, None] == jnp.arange(8)[None]) & (at_row % 8 == chunk)[:, None]).astype(BF)
    chosen = here(
        select_kernel,
        "select",
        jax.ShapeDtypeStruct((samples * 8, both_wide), BF),
        (received, pick, pick_bias, part_bias),
    )
    mine = lax.all_to_all(chosen.reshape(samples, 8, both_wide), SAMPLE, 0, 0)
    mine = mine.reshape(samples * 8, both_wide)
    my_step = lax.dynamic_index_in_dim(student_step, sample, keepdims=False)

    spare = -columns % 128
    head_block, _ = lax.optimization_barrier((jnp.pad(d_w1, ((0, 0), (0, spare))), mine))
    head_own = lax.all_gather(head_block, SAMPLE, axis=0, tiled=True)

    sigma_s = my_step.astype(F32) * 0.25
    sigma_t = lax.dynamic_index_in_dim(sig_all_t, sample, keepdims=False)
    velocity = here(
        student_kernel,
        "student",
        jax.ShapeDtypeStruct((seq, cells), F32),
        (latent_in, inverse_s, mine),
    )
    mine_first = lax.dynamic_slice_in_dim(velocity, at_core * half, half, 0)
    other = lax.dynamic_slice_in_dim(velocity, (1 - at_core) * half, half, 0)
    velocity = mine_first + sibling(other)
    velocity = velocity + lax.ppermute(velocity, "y", [(0, 1), (1, 0), (2, 3), (3, 2)])
    velocity = velocity + lax.ppermute(velocity, "y", [(0, 2), (2, 0), (1, 3), (3, 1)])

    def my_half(values):
        return lax.dynamic_slice_in_dim(values, at_core * half, half, 0)

    velocity = velocity + dot(my_half(h0), proj_out)
    latents = (my_half(latent_in).astype(F32) - sigma_s * velocity).astype(BF)
    noised = (
        (1.0 - sigma_t) * latents.astype(F32) + sigma_t * my_half(teacher_noise[0]).astype(F32)
    ).astype(BF)

    def both(values):
        other = sibling(values)
        first = jnp.where(at_core == 0, values, other)
        second = jnp.where(at_core == 0, other, values)
        return jnp.concatenate([first, second], axis=0)

    latents = both(latents)

    first_sib = sibling(first_own)

    token_rows = pltpu.VMEM((half, width), BF)
    inner = pltpu.VMEM((2, half, hidden), BF)
    rows_out = array((4, quarter, width), BF)
    mine_out = array((quarter, width), BF)
    inner_out = array((2, half, hidden), BF)
    y_0, slope_0, g_0, back_0 = here(
        first_forward_kernel,
        "first_forward",
        (array((half, width), BF), inner_out, array((half, width), BF), array((half, 2 * cells), F32)),
        (noised, proj_t, first_own, first_sib, t_w2, w2_sib),
        far=2,
        far_out=(0, 1),
        scratch=(
            pltpu.VMEM((2, hidden, width), BF),
            token_rows,
            inner,
            pltpu.SemaphoreType.DMA((4,)),
        ),
        limit=32,
    )

    def sums(partial, plan, sources):
        parts = swap_y(partial.reshape(4, quarter, width))
        sources, _ = lax.optimization_barrier((sources, partial))
        weights = resident(plan, sources)
        parts, weights = lax.optimization_barrier((parts, weights))
        return parts, weights

    last = (t_w1, w1_sib, t_w2, w2_sib)
    parts, weights = sums(y_0, (1, 1), last)
    g_1_mine, g_1 = here(
        first_middle_kernel,
        "first_middle",
        (mine_out, rows_out),
        (at_y.reshape(1), parts, g_0, gates[0]),
        scalars=1,
    )
    g_1 = swap_y(g_1).reshape(half, width)
    y_1, slope_1 = here(
        forward_kernel,
        "forward",
        (array((half, width), BF), inner_out),
        (g_1, scales[1], shifts[1]) + tuple(weights),
        far_out=(0, 1),
        scratch=(token_rows, inner, pltpu.SemaphoreType.DMA((2,))),
    )
    g_2_mine, g_2 = here(
        last_middle_kernel,
        "last_middle",
        (mine_out, rows_out),
        (swap_y(y_1.reshape(4, quarter, width)), g_1_mine, gates[1]),
    )
    head_own, d_w2_late, _ = lax.optimization_barrier((head_own, d_w2, g_2_mine))
    head_sib = sibling(head_own)
    d_w2_sib = sibling(d_w2_late)
    g_2 = swap_y(g_2).reshape(half, width)

    outs = jnp.pad(jnp.stack([d_w2, d_w2_sib]), ((0, 0), (0, 0), (0, spare)))
    use = [outs * (layer_pick[0] == layer).astype(F32)[None, :, None] for layer in range(layers)]

    def head(name, g, use):
        return here(
            head_kernel,
            name,
            (array((half, width), BF), array((half, 128), F32)),
            (g, use, head_own, head_sib),
            far=2,
            far_out=(0,),
            scratch=(
                pltpu.VMEM((2,) + head_own.shape, BF),
                token_rows,
                pltpu.SemaphoreType.DMA((3,)),
            ),
        )

    head_back_2, scores_2 = head("head_last", g_2, use[1])

    parts, weights = sums(head_back_2, (1, 1), last)
    dg_2, dy_1 = here(
        last_back_kernel,
        "last_back",
        (array((quarter, width), F32), rows_out),
        (parts, g_2_mine, gates[1]),
    )
    g_1, _ = lax.optimization_barrier((g_1, dg_2))
    head_back_1, scores_1 = head("head_first", g_1, use[0])
    du_1 = here(
        backward_kernel,
        "backward",
        array((half, width), BF),
        (swap_y(dy_1).reshape(half, width), scales[1]) + tuple(weights) + (slope_1, head_back_1),
        far=2,
        far_out=(0,),
        scratch=(inner, token_rows, token_rows, pltpu.SemaphoreType.DMA((3,))),
    )
    parts, weights = sums(du_1, (0,), (t_w2, w2_sib))
    direct, dy_0 = here(
        first_back_kernel,
        "first_back",
        (array((quarter, cells), F32), rows_out),
        (parts, g_1_mine, dg_2, gates[0], proj_t),
    )
    final = here(
        first_backward_kernel,
        "first_backward",
        array((half, 2 * cells), F32),
        (
            at_y.reshape(1),
            (1.0 - sigma_t).reshape(1),
            swap_y(dy_0).reshape(half, width),
            noised,
            back_0,
            scores_1 + scores_2,
            direct,
            first_own,
            first_sib,
        )
        + tuple(weights)
        + (slope_0,),
        scalars=2,
        far=1,
        scratch=(inner, pltpu.SemaphoreType.DMA((1,))),
    )
    final = final + lax.ppermute(final, "y", [(0, 1), (1, 0), (2, 3), (3, 2)])
    final = final + lax.ppermute(final, "y", [(0, 2), (2, 0), (1, 3), (3, 1)])
    final = both(final)
    return (latents[None], final[:, cells : cells + heads].T[None], final[:, :cells][None])


def solution(mesh):
    names = list(mesh.axis_names)
    shape = list(mesh.devices.shape)
    at = names.index("tp")
    names[at : at + 1] = ["y", "core"]
    shape[at : at + 1] = [4, 2]
    fine = Mesh(mesh.devices.reshape(shape), tuple(names))
    placed = (
        P(SAMPLE, None, None),
        P(),
        P(),
        P(SAMPLE, None, None),
        P(SAMPLE, None),
        P(None, TP),
        P(None, TP),
        P(None, TP),
        P(SAMPLE, TP),
        P(SAMPLE, TP),
        P(TP, SAMPLE),
        P(None, SAMPLE, TP),
        P(None, None, TP),
        P(None, TP, None),
        P(SAMPLE, TP),
        P(None, TP),
    )
    return jax.shard_map(
        body,
        mesh=fine,
        in_specs=placed,
        out_specs=(P(SAMPLE, None, None), P(SAMPLE, None, None), P(SAMPLE, None, None)),
        check_vma=False,
    )
```

profile of v0, /device:TPU:1, one launch (start us, length us, event | category | flops | bytes accessed | tf_op | source)
XLA Modules:
  0.0 334.8 jit_solution(12462646542855537789)
XLA Ops:
  10.2 1.4 modulation.1
  11.7 8.4 %all-to-all-start = ((bf16[16,8,912]{2,1,0:T(8,128)(2,1)}), bf16[16,8,912]{2,1,0:T(8,128)(2,1)S(1)}, u32[]{:S(2)}, u32[]{:S(2)}) async-start(bf16[16,8,912]{2,1,0:T(8,128)(2,1)} %bitcast.11), calls=%async_computation | async-start | bytes 524288 | tf_op jit(solution)/shard_map/all_to_all | solution.py:461
  23.1 4.7 %all-to-all-done = bf16[16,8,912]{2,1,0:T(8,128)(2,1)S(1)} async-done(((bf16[16,8,912]{2,1,0:T(8,128)(2,1)}), bf16[16,8,912]{2,1,0:T(8,128)(2,1)S(1)}, u32[]{:S(2)}, u32[]{:S(2)}) %all-to-all-start) | async-done | bytes 233504 | tf_op jit(solution)/shard_map/all_to_all | solution.py:461
  28.2 16.5 %all-gather = bf16[2432,210]{1,0:T(8,128)(2,1)S(1)} all-gather(bf16[304,210]{1,0:T(8,128)(2,1)S(1)} %maximum_bitcast_fusion), channel_id=2, replica_groups=mesh['fsdp'=8,'y'=4,'core'=2,'grp'=2] {'y','core'}, dimensions={0}, use_global_device_ids=true | all-gather | bytes 1149120 | tf_op jit(solution)/shard_map/all_gather | solution.py:465
  44.8 2.0 product.1
  46.7 1.2 copy-done.26
  48.8 3.7 %all-to-all-start.1 = ((bf16[16,16,2496]{2,1,0:T(8,128)(2,1)}), bf16[16,16,2496]{2,1,0:T(8,128)(2,1)S(1)}, u32[]{:S(2)}, u32[]{:S(2)}) async-start(bf16[16,16,2496]{2,1,0:T(8,128)(2,1)} %bitcast.86), calls=%async_computation.1 | async-start | bytes 2621440 | tf_op jit(solution)/shard_map/all_to_all | solution.py:487
  54.2 4.4 %copy-done.4 = bf16[2,2432,1216]{1,2,0:T(8,128)(2,1)S(1)} copy-done((bf16[2,2432,1216]{1,2,0:T(8,128)(2,1)S(1)}, bf16[2,2432,1216]{1,2,0:T(8,128)(2,1)}, u32[]{:S(2)}) %copy-start.4) | copy-done | bytes 11829272
  58.6 2.9 first_product.1.mat_own
  63.2 10.7 %all-to-all-done.1.parts_ref = bf16[16,16,2496]{2,1,0:T(8,128)(2,1)S(1)} async-done(((bf16[16,16,2496]{2,1,0:T(8,128)(2,1)}), bf16[16,16,2496]{2,1,0:T(8,128)(2,1)S(1)}, u32[]{:S(2)}, u32[]{:S(2)}) %all-to-all-start.1) | async-done | bytes 1277984 | tf_op jit(solution)/shard_map/all_to_all | solution.py:487
  75.2 4.3 %all-to-all-start.2 = ((bf16[16,8,2496]{2,1,0:T(8,128)(2,1)}), bf16[16,8,2496]{2,1,0:T(8,128)(2,1)S(1)}, u32[]{:S(2)}, u32[]{:S(2)}) async-start(bf16[16,8,2496]{2,1,0:T(8,128)(2,1)} %bitcast.84), calls=%async_computation.2 | async-start | bytes 1310720 | tf_op jit(solution)/shard_map/all_to_all | solution.py:525
  79.6 1.6 pad.13
  81.2 9.8 %all-to-all-done.2 = bf16[16,8,2496]{2,1,0:T(8,128)(2,1)S(1)} async-done(((bf16[16,8,2496]{2,1,0:T(8,128)(2,1)}), bf16[16,8,2496]{2,1,0:T(8,128)(2,1)S(1)}, u32[]{:S(2)}, u32[]{:S(2)}) %all-to-all-start.2) | async-done | bytes 639008 | tf_op jit(solution)/shard_map/all_to_all | solution.py:525
  92.4 2.6 collective-permute-start
  95.9 1.1 collective-permute-start.1
  100.3 2.7 collective-permute-start.2
  103.0 1.4 fusion.2
  104.4 1.2 collective-permute-done.2
  105.6 1.3 fusion.8
  106.9 4.5 %copy-done.2 = bf16[2,1216,2432]{2,1,0:T(8,128)(2,1)S(1)} copy-done((bf16[2,1216,2432]{2,1,0:T(8,128)(2,1)S(1)}, bf16[2,1216,2432]{2,1,0:T(8,128)(2,1)}, u32[]{:S(2)}) %copy-start.2) | copy-done | bytes 11829272
  111.4 6.2 %first_forward.1 = (bf16[128,2432]{1,0:T(8,128)(2,1)}, bf16[2,128,1216]{2,1,0:T(8,128)(2,1)S(1)}, bf16[128,2432]{1,0:T(8,128)(2,1)S(1)}, f32[128,128]{1,0:T(8,128)S(1)}) custom-call(bf16[128,64]{1,0:T(8,128)(2,1)S(1)} %get-tuple-element.124.x_ref, bf16[2432,64]{1,0:T(8,128)(2,1)S(1)} %slice.59.proj_ref, f32[72,1216]{1,0:T(8,128)S(1)} %copy-done.22, ...), custom_call_target="tpu_custom_call" | custom-call | tf_op jit(solution)/shard_map/first_forward/pallas_call | solution.py:386
  119.1 4.0 %all-to-all-start.3 = ((bf16[4,32,2432]{2,1,0:T(8,128)(2,1)}), bf16[4,32,2432]{2,1,0:T(8,128)(2,1)S(1)}, u32[]{:S(2)}, u32[]{:S(2)}) async-start(bf16[4,32,2432]{2,1,0:T(8,128)(2,1)} %bitcast.30), calls=%async_computation.3 | async-start | bytes 1245184 | tf_op jit(solution)/shard_map/all_to_all | solution.py:75
  123.1 4.4 %copy-done.5 = bf16[2,2432,1216]{1,2,0:T(8,128)(2,1)S(1)} copy-done((bf16[2,2432,1216]{1,2,0:T(8,128)(2,1)S(1)}, bf16[2,2432,1216]{1,2,0:T(8,128)(2,1)}, u32[]{:S(2)}) %copy-start.5) | copy-done | bytes 11829272
  127.5 6.8 %resident.3 = (bf16[2,1216,2432]{2,1,0:T(8,128)(2,1)S(1)}, bf16[2,1216,2432]{2,1,0:T(8,128)(2,1)S(1)}) custom-call(bf16[2,1216,2432]{2,1,0:T(8,128)(2,1)S(1)} %bitcast.77, bf16[2,1216,2432]{2,1,0:T(8,128)(2,1)} %collective-permute-done.6.refs_1_, bf16[2,1216,2432]{2,1,0:T(8,128)(2,1)} %refs_0_, bf16[2,1216,2432]{2,1,0:T(8,128)(2,1)} %collective-permute-done.5.sib.refs_3_.refs_1_), custom_call_target="tpu_custom_call" | custom-call | tf_op jit(solution)/shard_map/resident/pallas_call | solution.py:402
  134.3 4.3 %copy-done.13 = bf16[2,1216,2432]{2,1,0:T(8,128)(2,1)} copy-done((bf16[2,1216,2432]{2,1,0:T(8,128)(2,1)}, bf16[2,1216,2432]{2,1,0:T(8,128)(2,1)S(1)}, u32[]{:S(2)}) %copy-start.13) | copy-done | bytes 11829272
  138.6 4.4 %copy-done.15 = bf16[2,1216,2432]{2,1,0:T(8,128)(2,1)} copy-done((bf16[2,1216,2432]{2,1,0:T(8,128)(2,1)}, bf16[2,1216,2432]{2,1,0:T(8,128)(2,1)S(1)}, u32[]{:S(2)}) %copy-start.15) | copy-done | bytes 11829272
  143.1 13.2 %all_to_all.55 = bf16[4,32,2432]{2,1,0:T(8,128)(2,1)S(1)} all-to-all(bf16[4,32,2432]{2,1,0:T(8,128)(2,1)S(1)} %get-tuple-element.74), channel_id=1, replica_groups=mesh['fsdp'=8,'y'=4,'core'=2,'grp'=2] {'y'}, dimensions={0} | all-to-all | bytes 1245184 | tf_op jit(solution)/shard_map/all_to_all | solution.py:75
  156.4 4.4 %copy-done.14 = bf16[2,1216,2432]{2,1,0:T(8,128)(2,1)S(1)} copy-done((bf16[2,1216,2432]{2,1,0:T(8,128)(2,1)S(1)}, bf16[2,1216,2432]{2,1,0:T(8,128)(2,1)}, u32[]{:S(2)}) %copy-start.14) | copy-done | bytes 11829272
  160.7 4.4 %copy-done.16 = bf16[2,1216,2432]{2,1,0:T(8,128)(2,1)S(1)} copy-done((bf16[2,1216,2432]{2,1,0:T(8,128)(2,1)S(1)}, bf16[2,1216,2432]{2,1,0:T(8,128)(2,1)}, u32[]{:S(2)}) %copy-start.16) | copy-done | bytes 11829272
  165.1 6.6 %forward.1 = (bf16[128,2432]{1,0:T(8,128)(2,1)S(1)}, bf16[2,128,1216]{2,1,0:T(8,128)(2,1)S(1)}) custom-call(bf16[128,2432]{1,0:T(8,128)(2,1)S(1)} %bitcast.81, f32[1,2432]{1,0:T(1,128)S(1)} %copy-done.50, f32[1,2432]{1,0:T(1,128)S(1)} %copy-done.58, bf16[2,1216,2432]{2,1,0:T(8,128)(2,1)S(1)} %copy-done.14, bf16[2,1216,2432]{2,1,0:T(8,128)(2,1)S(1)} %copy-done.16), custom_call_target="tpu_custom_call" | custom-call | tf_op jit(solution)/shard_map/forward/pallas_call | solution.py:386
  172.5 10.8 %all_to_all.56.parts_ref = bf16[4,32,2432]{2,1,0:T(8,128)(2,1)S(1)} all-to-all(bf16[4,32,2432]{2,1,0:T(8,128)(2,1)S(1)} %bitcast.88), channel_id=1, replica_groups=mesh['fsdp'=8,'y'=4,'core'=2,'grp'=2] {'y'}, dimensions={0} | all-to-all | bytes 1245184 | tf_op jit(solution)/shard_map/all_to_all | solution.py:75
  184.9 3.2 collective-permute-start.8
  188.1 4.2 %all-to-all-start.6 = ((bf16[4,32,2432]{2,1,0:T(8,128)(2,1)}), bf16[4,32,2432]{2,1,0:T(8,128)(2,1)}, u32[]{:S(2)}, u32[]{:S(2)}) async-start(bf16[4,32,2432]{2,1,0:T(8,128)(2,1)} %copy-done.34), calls=%async_computation.6 | async-start | bytes 1245184 | tf_op jit(solution)/shard_map/all_to_all | solution.py:75
  192.6 1.1 collective-permute-done.7
  193.8 9.2 %all-to-all-done.6 = bf16[4,32,2432]{2,1,0:T(8,128)(2,1)} async-done(((bf16[4,32,2432]{2,1,0:T(8,128)(2,1)}), bf16[4,32,2432]{2,1,0:T(8,128)(2,1)}, u32[]{:S(2)}, u32[]{:S(2)}) %all-to-all-start.6) | async-done | bytes 622624 | tf_op jit(solution)/shard_map/all_to_all | solution.py:75
  203.1 2.2 copy-done.17
  205.2 4.4 %head_last.1 = (bf16[128,2432]{1,0:T(8,128)(2,1)S(1)}, f32[128,128]{1,0:T(8,128)S(1)}) custom-call(bf16[128,2432]{1,0:T(8,128)(2,1)} %bitcast.37.g_ref, f32[2,2,384]{2,1,0:T(2,128)S(1)} %get-tuple-element.137.use_ref, bf16[2432,384]{1,0:T(8,128)(2,1)S(1)} %copy-done.17, bf16[2432,384]{1,0:T(8,128)(2,1)S(1)} %collective-permute-done.8.sib), custom_call_target="tpu_custom_call" | custom-call | tf_op jit(solution)/shard_map/head_last/pallas_call | solution.py:386
  211.1 4.1 %all-to-all-start.7 = ((bf16[4,32,2432]{2,1,0:T(8,128)(2,1)}), bf16[4,32,2432]{2,1,0:T(8,128)(2,1)}, u32[]{:S(2)}, u32[]{:S(2)}) async-start(bf16[4,32,2432]{2,1,0:T(8,128)(2,1)} %bitcast.87), calls=%async_computation.7 | async-start | bytes 1245184 | tf_op jit(solution)/shard_map/all_to_all | solution.py:75
  215.2 4.4 %copy-done.6 = bf16[2,2432,1216]{1,2,0:T(8,128)(2,1)S(1)} copy-done((bf16[2,2432,1216]{1,2,0:T(8,128)(2,1)S(1)}, bf16[2,2432,1216]{1,2,0:T(8,128)(2,1)}, u32[]{:S(2)}) %copy-start.6) | copy-done | bytes 11829272
  219.6 6.7 %resident.4 = (bf16[2,1216,2432]{2,1,0:T(8,128)(2,1)S(1)}, bf16[2,1216,2432]{2,1,0:T(8,128)(2,1)S(1)}) custom-call(bf16[2,1216,2432]{2,1,0:T(8,128)(2,1)S(1)} %bitcast.78, bf16[2,1216,2432]{2,1,0:T(8,128)(2,1)} %collective-permute-done.6.refs_1_, bf16[2,1216,2432]{2,1,0:T(8,128)(2,1)} %refs_0_, bf16[2,1216,2432]{2,1,0:T(8,128)(2,1)} %collective-permute-done.5.sib.refs_3_.refs_1_), custom_call_target="tpu_custom_call" | custom-call | tf_op jit(solution)/shard_map/resident/pallas_call | solution.py:402
  226.3 4.3 %copy-done.9 = bf16[2,1216,2432]{2,1,0:T(8,128)(2,1)} copy-done((bf16[2,1216,2432]{2,1,0:T(8,128)(2,1)}, bf16[2,1216,2432]{2,1,0:T(8,128)(2,1)S(1)}, u32[]{:S(2)}) %copy-start.9) | copy-done | bytes 11829272
  230.6 4.3 %copy-done.11 = bf16[2,1216,2432]{2,1,0:T(8,128)(2,1)} copy-done((bf16[2,1216,2432]{2,1,0:T(8,128)(2,1)}, bf16[2,1216,2432]{2,1,0:T(8,128)(2,1)S(1)}, u32[]{:S(2)}) %copy-start.11) | copy-done | bytes 11829272
  235.9 1.5 last_back.1
  238.9 4.3 %all-to-all-start.8 = ((bf16[4,32,2432]{2,1,0:T(8,128)(2,1)}), bf16[4,32,2432]{2,1,0:T(8,128)(2,1)}, u32[]{:S(2)}, u32[]{:S(2)}) async-start(bf16[4,32,2432]{2,1,0:T(8,128)(2,1)} %copy-done.35), calls=%async_computation.8 | async-start | bytes 1245184 | tf_op jit(solution)/shard_map/all_to_all | solution.py:75
  243.3 1.5 copy-done.20
  244.8 3.3 head_first.1
  249.6 2.7 all-to-all-done.8
  252.3 4.4 %copy-done.10 = bf16[2,1216,2432]{2,1,0:T(8,128)(2,1)S(1)} copy-done((bf16[2,1216,2432]{2,1,0:T(8,128)(2,1)S(1)}, bf16[2,1216,2432]{2,1,0:T(8,128)(2,1)}, u32[]{:S(2)}) %copy-start.10) | copy-done | bytes 11829272
  256.7 4.4 %copy-done.12 = bf16[2,1216,2432]{2,1,0:T(8,128)(2,1)S(1)} copy-done((bf16[2,1216,2432]{2,1,0:T(8,128)(2,1)S(1)}, bf16[2,1216,2432]{2,1,0:T(8,128)(2,1)}, u32[]{:S(2)}) %copy-start.12) | copy-done | bytes 11829272
  261.0 1.1 copy-done.30
  263.2 8.6 %backward.1 = bf16[128,2432]{1,0:T(8,128)(2,1)} custom-call(bf16[128,2432]{1,0:T(8,128)(2,1)} %bitcast.42.dy_ref, f32[1,2432]{1,0:T(1,128)S(1)} %copy-done.51, bf16[2,1216,2432]{2,1,0:T(8,128)(2,1)S(1)} %copy-done.10, bf16[2,1216,2432]{2,1,0:T(8,128)(2,1)S(1)} %copy-done.12, bf16[2,128,1216]{2,1,0:T(8,128)(2,1)S(1)} %copy-done.30, ...), custom_call_target="tpu_custom_call" | custom-call | tf_op jit(solution)/shard_map/backward/pallas_call | solution.py:386
  271.8 3.5 %all-to-all-start.9 = ((bf16[4,32,2432]{2,1,0:T(8,128)(2,1)}), bf16[4,32,2432]{2,1,0:T(8,128)(2,1)S(1)}, u32[]{:S(2)}, u32[]{:S(2)}) async-start(bf16[4,32,2432]{2,1,0:T(8,128)(2,1)} %bitcast.44), calls=%async_computation.9 | async-start | bytes 1245184 | tf_op jit(solution)/shard_map/all_to_all | solution.py:75
  275.3 4.4 %copy-done.3 = bf16[2,1216,2432]{2,1,0:T(8,128)(2,1)S(1)} copy-done((bf16[2,1216,2432]{2,1,0:T(8,128)(2,1)S(1)}, bf16[2,1216,2432]{2,1,0:T(8,128)(2,1)}, u32[]{:S(2)}) %copy-start.3) | copy-done | bytes 11829272
  279.7 3.3 resident.5.down_ref
  283.0 4.3 %copy-done.7 = bf16[2,1216,2432]{2,1,0:T(8,128)(2,1)} copy-done((bf16[2,1216,2432]{2,1,0:T(8,128)(2,1)}, bf16[2,1216,2432]{2,1,0:T(8,128)(2,1)S(1)}, u32[]{:S(2)}) %copy-start.7) | copy-done | bytes 11829272
  287.4 1.2 first_back.1
  288.6 4.2 %all-to-all-start.10 = ((bf16[4,32,2432]{2,1,0:T(8,128)(2,1)}), bf16[4,32,2432]{2,1,0:T(8,128)(2,1)S(1)}, u32[]{:S(2)}, u32[]{:S(2)}) async-start(bf16[4,32,2432]{2,1,0:T(8,128)(2,1)} %get-tuple-element.102), calls=%async_computation.10 | async-start | bytes 1245184 | tf_op jit(solution)/shard_map/all_to_all | solution.py:75
  292.9 7.4 %all-to-all-done.10 = bf16[4,32,2432]{2,1,0:T(8,128)(2,1)S(1)} async-done(((bf16[4,32,2432]{2,1,0:T(8,128)(2,1)}), bf16[4,32,2432]{2,1,0:T(8,128)(2,1)S(1)}, u32[]{:S(2)}, u32[]{:S(2)}) %all-to-all-start.10) | async-done | bytes 622624 | tf_op jit(solution)/shard_map/all_to_all | solution.py:75
  300.3 4.4 %copy-done.8 = bf16[2,1216,2432]{2,1,0:T(8,128)(2,1)S(1)} copy-done((bf16[2,1216,2432]{2,1,0:T(8,128)(2,1)S(1)}, bf16[2,1216,2432]{2,1,0:T(8,128)(2,1)}, u32[]{:S(2)}) %copy-start.8) | copy-done | bytes 11829272
  304.7 5.7 %first_backward.1 = f32[128,128]{1,0:T(8,128)S(1)} custom-call(s32[1]{0:T(128)} %bitcast.26.at_ref, f32[1]{0:T(128)} %bitcast.28.rest_ref, bf16[128,2432]{1,0:T(8,128)(2,1)S(1)} %bitcast.85, bf16[128,64]{1,0:T(8,128)(2,1)S(1)} %get-tuple-element.124.x_ref, f32[128,128]{1,0:T(8,128)S(1)} %copy-done.53, f32[128,128]{1,0:T(8,128)S(1)} %add.181.score_ref, ...), custom_call_target="tpu_custom_call" | custom-call | tf_op jit(solution)/shard_map/first_backward/pallas_call | solution.py:386
  310.7 4.5 %collective-permute-start.3 = (bf16[128,64]{1,0:T(8,128)(2,1)S(1)}, bf16[128,64]{1,0:T(8,128)(2,1)S(1)}, u32[]{:S(2)}, u32[]{:S(2)}) collective-permute-start(bf16[128,64]{1,0:T(8,128)(2,1)S(1)} %copy-done.61), channel_id=1, source_target_pairs={{0,2},{2,0},{1,3},{3,1},{4,6},{6,4},{5,7},{7,5},{8,10},{10,8},{9,1... | collective-permute-start | bytes 49160 | tf_op jit(solution)/shard_map/ppermute | solution.py:71
  315.3 1.9 collective-permute-start.10
  317.2 2.8 collective-permute-done.10
  320.0 5.5 %collective-permute-start.11 = (f32[128,128]{1,0:T(8,128)S(1)}, f32[128,128]{1,0:T(8,128)S(1)}, u32[]{:S(2)}, u32[]{:S(2)}) collective-permute-start(f32[128,128]{1,0:T(8,128)S(1)} %add.183), channel_id=1, source_target_pairs={{0,2},{2,0},{1,3},{3,1},{4,6},{6,4},{5,7},{7,5},{8,10},{10,8},{9,1... | collective-permute-start | bytes 196616 | tf_op jit(solution)/shard_map/ppermute | solution.py:71
  (195 shorter events, 30.1 us)
Async XLA Ops:
  7.2 89.8 %copy-start = (bf16[1,256,64]{1,2,0:T(8,128)(2,1)S(1)}, bf16[1,256,64]{1,2,0:T(8,128)(2,1)}, u32[]{:S(2)}) copy-start(bf16[1,256,64]{1,2,0:T(8,128)(2,1)} %param.19) | copy-start | bytes 98308
  10.2 34.5 %copy-start.39 = (bf16[152,1216]{1,0:T(8,128)(2,1)S(1)}, bf16[152,1216]{1,0:T(8,128)(2,1)}, u32[]{:S(2)}) copy-start(bf16[152,1216]{1,0:T(8,128)(2,1)} %w1_ref.1) | copy-start | bytes 1108996
  10.2 34.5 %copy-start.40 = (bf16[1216,152]{0,1:T(8,128)(2,1)S(1)}, bf16[1216,152]{0,1:T(8,128)(2,1)}, u32[]{:S(2)}) copy-start(bf16[1216,152]{0,1:T(8,128)(2,1)} %param.26) | copy-start | bytes 1108996
  11.7 16.1 %all-to-all-start = ((bf16[16,8,912]{2,1,0:T(8,128)(2,1)}), bf16[16,8,912]{2,1,0:T(8,128)(2,1)S(1)}, u32[]{:S(2)}, u32[]{:S(2)}) async-start(bf16[16,8,912]{2,1,0:T(8,128)(2,1)} %bitcast.11), calls=%async_computation | async-start | bytes 524288 | tf_op jit(solution)/shard_map/all_to_all | solution.py:461
  20.1 28.3 %copy-start.64 = (s32[16]{0:T(128)S(1)}, s32[16]{0:T(128)}, u32[]{:S(2)}) copy-start(s32[16]{0:T(128)} %param.17) | copy-start | bytes 196
  47.9 59.0 %collective-permute-start.5 = (bf16[2,1216,2432]{2,1,0:T(8,128)(2,1)}, bf16[2,1216,2432]{2,1,0:T(8,128)(2,1)}, u32[]{:S(2)}, u32[]{:S(2)}) collective-permute-start(bf16[2,1216,2432]{2,1,0:T(8,128)(2,1)} %refs_0_), channel_id=1, source_target_pairs={{0,2},{2,0},{1,3},{3,1},{4,6},{6,4},{5,7},{7,5},{8,10},{10,8},{9,1... | collective-permute-start | bytes 35487752 | tf_op jit(solution)/shard_map/ppermute | solution.py:71
  48.1 75.0 %collective-permute-start.6 = (bf16[2,1216,2432]{2,1,0:T(8,128)(2,1)}, bf16[2,1216,2432]{2,1,0:T(8,128)(2,1)}, u32[]{:S(2)}, u32[]{:S(2)}) collective-permute-start(bf16[2,1216,2432]{2,1,0:T(8,128)(2,1)} %bitcast.75), channel_id=1, source_target_pairs={{0,2},{2,0},{1,3},{3,1},{4,6},{6,4},{5,7},{7,5},{8,10},{10,8},{9,1... | collective-permute-start | bytes 35487752 | tf_op jit(solution)/shard_map/ppermute | solution.py:71
  48.8 25.0 %all-to-all-start.1 = ((bf16[16,16,2496]{2,1,0:T(8,128)(2,1)}), bf16[16,16,2496]{2,1,0:T(8,128)(2,1)S(1)}, u32[]{:S(2)}, u32[]{:S(2)}) async-start(bf16[16,16,2496]{2,1,0:T(8,128)(2,1)} %bitcast.86), calls=%async_computation.1 | async-start | bytes 2621440 | tf_op jit(solution)/shard_map/all_to_all | solution.py:487
  54.2 4.4 %copy-start.4 = (bf16[2,2432,1216]{1,2,0:T(8,128)(2,1)S(1)}, bf16[2,2432,1216]{1,2,0:T(8,128)(2,1)}, u32[]{:S(2)}) copy-start(bf16[2,2432,1216]{1,2,0:T(8,128)(2,1)} %param.28) | copy-start | bytes 35487748
  73.9 21.1 %copy-start.63 = (s32[16]{0:T(128)S(1)}, s32[16]{0:T(128)}, u32[]{:S(2)}) copy-start(s32[16]{0:T(128)} %param.18) | copy-start | bytes 196
  75.2 21.7 %copy-start.65 = (s32[16]{0:T(128)S(1)}, s32[16]{0:T(128)}, u32[]{:S(2)}) copy-start(s32[16]{0:T(128)} %param.17) | copy-start | bytes 196
  75.2 24.3 %copy-start.22 = (f32[72,1216]{1,0:T(8,128)S(1)}, f32[72,1216]{1,0:T(8,128)}, u32[]{:S(2)}) copy-start(f32[72,1216]{1,0:T(8,128)} %copy-done.21) | copy-start | bytes 1050628
  75.2 15.7 %all-to-all-start.2 = ((bf16[16,8,2496]{2,1,0:T(8,128)(2,1)}), bf16[16,8,2496]{2,1,0:T(8,128)(2,1)S(1)}, u32[]{:S(2)}, u32[]{:S(2)}) async-start(bf16[16,8,2496]{2,1,0:T(8,128)(2,1)} %bitcast.84), calls=%async_computation.2 | async-start | bytes 1310720 | tf_op jit(solution)/shard_map/all_to_all | solution.py:525
  79.6 105.3 %all-gather.3.cloned.1.call-start = ((), (), s32[]{:S(2)}) async-start(), calls=%async_computation.11 | async-start | bytes 1984512 | tf_op jit(solution)/shard_map/all_gather | solution.py:531
  92.4 3.5 %collective-permute-start = (f32[128,64]{1,0:T(8,128)S(1)}, f32[128,64]{1,0:T(8,128)S(1)}, u32[]{:S(2)}, u32[]{:S(2)}) collective-permute-start(f32[128,64]{1,0:T(8,128)S(1)} %constant_dynamic-slice_fusion.1), channel_id=1, source_target_pairs={{0,2},{2,0},{1,3},{3,1},{4,6},{6,4},{5,7},{7,5},{8,10},{10,8},{9,1... | collective-permute-start | bytes 98312 | tf_op jit(solution)/shard_map/ppermute | solution.py:71
  95.9 4.4 %collective-permute-start.1 = (f32[128,64]{1,0:T(8,128)S(1)}, f32[128,64]{1,0:T(8,128)S(1)}, u32[]{:S(2)}, u32[]{:S(2)}) collective-permute-start(f32[128,64]{1,0:T(8,128)S(1)} %dynamic-slice_add_fusion), channel_id=1, source_target_pairs={{0,4},{4,0},{8,12},{12,8},{1,5},{5,1},{9,13},{13,9},{2,6},{6,2},{1... | collective-permute-start | bytes 98312 | tf_op jit(solution)/shard_map/ppermute | solution.py:544
  99.6 7.3 %collective-permute-start.4 = (f32[72,1216]{1,0:T(8,128)S(1)}, f32[72,1216]{1,0:T(8,128)S(1)}, u32[]{:S(2)}, u32[]{:S(2)}) collective-permute-start(f32[72,1216]{1,0:T(8,128)S(1)} %copy-done.22), channel_id=1, source_target_pairs={{0,2},{2,0},{1,3},{3,1},{4,6},{6,4},{5,7},{7,5},{8,10},{10,8},{9,1... | collective-permute-start | bytes 1050632 | tf_op jit(solution)/shard_map/ppermute | solution.py:71
  100.3 5.3 %collective-permute-start.2 = (f32[128,64]{1,0:T(8,128)S(1)}, f32[128,64]{1,0:T(8,128)S(1)}, u32[]{:S(2)}, u32[]{:S(2)}) collective-permute-start(f32[128,64]{1,0:T(8,128)S(1)} %add.177), channel_id=1, source_target_pairs={{0,8},{8,0},{4,12},{12,4},{1,9},{9,1},{5,13},{13,5},{2,10},{10,2},... | collective-permute-start | bytes 98312 | tf_op jit(solution)/shard_map/ppermute | solution.py:545
  106.9 10.8 %copy-start.24 = (f32[72,1216]{1,0:T(8,128)}, f32[72,1216]{1,0:T(8,128)S(1)}, u32[]{:S(2)}) copy-start(f32[72,1216]{1,0:T(8,128)S(1)} %collective-permute-done.4.mat_sib) | copy-start | bytes 1050628
  106.9 4.6 %copy-start.2 = (bf16[2,1216,2432]{2,1,0:T(8,128)(2,1)S(1)}, bf16[2,1216,2432]{2,1,0:T(8,128)(2,1)}, u32[]{:S(2)}) copy-start(bf16[2,1216,2432]{2,1,0:T(8,128)(2,1)} %refs_0_) | copy-start | bytes 35487748
  119.1 23.8 %all-to-all-start.3 = ((bf16[4,32,2432]{2,1,0:T(8,128)(2,1)}), bf16[4,32,2432]{2,1,0:T(8,128)(2,1)S(1)}, u32[]{:S(2)}, u32[]{:S(2)}) async-start(bf16[4,32,2432]{2,1,0:T(8,128)(2,1)} %bitcast.30), calls=%async_computation.3 | async-start | bytes 1245184 | tf_op jit(solution)/shard_map/all_to_all | solution.py:75
  123.1 4.4 %copy-start.5 = (bf16[2,2432,1216]{1,2,0:T(8,128)(2,1)S(1)}, bf16[2,2432,1216]{1,2,0:T(8,128)(2,1)}, u32[]{:S(2)}) copy-start(bf16[2,2432,1216]{1,2,0:T(8,128)(2,1)} %param.28) | copy-start | bytes 35487748
  127.5 15.5 %copy-start.46 = (f32[1,2432]{1,0:T(1,128)S(1)}, f32[1,2432]{1,0:T(1,128)}, u32[]{:S(2)}) copy-start(f32[1,2432]{1,0:T(1,128)} %get-tuple-element.133.gate_ref) | copy-start | bytes 29188
  134.3 4.3 %copy-start.13 = (bf16[2,1216,2432]{2,1,0:T(8,128)(2,1)}, bf16[2,1216,2432]{2,1,0:T(8,128)(2,1)S(1)}, u32[]{:S(2)}) copy-start(bf16[2,1216,2432]{2,1,0:T(8,128)(2,1)S(1)} %get-tuple-element.75.up_ref) | copy-start | bytes 35487748
  138.6 4.4 %copy-start.15 = (bf16[2,1216,2432]{2,1,0:T(8,128)(2,1)}, bf16[2,1216,2432]{2,1,0:T(8,128)(2,1)S(1)}, u32[]{:S(2)}) copy-start(bf16[2,1216,2432]{2,1,0:T(8,128)(2,1)S(1)} %get-tuple-element.76.down_ref) | copy-start | bytes 35487748
  143.0 13.4 %copy-start.58 = (f32[1,2432]{1,0:T(1,128)S(1)}, f32[1,2432]{1,0:T(1,128)}, u32[]{:S(2)}) copy-start(f32[1,2432]{1,0:T(1,128)} %get-tuple-element.131.shift_ref) | copy-start | bytes 29188
  143.0 13.4 %copy-start.50 = (f32[1,2432]{1,0:T(1,128)S(1)}, f32[1,2432]{1,0:T(1,128)}, u32[]{:S(2)}) copy-start(f32[1,2432]{1,0:T(1,128)} %get-tuple-element.132.scale_ref) | copy-start | bytes 29188
  143.1 40.1 %copy-start.37 = (bf16[32,2432]{1,0:T(8,128)(2,1)}, bf16[32,2432]{1,0:T(8,128)(2,1)S(1)}, u32[]{:S(2)}) copy-start(bf16[32,2432]{1,0:T(8,128)(2,1)S(1)} %get-tuple-element.78.g_ref) | copy-start | bytes 466948
  156.4 4.4 %copy-start.14 = (bf16[2,1216,2432]{2,1,0:T(8,128)(2,1)S(1)}, bf16[2,1216,2432]{2,1,0:T(8,128)(2,1)}, u32[]{:S(2)}) copy-start(bf16[2,1216,2432]{2,1,0:T(8,128)(2,1)} %copy-done.13) | copy-start | bytes 35487748
  160.7 4.4 %copy-start.16 = (bf16[2,1216,2432]{2,1,0:T(8,128)(2,1)S(1)}, bf16[2,1216,2432]{2,1,0:T(8,128)(2,1)}, u32[]{:S(2)}) copy-start(bf16[2,1216,2432]{2,1,0:T(8,128)(2,1)} %copy-done.15) | copy-start | bytes 35487748
  165.1 18.2 %copy-start.48 = (f32[1,2432]{1,0:T(1,128)S(1)}, f32[1,2432]{1,0:T(1,128)}, u32[]{:S(2)}) copy-start(f32[1,2432]{1,0:T(1,128)} %get-tuple-element.130.gate_ref) | copy-start | bytes 29188
  172.5 19.8 %copy-start.62 = (f32[2,304]{1,0:T(2,128)S(1)}, f32[2,304]{1,0:T(2,128)}, u32[]{:S(2)}) copy-start(f32[2,304]{1,0:T(2,128)} %param.31) | copy-start | bytes 7300
  172.5 20.1 %copy-start.66 = (s32[1,2]{1,0:T(1,128)S(1)}, s32[1,2]{1,0:T(1,128)}, u32[]{:S(2)}) copy-start(s32[1,2]{1,0:T(1,128)} %param.20) | copy-start | bytes 28
  184.9 18.2 %collective-permute-start.8 = (bf16[2432,384]{1,0:T(8,128)(2,1)}, bf16[2432,384]{1,0:T(8,128)(2,1)S(1)}, u32[]{:S(2)}, u32[]{:S(2)}) collective-permute-start(bf16[2432,384]{1,0:T(8,128)(2,1)} %all-gather.3.cloned.1.call-done.own), channel_id=1, source_target_pairs={{0,2},{2,0},{1,3},{3,1},{4,6},{6,4},{5,7},{7,5},{8,10},{10,8},{9,1... | collective-permute-start | bytes 5603336 | tf_op jit(solution)/shard_map/ppermute | solution.py:71
  188.1 14.9 %all-to-all-start.6 = ((bf16[4,32,2432]{2,1,0:T(8,128)(2,1)}), bf16[4,32,2432]{2,1,0:T(8,128)(2,1)}, u32[]{:S(2)}, u32[]{:S(2)}) async-start(bf16[4,32,2432]{2,1,0:T(8,128)(2,1)} %copy-done.34), calls=%async_computation.6 | async-start | bytes 1245184 | tf_op jit(solution)/shard_map/all_to_all | solution.py:75
  192.3 1.5 collective-permute-start.7
  203.1 8.0 %copy-start.19 = (bf16[2432,384]{1,0:T(8,128)(2,1)}, bf16[2432,384]{1,0:T(8,128)(2,1)S(1)}, u32[]{:S(2)}) copy-start(bf16[2432,384]{1,0:T(8,128)(2,1)S(1)} %collective-permute-done.8.sib) | copy-start | bytes 5603332
  211.1 23.8 %all-to-all-start.7 = ((bf16[4,32,2432]{2,1,0:T(8,128)(2,1)}), bf16[4,32,2432]{2,1,0:T(8,128)(2,1)}, u32[]{:S(2)}, u32[]{:S(2)}) async-start(bf16[4,32,2432]{2,1,0:T(8,128)(2,1)} %bitcast.87), calls=%async_computation.7 | async-start | bytes 1245184 | tf_op jit(solution)/shard_map/all_to_all | solution.py:75
  215.2 4.4 %copy-start.6 = (bf16[2,2432,1216]{1,2,0:T(8,128)(2,1)S(1)}, bf16[2,2432,1216]{1,2,0:T(8,128)(2,1)}, u32[]{:S(2)}) copy-start(bf16[2,2432,1216]{1,2,0:T(8,128)(2,1)} %param.28) | copy-start | bytes 35487748
  219.6 15.3 %copy-start.49 = (f32[1,2432]{1,0:T(1,128)S(1)}, f32[1,2432]{1,0:T(1,128)}, u32[]{:S(2)}) copy-start(f32[1,2432]{1,0:T(1,128)} %get-tuple-element.130.gate_ref) | copy-start | bytes 29188
  234.9 8.4 %copy-start.18 = (bf16[2432,384]{1,0:T(8,128)(2,1)S(1)}, bf16[2432,384]{1,0:T(8,128)(2,1)}, u32[]{:S(2)}) copy-start(bf16[2432,384]{1,0:T(8,128)(2,1)} %all-gather.3.cloned.1.call-done.own) | copy-start | bytes 5603332
  238.9 13.4 %copy-start.51 = (f32[1,2432]{1,0:T(1,128)S(1)}, f32[1,2432]{1,0:T(1,128)}, u32[]{:S(2)}) copy-start(f32[1,2432]{1,0:T(1,128)} %get-tuple-element.132.scale_ref) | copy-start | bytes 29188
  238.9 13.4 %all-to-all-start.8 = ((bf16[4,32,2432]{2,1,0:T(8,128)(2,1)}), bf16[4,32,2432]{2,1,0:T(8,128)(2,1)}, u32[]{:S(2)}, u32[]{:S(2)}) async-start(bf16[4,32,2432]{2,1,0:T(8,128)(2,1)} %copy-done.35), calls=%async_computation.8 | async-start | bytes 1245184 | tf_op jit(solution)/shard_map/all_to_all | solution.py:75
  252.3 4.4 %copy-start.10 = (bf16[2,1216,2432]{2,1,0:T(8,128)(2,1)S(1)}, bf16[2,1216,2432]{2,1,0:T(8,128)(2,1)}, u32[]{:S(2)}) copy-start(bf16[2,1216,2432]{2,1,0:T(8,128)(2,1)} %copy-done.9) | copy-start | bytes 35487748
  256.7 4.4 %copy-start.12 = (bf16[2,1216,2432]{2,1,0:T(8,128)(2,1)S(1)}, bf16[2,1216,2432]{2,1,0:T(8,128)(2,1)}, u32[]{:S(2)}) copy-start(bf16[2,1216,2432]{2,1,0:T(8,128)(2,1)} %copy-done.11) | copy-start | bytes 35487748
  271.8 15.5 %all-to-all-start.9 = ((bf16[4,32,2432]{2,1,0:T(8,128)(2,1)}), bf16[4,32,2432]{2,1,0:T(8,128)(2,1)S(1)}, u32[]{:S(2)}, u32[]{:S(2)}) async-start(bf16[4,32,2432]{2,1,0:T(8,128)(2,1)} %bitcast.44), calls=%async_computation.9 | async-start | bytes 1245184 | tf_op jit(solution)/shard_map/all_to_all | solution.py:75
  275.3 4.4 %copy-start.3 = (bf16[2,1216,2432]{2,1,0:T(8,128)(2,1)S(1)}, bf16[2,1216,2432]{2,1,0:T(8,128)(2,1)}, u32[]{:S(2)}) copy-start(bf16[2,1216,2432]{2,1,0:T(8,128)(2,1)} %refs_0_) | copy-start | bytes 35487748
  279.7 7.7 %copy-start.38 = (bf16[32,2432]{1,0:T(8,128)(2,1)S(1)}, bf16[32,2432]{1,0:T(8,128)(2,1)}, u32[]{:S(2)}) copy-start(bf16[32,2432]{1,0:T(8,128)(2,1)} %copy-done.37) | copy-start | bytes 466948
  279.7 7.7 %copy-start.43 = (f32[32,2432]{1,0:T(8,128)S(1)}, f32[32,2432]{1,0:T(8,128)}, u32[]{:S(2)}) copy-start(f32[32,2432]{1,0:T(8,128)} %copy-done.42) | copy-start | bytes 933892
  279.7 7.7 %copy-start.47 = (f32[1,2432]{1,0:T(1,128)S(1)}, f32[1,2432]{1,0:T(1,128)}, u32[]{:S(2)}) copy-start(f32[1,2432]{1,0:T(1,128)} %get-tuple-element.133.gate_ref) | copy-start | bytes 29188
  283.0 4.3 %copy-start.7 = (bf16[2,1216,2432]{2,1,0:T(8,128)(2,1)}, bf16[2,1216,2432]{2,1,0:T(8,128)(2,1)S(1)}, u32[]{:S(2)}) copy-start(bf16[2,1216,2432]{2,1,0:T(8,128)(2,1)S(1)} %resident.5.down_ref) | copy-start | bytes 35487748
  287.3 5.5 %copy-start.55 = (f32[128,128]{1,0:T(8,128)S(1)}, f32[128,128]{1,0:T(8,128)}, u32[]{:S(2)}) copy-start(f32[128,128]{1,0:T(8,128)} %copy-done.54) | copy-start | bytes 196612
  287.3 5.5 %copy-start.57 = (f32[128,128]{1,0:T(8,128)S(1)}, f32[128,128]{1,0:T(8,128)}, u32[]{:S(2)}) copy-start(f32[128,128]{1,0:T(8,128)} %copy-done.56) | copy-start | bytes 196612
  287.3 13.0 %copy-start.25 = (f32[72,1216]{1,0:T(8,128)S(1)}, f32[72,1216]{1,0:T(8,128)}, u32[]{:S(2)}) copy-start(f32[72,1216]{1,0:T(8,128)} %copy-done.24) | copy-start | bytes 1050628
  287.3 13.0 %copy-start.28 = (bf16[2,128,1216]{2,1,0:T(8,128)(2,1)S(1)}, bf16[2,128,1216]{2,1,0:T(8,128)(2,1)}, u32[]{:S(2)}) copy-start(bf16[2,128,1216]{2,1,0:T(8,128)(2,1)} %copy-done.27) | copy-start | bytes 1867780
  287.3 13.0 %copy-start.53 = (f32[128,128]{1,0:T(8,128)S(1)}, f32[128,128]{1,0:T(8,128)}, u32[]{:S(2)}) copy-start(f32[128,128]{1,0:T(8,128)} %copy-done.52) | copy-start | bytes 196612
  288.6 11.7 %all-to-all-start.10 = ((bf16[4,32,2432]{2,1,0:T(8,128)(2,1)}), bf16[4,32,2432]{2,1,0:T(8,128)(2,1)S(1)}, u32[]{:S(2)}, u32[]{:S(2)}) async-start(bf16[4,32,2432]{2,1,0:T(8,128)(2,1)} %get-tuple-element.102), calls=%async_computation.10 | async-start | bytes 1245184 | tf_op jit(solution)/shard_map/all_to_all | solution.py:75
  300.3 4.4 %copy-start.8 = (bf16[2,1216,2432]{2,1,0:T(8,128)(2,1)S(1)}, bf16[2,1216,2432]{2,1,0:T(8,128)(2,1)}, u32[]{:S(2)}) copy-start(bf16[2,1216,2432]{2,1,0:T(8,128)(2,1)} %copy-done.7) | copy-start | bytes 35487748
  304.7 6.1 %copy-start.61 = (bf16[128,64]{1,0:T(8,128)(2,1)S(1)}, bf16[128,64]{1,0:T(8,128)(2,1)}, u32[]{:S(2)}) copy-start(bf16[128,64]{1,0:T(8,128)(2,1)} %get-tuple-element.125) | copy-start | bytes 49156
  304.7 23.3 %copy-start.1 = (bf16[1,256,64]{1,2,0:T(8,128)(2,1)S(1)}, bf16[1,256,64]{1,2,0:T(8,128)(2,1)}, u32[]{:S(2)}) copy-start(bf16[1,256,64]{1,2,0:T(8,128)(2,1)} %param.19) | copy-start | bytes 98308
  310.3 4.9 %collective-permute-start.9 = (f32[128,128]{1,0:T(8,128)S(1)}, f32[128,128]{1,0:T(8,128)S(1)}, u32[]{:S(2)}, u32[]{:S(2)}) collective-permute-start(f32[128,128]{1,0:T(8,128)S(1)} %first_backward.1), channel_id=1, source_target_pairs={{0,4},{4,0},{8,12},{12,8},{1,5},{5,1},{9,13},{13,9},{2,6},{6,2},{1... | collective-permute-start | bytes 196616 | tf_op jit(solution)/shard_map/ppermute | solution.py:689
  310.7 6.4 %collective-permute-start.3 = (bf16[128,64]{1,0:T(8,128)(2,1)S(1)}, bf16[128,64]{1,0:T(8,128)(2,1)S(1)}, u32[]{:S(2)}, u32[]{:S(2)}) collective-permute-start(bf16[128,64]{1,0:T(8,128)(2,1)S(1)} %copy-done.61), channel_id=1, source_target_pairs={{0,2},{2,0},{1,3},{3,1},{4,6},{6,4},{5,7},{7,5},{8,10},{10,8},{9,1... | collective-permute-start | bytes 49160 | tf_op jit(solution)/shard_map/ppermute | solution.py:71
  315.3 4.7 %collective-permute-start.10 = (f32[128,128]{1,0:T(8,128)S(1)}, f32[128,128]{1,0:T(8,128)S(1)}, u32[]{:S(2)}, u32[]{:S(2)}) collective-permute-start(f32[128,128]{1,0:T(8,128)S(1)} %add.182), channel_id=1, source_target_pairs={{0,8},{8,0},{4,12},{12,4},{1,9},{9,1},{5,13},{13,5},{2,10},{10,2},... | collective-permute-start | bytes 196616 | tf_op jit(solution)/shard_map/ppermute | solution.py:690
  320.0 6.5 %collective-permute-start.11 = (f32[128,128]{1,0:T(8,128)S(1)}, f32[128,128]{1,0:T(8,128)S(1)}, u32[]{:S(2)}, u32[]{:S(2)}) collective-permute-start(f32[128,128]{1,0:T(8,128)S(1)} %add.183), channel_id=1, source_target_pairs={{0,2},{2,0},{1,3},{3,1},{4,6},{6,4},{5,7},{7,5},{8,10},{10,8},{9,1... | collective-permute-start | bytes 196616 | tf_op jit(solution)/shard_map/ppermute | solution.py:71
  (25 other events, 32.9 us)
Sparse Core Ops, SparseCore 0:
  91.1 66.0 all-gather.2
where the time goes:
time: 337 us; the launch traced here: 335 us
  local copies, waits for them, and re-layouts  95.4 us (28%)
  starting transfers between devices  64.2 us (19%)
  Pallas kernels  62.3 us (18%)
  waiting for transfers between devices  50.8 us (15%)
  blocking collectives  40.5 us (12%)
  between operations  16.2 us (5%)
    unnamed x142, local copies, waits for them, and re-layouts  90.4 us
    pallas_call x15, Pallas kernels, here(): pl.pallas_call(kernel, name=name, out_shape=out_shape, in_specs=[pl.Block...  45.5 us
    all_to_all x6, starting transfers between devices, swap_y(): return lax.all_to_all(values, 'y', 0, 0)  24.3 us
    all_to_all x2, blocking collectives, swap_y(): return lax.all_to_all(values, 'y', 0, 0)  24 us
    all_to_all x6, waiting for transfers between devices, swap_y(): return lax.all_to_all(values, 'y', 0, 0)  19.4 us
    ppermute x8, starting transfers between devices, sibling(): return lax.ppermute(values, 'core', [(0, 1), (1, 0)])  17.4 us
    pallas_call x3, Pallas kernels, resident(): pl.pallas_call(functools.partial(resident_kernel, plan), name='resident',...  16.8 us
    all_gather x1, blocking collectives, body(): gathered = lax.all_gather(packed, TP, axis=0, tiled=False)  16.5 us
  transfers between devices with their start and end apart: 22, of which 11 were waited for; matrix products, arithmetic and copies ran while one was open for 4% of the time, Pallas kernels for 11%

commit v1 on v0

--- a/solution.py
+++ b/solution.py
@@ -210,66 +210,74 @@
     send.wait()
 
 
-def resident_kernel(plan, *refs):
-    sources, out_refs, sems = refs[: 2 * len(plan)], refs[2 * len(plan) : -1], refs[-1]
-    copies = []
-    for index, layer in enumerate(plan):
-        copies += matrices(layer, sources[2 * index : 2 * index + 2], out_refs[index])
-    stream = Stream(copies, sems)
-    for _ in copies:
-        stream.next()
-
-
 def forward_kernel(
-    g_ref, scale_ref, shift_ref, up_ref, down_ref, y_out, slope_out, y_ref, slope_ref, sems
+    g_ref, scale_ref, shift_ref, up_own, up_sib, down_own, down_sib, y_out, slope_out,
+    up_ref, down_ref, y_ref, slope_ref, sems
 ):
+    stream = Stream(
+        matrices(1, (up_own, up_sib), up_ref) + matrices(1, (down_own, down_sib), down_ref), sems
+    )
     normed, _ = normalize(g_ref[...].astype(F32))
     u = (normed * (1.0 + scale_ref[...]) + shift_ref[...]).astype(BF)
     actives = []
     for side in range(2):
+        stream.next()
         active, slope = gelu_both(dot_back(u, up_ref[side]))
         slope_ref[side] = slope.astype(BF)
         actives.append(active.astype(BF))
-    keep = pltpu.make_async_copy(slope_ref, slope_out, sems.at[0])
+    keep = pltpu.make_async_copy(slope_ref, slope_out, sems.at[4])
     keep.start()
-    y_ref[...] = (dot(actives[0], down_ref[0]) + dot(actives[1], down_ref[1])).astype(BF)
-    send = pltpu.make_async_copy(y_ref, y_out, sems.at[1])
+    stream.next()
+    y = dot(actives[0], down_ref[0])
+    stream.next()
+    y_ref[...] = (y + dot(actives[1], down_ref[1])).astype(BF)
+    send = pltpu.make_async_copy(y_ref, y_out, sems.at[5])
     send.start()
     keep.wait()
     send.wait()
 
 
 def backward_kernel(
-    dy_ref, scale_ref, up_ref, down_ref, slope, head, out, slope_ref, head_ref, out_ref, sems
+    dy_ref, scale_ref, slope, head, up_own, up_sib, down_own, down_sib, out,
+    up_ref, down_ref, slope_ref, head_ref, out_ref, sems
 ):
-    stream = Stream([(slope, slope_ref), (head, head_ref)], sems)
+    stream = Stream(
+        [(slope, slope_ref)]
+        + matrices(1, (down_own, down_sib), down_ref)
+        + matrices(1, (up_own, up_sib), up_ref)
+        + [(head, head_ref)],
+        sems,
+    )
     dy = dy_ref[...]
-    da = dot_back(dy, down_ref[0])
-    stream.next()
-    dz_own = (da * slope_ref[0].astype(F32)).astype(BF)
-    dz_sib = (dot_back(dy, down_ref[1]) * slope_ref[1].astype(F32)).astype(BF)
-    du = dot(dz_own, up_ref[0]) + dot(dz_sib, up_ref[1])
+    stream.next()
+    dz = []
+    for side in range(2):
+        stream.next()
+        dz.append((dot_back(dy, down_ref[side]) * slope_ref[side].astype(F32)).astype(BF))
+    stream.next()
+    du = dot(dz[0], up_ref[0])
+    stream.next()
+    du = du + dot(dz[1], up_ref[1])
     stream.next()
     out_ref[...] = (du * (1.0 + scale_ref[...]) + head_ref[...].astype(F32)).astype(BF)
-    send = pltpu.make_async_copy(out_ref, out, sems.at[2])
+    send = pltpu.make_async_copy(out_ref, out, sems.at[6])
     send.start()
     send.wait()
 
 
 def first_backward_kernel(
-    at_ref, rest_ref, dy_ref, x_ref, back_ref, score_ref, direct_ref, mat_own, mat_sib, down_ref, slope,
-    out_ref, slope_ref, sems
+    at_ref, rest_ref, dy_ref, x_ref, back_ref, score_ref, direct_ref, mat_own, mat_sib, slope, own, sib,
+    out_ref, w_ref, slope_ref, sems
 ):
     cells = x_ref.shape[1]
-    stream = Stream([(slope, slope_ref)], sems)
+    stream = Stream([(slope, slope_ref)] + matrices(0, (own, sib), w_ref), sems)
     dy = dy_ref[...]
+    stream.next()
     total = None
     for side, mat_ref in enumerate((mat_own, mat_sib)):
         high, low = split(mat_ref[:cells])
-        da = dot_back(dy, down_ref[side])
-        if side == 0:
-            stream.next()
-        dz = (da * slope_ref[side].astype(F32)).astype(BF)
+        stream.next()
+        dz = (dot_back(dy, w_ref[side]) * slope_ref[side].astype(F32)).astype(BF)
         part = dot_back(dz, high) + dot_back(dz, low)
         total = part if total is None else total + part
     inverse = back_ref[:, cells : cells + 1]
@@ -380,34 +388,25 @@
 def here(kernel, name, out_shape, operands, scalars=0, far=0, far_out=(), scratch=(), limit=20):
     many = isinstance(out_shape, tuple)
     near = len(operands) - scalars - far
+    shapes = tuple(
+        pltpu.HBM(shape.shape, shape.dtype) if index in far_out else shape
+        for index, shape in enumerate(out_shape if many else (out_shape,))
+    )
+    operands = operands[: scalars + near] + tuple(
+        pltpu.with_memory_space_constraint(operand, pltpu.HBM) for operand in operands[scalars + near :]
+    )
     specs = tuple(
         FAR if index in far_out else WHOLE for index in range(len(out_shape) if many else 1)
     )
     return pl.pallas_call(
         kernel,
         name=name,
-        out_shape=out_shape,
+        out_shape=shapes if many else shapes[0],
         in_specs=[pl.BlockSpec(memory_space=pltpu.SMEM)] * scalars + [WHOLE] * near + [FAR] * far,
         out_specs=specs if many else specs[0],
         scratch_shapes=list(scratch),
         compiler_params=pltpu.CompilerParams(vmem_limit_bytes=limit * 2**20),
     )(*operands)
-
-
-def resident(plan, sources):
-    shapes = tuple(
-        pltpu.VMEM((2,) + sources[2 * index].shape[1:], sources[2 * index].dtype)
-        for index in range(len(plan))
-    )
-    return pl.pallas_call(
-        functools.partial(resident_kernel, plan),
-        name="resident",
-        out_shape=shapes,
-        in_specs=[FAR] * len(sources),
-        out_specs=(WHOLE,) * len(plan),
-        scratch_shapes=[pltpu.SemaphoreType.DMA((len(sources),))],
-        compiler_params=pltpu.CompilerParams(vmem_limit_bytes=4 * 2**20),
-    )(*sources)
 
 
 def array(shape, dtype):
@@ -500,6 +499,7 @@
         (proj_t, scales[0], shifts[0], t_w1),
         far=1,
         scratch=(pltpu.VMEM((1, hidden, width), BF), pltpu.SemaphoreType.DMA((1,))),
+        limit=44,
     )
     latent_in = noisy_latents[0]
     h0 = dot_back(latent_in, proj_s).astype(BF)
@@ -581,23 +581,19 @@
             inner,
             pltpu.SemaphoreType.DMA((4,)),
         ),
-        limit=32,
-    )
-
-    def sums(partial, plan, sources):
-        parts = swap_y(partial.reshape(4, quarter, width))
-        sources, _ = lax.optimization_barrier((sources, partial))
-        weights = resident(plan, sources)
-        parts, weights = lax.optimization_barrier((parts, weights))
-        return parts, weights
+        limit=44,
+    )
+
+    def sums(partial):
+        return swap_y(partial.reshape(4, quarter, width))
 
     last = (t_w1, w1_sib, t_w2, w2_sib)
-    parts, weights = sums(y_0, (1, 1), last)
+    matrix = pltpu.VMEM((2, hidden, width), BF)
     g_1_mine, g_1 = here(
         first_middle_kernel,
         "first_middle",
         (mine_out, rows_out),
-        (at_y.reshape(1), parts, g_0, gates[0]),
+        (at_y.reshape(1), sums(y_0), g_0, gates[0]),
         scalars=1,
     )
     g_1 = swap_y(g_1).reshape(half, width)
@@ -605,15 +601,17 @@
         forward_kernel,
         "forward",
         (array((half, width), BF), inner_out),
-        (g_1, scales[1], shifts[1]) + tuple(weights),
+        (g_1, scales[1], shifts[1]) + last,
+        far=4,
         far_out=(0, 1),
-        scratch=(token_rows, inner, pltpu.SemaphoreType.DMA((2,))),
+        scratch=(matrix, matrix, token_rows, inner, pltpu.SemaphoreType.DMA((6,))),
+        limit=44,
     )
     g_2_mine, g_2 = here(
         last_middle_kernel,
         "last_middle",
         (mine_out, rows_out),
-        (swap_y(y_1.reshape(4, quarter, width)), g_1_mine, gates[1]),
+        (sums(y_1), g_1_mine, gates[1]),
     )
     head_own, d_w2_late, _ = lax.optimization_barrier((head_own, d_w2, g_2_mine))
     head_sib = sibling(head_own)
@@ -640,12 +638,11 @@
 
     head_back_2, scores_2 = head("head_last", g_2, use[1])
 
-    parts, weights = sums(head_back_2, (1, 1), last)
     dg_2, dy_1 = here(
         last_back_kernel,
         "last_back",
         (array((quarter, width), F32), rows_out),
-        (parts, g_2_mine, gates[1]),
+        (sums(head_back_2), g_2_mine, gates[1]),
     )
     g_1, _ = lax.optimization_barrier((g_1, dg_2))
     head_back_1, scores_1 = head("head_first", g_1, use[0])
@@ -653,17 +650,17 @@
         backward_kernel,
         "backward",
         array((half, width), BF),
-        (swap_y(dy_1).reshape(half, width), scales[1]) + tuple(weights) + (slope_1, head_back_1),
-        far=2,
+        (swap_y(dy_1).reshape(half, width), scales[1], slope_1, head_back_1) + last,
+        far=6,
         far_out=(0,),
-        scratch=(inner, token_rows, token_rows, pltpu.SemaphoreType.DMA((3,))),
-    )
-    parts, weights = sums(du_1, (0,), (t_w2, w2_sib))
+        scratch=(matrix, matrix, inner, token_rows, token_rows, pltpu.SemaphoreType.DMA((7,))),
+        limit=44,
+    )
     direct, dy_0 = here(
         first_back_kernel,
         "first_back",
         (array((quarter, cells), F32), rows_out),
-        (parts, g_1_mine, dg_2, gates[0], proj_t),
+        (sums(du_1), g_1_mine, dg_2, gates[0], proj_t),
     )
     final = here(
         first_backward_kernel,
@@ -679,12 +676,14 @@
             direct,
             first_own,
             first_sib,
-        )
-        + tuple(weights)
-        + (slope_0,),
+            slope_0,
+            t_w2,
+            w2_sib,
+        ),
         scalars=2,
-        far=1,
-        scratch=(inner, pltpu.SemaphoreType.DMA((1,))),
+        far=3,
+        scratch=(matrix, inner, pltpu.SemaphoreType.DMA((3,))),
+        limit=44,
     )
     final = final + lax.ppermute(final, "y", [(0, 1), (1, 0), (2, 3), (3, 2)])
     final = final + lax.ppermute(final, "y", [(0, 2), (2, 0), (1, 3), (3, 1)])

time: 337 us -> 281 us (0.83)
  local copies, waits for them, and re-layouts: 95.4 us -> 11 us
  waiting for transfers between devices: 50.8 us -> 75.3 us
  blocking collectives: 40.5 us -> 51.6 us
  starting transfers between devices: 64.2 us -> 60 us
    unnamed x142 -> x48, local copies, waits for them, and re-layouts: 90.4 us -> 7.5 us
    all_to_all x6 -> x5, waiting for transfers between devices: 19.4 us -> 37.6 us  [swap_y(): return lax.all_to_all(values, 'y', 0, 0)]
    all_to_all x2 -> x3, blocking collectives: 24 us -> 35.1 us  [swap_y(): return lax.all_to_all(values, 'y', 0, 0)]
    all_to_all x6 -> x5, starting transfers between devices: 24.3 us -> 18.2 us  [swap_y(): return lax.all_to_all(values, 'y', 0, 0)]
    pallas_call x18 -> x15, Pallas kernels: 62.3 us -> 61.4 us  [here(): pl.pallas_call(kernel, name=name, out_shape=shapes if many else shapes[0]...]
  transfers between devices with their start and end apart: 22 -> 21, of which waited for: 11 -> 13; matrix products, arithmetic and copies ran while one was open for 4% -> 3% of each run, Pallas kernels for 11% -> 11%
where the time goes in v1:
time: 281 us; the launch traced here: 280 us
  waiting for transfers between devices  75.3 us (27%)
  Pallas kernels  61.4 us (22%)
  starting transfers between devices  60 us (21%)
  blocking collectives  51.6 us (18%)
  between operations  16 us (6%)
  local copies, waits for them, and re-layouts  11 us (4%)
    pallas_call x15, Pallas kernels, here(): pl.pallas_call(kernel, name=name, out_shape=shapes if many else shapes[0]...  61.4 us
    all_to_all x5, waiting for transfers between devices, swap_y(): return lax.all_to_all(values, 'y', 0, 0)  37.6 us
    all_to_all x3, blocking collectives, swap_y(): return lax.all_to_all(values, 'y', 0, 0)  35.1 us
    ppermute x8, starting transfers between devices, sibling(): return lax.ppermute(values, 'core', [(0, 1), (1, 0)])  19.2 us
    all_to_all x5, starting transfers between devices, swap_y(): return lax.all_to_all(values, 'y', 0, 0)  18.2 us
    all_gather x1, blocking collectives, body(): gathered = lax.all_gather(packed, TP, axis=0, tiled=False)  16.5 us
    all_to_all x1, waiting for transfers between devices, body(): lax.all_to_all(parts.reshape(samples, piece, both_wide), SAMPLE, 0, 0)  13.8 us
    all_to_all x1, waiting for transfers between devices, body(): mine = lax.all_to_all(chosen.reshape(samples, 8, both_wide), SAMPLE, 0, 0)  10.7 us
  transfers between devices with their start and end apart: 21, of which 13 were waited for; matrix products, arithmetic and copies ran while one was open for 3% of the time, Pallas kernels for 11%

profile of v1, /device:TPU:1, one launch (start us, length us, event | category | flops | bytes accessed | tf_op | source)
XLA Modules:
  0.0 280.1 jit_solution(7874684551128726176)
XLA Ops:
  7.2 0.7 convert_element_type.94
  8.2 1.1 copy-done.6
  9.3 1.0 copy-done.9
  10.3 1.4 modulation.1
  11.7 8.6 %all-to-all-start = ((bf16[16,8,912]{2,1,0:T(8,128)(2,1)}), bf16[16,8,912]{2,1,0:T(8,128)(2,1)S(1)}, u32[]{:S(2)}, u32[]{:S(2)}) async-start(bf16[16,8,912]{2,1,0:T(8,128)(2,1)} %bitcast.11), calls=%async_computation | async-start | bytes 524288 | tf_op jit(solution)/shard_map/all_to_all | solution.py:460
  20.9 7.1 %all-to-all-done = bf16[16,8,912]{2,1,0:T(8,128)(2,1)S(1)} async-done(((bf16[16,8,912]{2,1,0:T(8,128)(2,1)}), bf16[16,8,912]{2,1,0:T(8,128)(2,1)S(1)}, u32[]{:S(2)}, u32[]{:S(2)}) %all-to-all-start) | async-done | bytes 233504 | tf_op jit(solution)/shard_map/all_to_all | solution.py:460
  28.4 16.5 %all-gather = bf16[2432,210]{1,0:T(8,128)(2,1)S(1)} all-gather(bf16[304,210]{1,0:T(8,128)(2,1)S(1)} %maximum_bitcast_fusion), channel_id=2, replica_groups=mesh['fsdp'=8,'y'=4,'core'=2,'grp'=2] {'y','core'}, dimensions={0}, use_global_device_ids=true | all-gather | bytes 1149120 | tf_op jit(solution)/shard_map/all_gather | solution.py:464
  44.9 2.0 product.1
  46.9 1.2 copy-done.5
  49.0 3.7 %all-to-all-start.1 = ((bf16[16,16,2496]{2,1,0:T(8,128)(2,1)}), bf16[16,16,2496]{2,1,0:T(8,128)(2,1)S(1)}, u32[]{:S(2)}, u32[]{:S(2)}) async-start(bf16[16,16,2496]{2,1,0:T(8,128)(2,1)} %bitcast.84), calls=%async_computation.1 | async-start | bytes 2621440 | tf_op jit(solution)/shard_map/all_to_all | solution.py:486
  53.7 4.7 %first_product.1.mat_own = f32[72,1216]{1,0:T(8,128)S(1)} custom-call(bf16[2432,64]{1,0:T(8,128)(2,1)S(1)} %slice.59.proj_ref, f32[1,2432]{1,0:T(1,128)S(1)} %get-tuple-element.91.scale_ref, f32[1,2432]{1,0:T(1,128)S(1)} %get-tuple-element.90.shift_ref, bf16[2,1216,2432]{2,1,0:T(8,128)(2,1)} %bitcast.88), custom_call_target="tpu_custom_call" | custom-call | tf_op jit(solution)/shard_map/first_product/pallas_call | solution.py:401
  58.5 0.6 convert_reduce_fusion
  59.1 0.4 fusion.1
  59.5 0.7 copy-done.10
  60.2 13.8 %all-to-all-done.1.parts_ref = bf16[16,16,2496]{2,1,0:T(8,128)(2,1)S(1)} async-done(((bf16[16,16,2496]{2,1,0:T(8,128)(2,1)}), bf16[16,16,2496]{2,1,0:T(8,128)(2,1)S(1)}, u32[]{:S(2)}, u32[]{:S(2)}) %all-to-all-start.1) | async-done | bytes 1277984 | tf_op jit(solution)/shard_map/all_to_all | solution.py:486
  74.0 0.5 select.20
  74.5 0.9 copy-done.4
  75.4 4.3 %all-to-all-start.2 = ((bf16[16,8,2496]{2,1,0:T(8,128)(2,1)}), bf16[16,8,2496]{2,1,0:T(8,128)(2,1)S(1)}, u32[]{:S(2)}, u32[]{:S(2)}) async-start(bf16[16,8,2496]{2,1,0:T(8,128)(2,1)} %bitcast.80), calls=%async_computation.2 | async-start | bytes 1310720 | tf_op jit(solution)/shard_map/all_to_all | solution.py:525
  79.8 0.7 pad.13
  80.4 10.7 %all-to-all-done.2 = bf16[16,8,2496]{2,1,0:T(8,128)(2,1)S(1)} async-done(((bf16[16,8,2496]{2,1,0:T(8,128)(2,1)}), bf16[16,8,2496]{2,1,0:T(8,128)(2,1)S(1)}, u32[]{:S(2)}, u32[]{:S(2)}) %all-to-all-start.2) | async-done | bytes 639008 | tf_op jit(solution)/shard_map/all_to_all | solution.py:525
  91.4 1.1 student.1
  92.5 2.6 collective-permute-start
  95.1 0.9 collective-permute-done
  96.0 1.1 collective-permute-start.1
  97.1 0.6 dynamic_slice.22
  98.3 0.6 dynamic_slice.25
  99.7 0.7 collective-permute-start.4
  100.4 2.6 collective-permute-start.2
  103.1 1.4 fusion.2
  104.5 1.2 collective-permute-done.2
  105.7 0.7 fusion.8
  106.4 7.4 %first_forward.1 = (bf16[128,2432]{1,0:T(8,128)(2,1)}, bf16[2,128,1216]{2,1,0:T(8,128)(2,1)}, bf16[128,2432]{1,0:T(8,128)(2,1)S(1)}, f32[128,128]{1,0:T(8,128)S(1)}) custom-call(bf16[128,64]{1,0:T(8,128)(2,1)S(1)} %get-tuple-element.80.x_ref, bf16[2432,64]{1,0:T(8,128)(2,1)S(1)} %slice.59.proj_ref, f32[72,1216]{1,0:T(8,128)S(1)} %copy-done.3, ...), custom_call_target="tpu_custom_call" | custom-call | tf_op jit(solution)/shard_map/first_forward/pallas_call | solution.py:401
  113.8 4.0 %all-to-all-start.3 = ((bf16[4,32,2432]{2,1,0:T(8,128)(2,1)}), bf16[4,32,2432]{2,1,0:T(8,128)(2,1)S(1)}, u32[]{:S(2)}, u32[]{:S(2)}) async-start(bf16[4,32,2432]{2,1,0:T(8,128)(2,1)} %bitcast.92), calls=%async_computation.3 | async-start | bytes 1245184 | tf_op jit(solution)/shard_map/all_to_all | solution.py:75
  117.8 9.7 %all-to-all-done.3.parts_ref = bf16[4,32,2432]{2,1,0:T(8,128)(2,1)S(1)} async-done(((bf16[4,32,2432]{2,1,0:T(8,128)(2,1)}), bf16[4,32,2432]{2,1,0:T(8,128)(2,1)S(1)}, u32[]{:S(2)}, u32[]{:S(2)}) %all-to-all-start.3) | async-done | bytes 622624 | tf_op jit(solution)/shard_map/all_to_all | solution.py:75
  127.5 0.9 first_middle.1
  128.5 3.5 %all-to-all-start.4 = ((bf16[4,32,2432]{2,1,0:T(8,128)(2,1)}), bf16[4,32,2432]{2,1,0:T(8,128)(2,1)S(1)}, u32[]{:S(2)}, u32[]{:S(2)}) async-start(bf16[4,32,2432]{2,1,0:T(8,128)(2,1)} %get-tuple-element.45), calls=%async_computation.4 | async-start | bytes 1245184 | tf_op jit(solution)/shard_map/all_to_all | solution.py:75
  131.9 8.8 %all-to-all-done.4 = bf16[4,32,2432]{2,1,0:T(8,128)(2,1)S(1)} async-done(((bf16[4,32,2432]{2,1,0:T(8,128)(2,1)}), bf16[4,32,2432]{2,1,0:T(8,128)(2,1)S(1)}, u32[]{:S(2)}, u32[]{:S(2)}) %all-to-all-start.4) | async-done | bytes 622624 | tf_op jit(solution)/shard_map/all_to_all | solution.py:75
  140.8 10.7 %forward.1 = (bf16[128,2432]{1,0:T(8,128)(2,1)}, bf16[2,128,1216]{2,1,0:T(8,128)(2,1)}) custom-call(bf16[128,2432]{1,0:T(8,128)(2,1)S(1)} %bitcast.77, f32[1,2432]{1,0:T(1,128)S(1)} %get-tuple-element.88.scale_ref, f32[1,2432]{1,0:T(1,128)S(1)} %get-tuple-element.87.shift_ref, bf16[2,1216,2432]{2,1,0:T(8,128)(2,1)} %bitcast.89, ...), custom_call_target="tpu_custom_call" | custom-call | tf_op jit(solution)/shard_map/forward/pallas_call | solution.py:401
  151.6 11.5 %all_to_all.55.parts_ref = bf16[4,32,2432]{2,1,0:T(8,128)(2,1)S(1)} all-to-all(bf16[4,32,2432]{2,1,0:T(8,128)(2,1)} %bitcast.94), channel_id=1, replica_groups=mesh['fsdp'=8,'y'=4,'core'=2,'grp'=2] {'y'}, dimensions={0} | all-to-all | bytes 1245184 | tf_op jit(solution)/shard_map/all_to_all | solution.py:75
  163.1 1.0 last_middle.1
  164.1 3.4 %collective-permute-start.8 = (bf16[2432,384]{1,0:T(8,128)(2,1)}, bf16[2432,384]{1,0:T(8,128)(2,1)}, u32[]{:S(2)}, u32[]{:S(2)}) collective-permute-start(bf16[2432,384]{1,0:T(8,128)(2,1)} %all-gather.3.cloned.1.call-done.own), channel_id=1, source_target_pairs={{0,2},{2,0},{1,3},{3,1},{4,6},{6,4},{5,7},{7,5},{8,10},{10,8},{9,1... | collective-permute-start | bytes 5603336 | tf_op jit(solution)/shard_map/ppermute | solution.py:71
  167.5 3.6 %all-to-all-start.6 = ((bf16[4,32,2432]{2,1,0:T(8,128)(2,1)}), bf16[4,32,2432]{2,1,0:T(8,128)(2,1)S(1)}, u32[]{:S(2)}, u32[]{:S(2)}) async-start(bf16[4,32,2432]{2,1,0:T(8,128)(2,1)} %get-tuple-element.48), calls=%async_computation.6 | async-start | bytes 1245184 | tf_op jit(solution)/shard_map/all_to_all | solution.py:75
  171.4 1.1 collective-permute-done.7
  172.6 8.9 %all-to-all-done.6 = bf16[4,32,2432]{2,1,0:T(8,128)(2,1)S(1)} async-done(((bf16[4,32,2432]{2,1,0:T(8,128)(2,1)}), bf16[4,32,2432]{2,1,0:T(8,128)(2,1)S(1)}, u32[]{:S(2)}, u32[]{:S(2)}) %all-to-all-start.6) | async-done | bytes 622624 | tf_op jit(solution)/shard_map/all_to_all | solution.py:75
  181.5 4.9 %head_last.1 = (bf16[128,2432]{1,0:T(8,128)(2,1)}, f32[128,128]{1,0:T(8,128)S(1)}) custom-call(bf16[128,2432]{1,0:T(8,128)(2,1)S(1)} %bitcast.82, f32[2,2,384]{2,1,0:T(2,128)S(1)} %get-tuple-element.93.use_ref, bf16[2432,384]{1,0:T(8,128)(2,1)} %all-gather.3.cloned.1.call-done.own, bf16[2432,384]{1,0:T(8,128)(2,1)} %collective-permute-done.8.sib), custom_call_target="tpu_custom_call" | custom-call | tf_op jit(solution)/shard_map/head_last/pallas_call | solution.py:401
  186.4 12.6 %all_to_all.56.parts_ref = bf16[4,32,2432]{2,1,0:T(8,128)(2,1)S(1)} all-to-all(bf16[4,32,2432]{2,1,0:T(8,128)(2,1)} %bitcast.93), channel_id=1, replica_groups=mesh['fsdp'=8,'y'=4,'core'=2,'grp'=2] {'y'}, dimensions={0} | all-to-all | bytes 1245184 | tf_op jit(solution)/shard_map/all_to_all | solution.py:75
  199.0 1.2 last_back.1
  200.3 3.5 %all-to-all-start.8 = ((bf16[4,32,2432]{2,1,0:T(8,128)(2,1)}), bf16[4,32,2432]{2,1,0:T(8,128)(2,1)S(1)}, u32[]{:S(2)}, u32[]{:S(2)}) async-start(bf16[4,32,2432]{2,1,0:T(8,128)(2,1)} %get-tuple-element.54), calls=%async_computation.8 | async-start | bytes 1245184 | tf_op jit(solution)/shard_map/all_to_all | solution.py:75
  203.8 4.9 %head_first.1 = (bf16[128,2432]{1,0:T(8,128)(2,1)}, f32[128,128]{1,0:T(8,128)S(1)}) custom-call(bf16[128,2432]{1,0:T(8,128)(2,1)S(1)} %bitcast.78, f32[2,2,384]{2,1,0:T(2,128)S(1)} %get-tuple-element.92.use_ref, bf16[2432,384]{1,0:T(8,128)(2,1)} %all-gather.3.cloned.1.call-done.own, bf16[2432,384]{1,0:T(8,128)(2,1)} %collective-permute-done.8.sib), custom_call_target="tpu_custom_call" | custom-call | tf_op jit(solution)/shard_map/head_first/pallas_call | solution.py:401
  208.7 3.0 %all-to-all-done.8 = bf16[4,32,2432]{2,1,0:T(8,128)(2,1)S(1)} async-done(((bf16[4,32,2432]{2,1,0:T(8,128)(2,1)}), bf16[4,32,2432]{2,1,0:T(8,128)(2,1)S(1)}, u32[]{:S(2)}, u32[]{:S(2)}) %all-to-all-start.8) | async-done | bytes 622624 | tf_op jit(solution)/shard_map/all_to_all | solution.py:75
  211.7 10.9 %backward.1 = bf16[128,2432]{1,0:T(8,128)(2,1)} custom-call(bf16[128,2432]{1,0:T(8,128)(2,1)S(1)} %bitcast.83, f32[1,2432]{1,0:T(1,128)S(1)} %get-tuple-element.88.scale_ref, bf16[2,128,1216]{2,1,0:T(8,128)(2,1)} %get-tuple-element.55.slope, bf16[128,2432]{1,0:T(8,128)(2,1)} %get-tuple-element.58.head, bf16[2,1216,2432]{2,1,0:T(8,128)(2,1)} %bitcast.90, ...), custom_call_target="tpu_custom_call" | custom-call | tf_op jit(solution)/shard_map/backward/pallas_call | solution.py:401
  222.6 10.9 %all_to_all.57.parts_ref = bf16[4,32,2432]{2,1,0:T(8,128)(2,1)S(1)} all-to-all(bf16[4,32,2432]{2,1,0:T(8,128)(2,1)} %bitcast.91), channel_id=1, replica_groups=mesh['fsdp'=8,'y'=4,'core'=2,'grp'=2] {'y'}, dimensions={0} | all-to-all | bytes 1245184 | tf_op jit(solution)/shard_map/all_to_all | solution.py:75
  233.5 1.3 first_back.1
  234.8 3.7 %all-to-all-start.10 = ((bf16[4,32,2432]{2,1,0:T(8,128)(2,1)}), bf16[4,32,2432]{2,1,0:T(8,128)(2,1)S(1)}, u32[]{:S(2)}, u32[]{:S(2)}) async-start(bf16[4,32,2432]{2,1,0:T(8,128)(2,1)} %get-tuple-element.59), calls=%async_computation.10 | async-start | bytes 1245184 | tf_op jit(solution)/shard_map/all_to_all | solution.py:75
  238.6 7.1 %all-to-all-done.10 = bf16[4,32,2432]{2,1,0:T(8,128)(2,1)S(1)} async-done(((bf16[4,32,2432]{2,1,0:T(8,128)(2,1)}), bf16[4,32,2432]{2,1,0:T(8,128)(2,1)S(1)}, u32[]{:S(2)}, u32[]{:S(2)}) %all-to-all-start.10) | async-done | bytes 622624 | tf_op jit(solution)/shard_map/all_to_all | solution.py:75
  245.7 8.4 %first_backward.1 = f32[128,128]{1,0:T(8,128)S(1)} custom-call(s32[1]{0:T(128)} %bitcast.26.at_ref, f32[1]{0:T(128)} %bitcast.28.rest_ref, bf16[128,2432]{1,0:T(8,128)(2,1)S(1)} %bitcast.81, bf16[128,64]{1,0:T(8,128)(2,1)S(1)} %get-tuple-element.80.x_ref, f32[128,128]{1,0:T(8,128)S(1)} %get-tuple-element.60.back_ref, f32[128,128]{1,0:T(8,128)S(1)} %add.181.score_ref, ...), custom_call_target="tpu_custom_call" | custom-call | tf_op jit(solution)/shard_map/first_backward/pallas_call | solution.py:401
  254.1 0.4 collective-permute-start.9
  254.5 6.1 %collective-permute-start.3 = (bf16[128,64]{1,0:T(8,128)(2,1)S(1)}, bf16[128,64]{1,0:T(8,128)(2,1)S(1)}, u32[]{:S(2)}, u32[]{:S(2)}) collective-permute-start(bf16[128,64]{1,0:T(8,128)(2,1)S(1)} %get-tuple-element.81), channel_id=1, source_target_pairs={{0,2},{2,0},{1,3},{3,1},{4,6},{6,4},{5,7},{7,5},{8,10},{10,8},{9,1... | collective-permute-start | bytes 49160 | tf_op jit(solution)/shard_map/ppermute | solution.py:71
  260.6 1.9 collective-permute-start.10
  262.5 2.8 %collective-permute-done.10 = f32[128,128]{1,0:T(8,128)S(1)} collective-permute-done((f32[128,128]{1,0:T(8,128)S(1)}, f32[128,128]{1,0:T(8,128)S(1)}, u32[]{:S(2)}, u32[]{:S(2)}) %collective-permute-start.10) | collective-permute-done | bytes 65568 | tf_op jit(solution)/shard_map/ppermute | solution.py:689
  265.3 5.5 %collective-permute-start.11 = (f32[128,128]{1,0:T(8,128)S(1)}, f32[128,128]{1,0:T(8,128)S(1)}, u32[]{:S(2)}, u32[]{:S(2)}) collective-permute-start(f32[128,128]{1,0:T(8,128)S(1)} %add.183), channel_id=1, source_target_pairs={{0,2},{2,0},{1,3},{3,1},{4,6},{6,4},{5,7},{7,5},{8,10},{10,8},{9,1... | collective-permute-start | bytes 196616 | tf_op jit(solution)/shard_map/ppermute | solution.py:71
  270.9 0.7 copy.78
  271.9 0.7 copy.80
  272.6 0.7 copy.79
  (97 shorter events, 4.4 us)
Async XLA Ops:
  7.2 89.9 %copy-start = (bf16[1,256,64]{1,2,0:T(8,128)(2,1)S(1)}, bf16[1,256,64]{1,2,0:T(8,128)(2,1)}, u32[]{:S(2)}) copy-start(bf16[1,256,64]{1,2,0:T(8,128)(2,1)} %param.19) | copy-start | bytes 98308
  7.2 13.2 %copy-start.13 = (bf16[64,304]{1,0:T(8,128)(2,1)S(1)}, bf16[64,304]{1,0:T(8,128)(2,1)}, u32[]{:S(2)}) copy-start(bf16[64,304]{1,0:T(8,128)(2,1)} %param.21) | copy-start | bytes 116740
  8.2 1.1 copy-start.6
  9.3 1.0 copy-start.9
  10.2 10.2 %copy-start.14 = (bf16[64,304]{1,0:T(8,128)(2,1)S(1)}, bf16[64,304]{1,0:T(8,128)(2,1)}, u32[]{:S(2)}) copy-start(bf16[64,304]{1,0:T(8,128)(2,1)} %param.22) | copy-start | bytes 116740
  10.2 10.4 %copy-start.15 = (bf16[64,304]{1,0:T(8,128)(2,1)S(1)}, bf16[64,304]{1,0:T(8,128)(2,1)}, u32[]{:S(2)}) copy-start(bf16[64,304]{1,0:T(8,128)(2,1)} %param.23) | copy-start | bytes 116740
  11.6 33.2 %copy-start.7 = (bf16[152,1216]{1,0:T(8,128)(2,1)S(1)}, bf16[152,1216]{1,0:T(8,128)(2,1)}, u32[]{:S(2)}) copy-start(bf16[152,1216]{1,0:T(8,128)(2,1)} %w1_ref.1) | copy-start | bytes 1108996
  11.6 33.2 %copy-start.8 = (bf16[1216,152]{0,1:T(8,128)(2,1)S(1)}, bf16[1216,152]{0,1:T(8,128)(2,1)}, u32[]{:S(2)}) copy-start(bf16[1216,152]{0,1:T(8,128)(2,1)} %param.26) | copy-start | bytes 1108996
  11.7 16.3 %all-to-all-start = ((bf16[16,8,912]{2,1,0:T(8,128)(2,1)}), bf16[16,8,912]{2,1,0:T(8,128)(2,1)S(1)}, u32[]{:S(2)}, u32[]{:S(2)}) async-start(bf16[16,8,912]{2,1,0:T(8,128)(2,1)} %bitcast.11), calls=%async_computation | async-start | bytes 524288 | tf_op jit(solution)/shard_map/all_to_all | solution.py:460
  28.2 20.3 %copy-start.18 = (s32[16]{0:T(128)S(1)}, s32[16]{0:T(128)}, u32[]{:S(2)}) copy-start(s32[16]{0:T(128)} %param.17) | copy-start | bytes 196
  46.9 1.2 copy-start.5
  48.0 58.4 %collective-permute-start.5 = (bf16[2,1216,2432]{2,1,0:T(8,128)(2,1)}, bf16[2,1216,2432]{2,1,0:T(8,128)(2,1)}, u32[]{:S(2)}, u32[]{:S(2)}) collective-permute-start(bf16[2,1216,2432]{2,1,0:T(8,128)(2,1)} %own.1), channel_id=1, source_target_pairs={{0,2},{2,0},{1,3},{3,1},{4,6},{6,4},{5,7},{7,5},{8,10},{10,8},{9,1... | collective-permute-start | bytes 35487752 | tf_op jit(solution)/shard_map/ppermute | solution.py:71
  48.2 83.7 %collective-permute-start.6 = (bf16[2,1216,2432]{2,1,0:T(8,128)(2,1)}, bf16[2,1216,2432]{2,1,0:T(8,128)(2,1)}, u32[]{:S(2)}, u32[]{:S(2)}) collective-permute-start(bf16[2,1216,2432]{2,1,0:T(8,128)(2,1)} %bitcast.87), channel_id=1, source_target_pairs={{0,2},{2,0},{1,3},{3,1},{4,6},{6,4},{5,7},{7,5},{8,10},{10,8},{9,1... | collective-permute-start | bytes 35487752 | tf_op jit(solution)/shard_map/ppermute | solution.py:71
  49.0 25.0 %all-to-all-start.1 = ((bf16[16,16,2496]{2,1,0:T(8,128)(2,1)}), bf16[16,16,2496]{2,1,0:T(8,128)(2,1)S(1)}, u32[]{:S(2)}, u32[]{:S(2)}) async-start(bf16[16,16,2496]{2,1,0:T(8,128)(2,1)} %bitcast.84), calls=%async_computation.1 | async-start | bytes 2621440 | tf_op jit(solution)/shard_map/all_to_all | solution.py:486
  53.7 4.7 %copy-start.11 = (bf16[1,256,64]{1,2,0:T(8,128)(2,1)S(1)}, bf16[1,256,64]{1,2,0:T(8,128)(2,1)}, u32[]{:S(2)}) copy-start(bf16[1,256,64]{1,2,0:T(8,128)(2,1)} %param.16) | copy-start | bytes 98308
  58.5 1.0 copy-start.2
  59.1 1.1 copy-start.10
  60.2 19.6 %copy-start.12 = (bf16[152,304]{1,0:T(8,128)(2,1)S(1)}, bf16[152,304]{1,0:T(8,128)(2,1)}, u32[]{:S(2)}) copy-start(bf16[152,304]{1,0:T(8,128)(2,1)} %param.30) | copy-start | bytes 277252
  74.5 0.9 copy-start.4
  75.4 19.7 %copy-start.17 = (s32[16]{0:T(128)S(1)}, s32[16]{0:T(128)}, u32[]{:S(2)}) copy-start(s32[16]{0:T(128)} %param.18) | copy-start | bytes 196
  75.4 24.3 %copy-start.3 = (f32[72,1216]{1,0:T(8,128)S(1)}, f32[72,1216]{1,0:T(8,128)}, u32[]{:S(2)}) copy-start(f32[72,1216]{1,0:T(8,128)} %copy-done.2) | copy-start | bytes 1050628
  75.4 15.7 %all-to-all-start.2 = ((bf16[16,8,2496]{2,1,0:T(8,128)(2,1)}), bf16[16,8,2496]{2,1,0:T(8,128)(2,1)S(1)}, u32[]{:S(2)}, u32[]{:S(2)}) async-start(bf16[16,8,2496]{2,1,0:T(8,128)(2,1)} %bitcast.80), calls=%async_computation.2 | async-start | bytes 1310720 | tf_op jit(solution)/shard_map/all_to_all | solution.py:525
  79.7 84.4 %all-gather.3.cloned.1.call-start = ((), (), s32[]{:S(2)}) async-start(), calls=%async_computation.11 | async-start | bytes 1984512 | tf_op jit(solution)/shard_map/all_gather | solution.py:531
  92.5 3.5 %collective-permute-start = (f32[128,64]{1,0:T(8,128)S(1)}, f32[128,64]{1,0:T(8,128)S(1)}, u32[]{:S(2)}, u32[]{:S(2)}) collective-permute-start(f32[128,64]{1,0:T(8,128)S(1)} %constant_dynamic-slice_fusion.1), channel_id=1, source_target_pairs={{0,2},{2,0},{1,3},{3,1},{4,6},{6,4},{5,7},{7,5},{8,10},{10,8},{9,1... | collective-permute-start | bytes 98312 | tf_op jit(solution)/shard_map/ppermute | solution.py:71
  96.0 4.4 %collective-permute-start.1 = (f32[128,64]{1,0:T(8,128)S(1)}, f32[128,64]{1,0:T(8,128)S(1)}, u32[]{:S(2)}, u32[]{:S(2)}) collective-permute-start(f32[128,64]{1,0:T(8,128)S(1)} %dynamic-slice_add_fusion), channel_id=1, source_target_pairs={{0,4},{4,0},{8,12},{12,8},{1,5},{5,1},{9,13},{13,9},{2,6},{6,2},{1... | collective-permute-start | bytes 98312 | tf_op jit(solution)/shard_map/ppermute | solution.py:544
  99.7 6.7 %collective-permute-start.4 = (f32[72,1216]{1,0:T(8,128)S(1)}, f32[72,1216]{1,0:T(8,128)S(1)}, u32[]{:S(2)}, u32[]{:S(2)}) collective-permute-start(f32[72,1216]{1,0:T(8,128)S(1)} %copy-done.3), channel_id=1, source_target_pairs={{0,2},{2,0},{1,3},{3,1},{4,6},{6,4},{5,7},{7,5},{8,10},{10,8},{9,1... | collective-permute-start | bytes 1050632 | tf_op jit(solution)/shard_map/ppermute | solution.py:71
  100.4 5.3 %collective-permute-start.2 = (f32[128,64]{1,0:T(8,128)S(1)}, f32[128,64]{1,0:T(8,128)S(1)}, u32[]{:S(2)}, u32[]{:S(2)}) collective-permute-start(f32[128,64]{1,0:T(8,128)S(1)} %add.177), channel_id=1, source_target_pairs={{0,8},{8,0},{4,12},{12,4},{1,9},{9,1},{5,13},{13,5},{2,10},{10,2},... | collective-permute-start | bytes 98312 | tf_op jit(solution)/shard_map/ppermute | solution.py:545
  113.8 13.7 %all-to-all-start.3 = ((bf16[4,32,2432]{2,1,0:T(8,128)(2,1)}), bf16[4,32,2432]{2,1,0:T(8,128)(2,1)S(1)}, u32[]{:S(2)}, u32[]{:S(2)}) async-start(bf16[4,32,2432]{2,1,0:T(8,128)(2,1)} %bitcast.92), calls=%async_computation.3 | async-start | bytes 1245184 | tf_op jit(solution)/shard_map/all_to_all | solution.py:75
  128.5 12.3 %all-to-all-start.4 = ((bf16[4,32,2432]{2,1,0:T(8,128)(2,1)}), bf16[4,32,2432]{2,1,0:T(8,128)(2,1)S(1)}, u32[]{:S(2)}, u32[]{:S(2)}) async-start(bf16[4,32,2432]{2,1,0:T(8,128)(2,1)} %get-tuple-element.45), calls=%async_computation.4 | async-start | bytes 1245184 | tf_op jit(solution)/shard_map/all_to_all | solution.py:75
  151.5 19.6 %copy-start.16 = (f32[2,304]{1,0:T(2,128)S(1)}, f32[2,304]{1,0:T(2,128)}, u32[]{:S(2)}) copy-start(f32[2,304]{1,0:T(2,128)} %param.31) | copy-start | bytes 7300
  151.6 19.8 %copy-start.19 = (s32[1,2]{1,0:T(1,128)S(1)}, s32[1,2]{1,0:T(1,128)}, u32[]{:S(2)}) copy-start(s32[1,2]{1,0:T(1,128)} %param.20) | copy-start | bytes 28
  164.1 17.4 %collective-permute-start.8 = (bf16[2432,384]{1,0:T(8,128)(2,1)}, bf16[2432,384]{1,0:T(8,128)(2,1)}, u32[]{:S(2)}, u32[]{:S(2)}) collective-permute-start(bf16[2432,384]{1,0:T(8,128)(2,1)} %all-gather.3.cloned.1.call-done.own), channel_id=1, source_target_pairs={{0,2},{2,0},{1,3},{3,1},{4,6},{6,4},{5,7},{7,5},{8,10},{10,8},{9,1... | collective-permute-start | bytes 5603336 | tf_op jit(solution)/shard_map/ppermute | solution.py:71
  167.5 14.0 %all-to-all-start.6 = ((bf16[4,32,2432]{2,1,0:T(8,128)(2,1)}), bf16[4,32,2432]{2,1,0:T(8,128)(2,1)S(1)}, u32[]{:S(2)}, u32[]{:S(2)}) async-start(bf16[4,32,2432]{2,1,0:T(8,128)(2,1)} %get-tuple-element.48), calls=%async_computation.6 | async-start | bytes 1245184 | tf_op jit(solution)/shard_map/all_to_all | solution.py:75
  171.1 1.4 collective-permute-start.7
  200.3 11.4 %all-to-all-start.8 = ((bf16[4,32,2432]{2,1,0:T(8,128)(2,1)}), bf16[4,32,2432]{2,1,0:T(8,128)(2,1)S(1)}, u32[]{:S(2)}, u32[]{:S(2)}) async-start(bf16[4,32,2432]{2,1,0:T(8,128)(2,1)} %get-tuple-element.54), calls=%async_computation.8 | async-start | bytes 1245184 | tf_op jit(solution)/shard_map/all_to_all | solution.py:75
  234.8 10.9 %all-to-all-start.10 = ((bf16[4,32,2432]{2,1,0:T(8,128)(2,1)}), bf16[4,32,2432]{2,1,0:T(8,128)(2,1)S(1)}, u32[]{:S(2)}, u32[]{:S(2)}) async-start(bf16[4,32,2432]{2,1,0:T(8,128)(2,1)} %get-tuple-element.59), calls=%async_computation.10 | async-start | bytes 1245184 | tf_op jit(solution)/shard_map/all_to_all | solution.py:75
  245.7 27.6 %copy-start.1 = (bf16[1,256,64]{1,2,0:T(8,128)(2,1)S(1)}, bf16[1,256,64]{1,2,0:T(8,128)(2,1)}, u32[]{:S(2)}) copy-start(bf16[1,256,64]{1,2,0:T(8,128)(2,1)} %param.19) | copy-start | bytes 98308
  254.1 6.5 %collective-permute-start.9 = (f32[128,128]{1,0:T(8,128)S(1)}, f32[128,128]{1,0:T(8,128)S(1)}, u32[]{:S(2)}, u32[]{:S(2)}) collective-permute-start(f32[128,128]{1,0:T(8,128)S(1)} %first_backward.1), channel_id=1, source_target_pairs={{0,4},{4,0},{8,12},{12,8},{1,5},{5,1},{9,13},{13,9},{2,6},{6,2},{1... | collective-permute-start | bytes 196616 | tf_op jit(solution)/shard_map/ppermute | solution.py:688
  254.5 8.0 %collective-permute-start.3 = (bf16[128,64]{1,0:T(8,128)(2,1)S(1)}, bf16[128,64]{1,0:T(8,128)(2,1)S(1)}, u32[]{:S(2)}, u32[]{:S(2)}) collective-permute-start(bf16[128,64]{1,0:T(8,128)(2,1)S(1)} %get-tuple-element.81), channel_id=1, source_target_pairs={{0,2},{2,0},{1,3},{3,1},{4,6},{6,4},{5,7},{7,5},{8,10},{10,8},{9,1... | collective-permute-start | bytes 49160 | tf_op jit(solution)/shard_map/ppermute | solution.py:71
  260.6 4.7 %collective-permute-start.10 = (f32[128,128]{1,0:T(8,128)S(1)}, f32[128,128]{1,0:T(8,128)S(1)}, u32[]{:S(2)}, u32[]{:S(2)}) collective-permute-start(f32[128,128]{1,0:T(8,128)S(1)} %add.182), channel_id=1, source_target_pairs={{0,8},{8,0},{4,12},{12,4},{1,9},{9,1},{5,13},{13,5},{2,10},{10,2},... | collective-permute-start | bytes 196616 | tf_op jit(solution)/shard_map/ppermute | solution.py:689
  265.3 6.5 %collective-permute-start.11 = (f32[128,128]{1,0:T(8,128)S(1)}, f32[128,128]{1,0:T(8,128)S(1)}, u32[]{:S(2)}, u32[]{:S(2)}) collective-permute-start(f32[128,128]{1,0:T(8,128)S(1)} %add.183), channel_id=1, source_target_pairs={{0,2},{2,0},{1,3},{3,1},{4,6},{6,4},{5,7},{7,5},{8,10},{10,8},{9,1... | collective-permute-start | bytes 196616 | tf_op jit(solution)/shard_map/ppermute | solution.py:71
Sparse Core Ops, SparseCore 0:
  91.2 66.0 all-gather.2

commit v2 on v1

--- a/solution.py
+++ b/solution.py
@@ -94,14 +94,21 @@
     return [(source.at[layer], target.at[side]) for side, source in enumerate(sources)]
 
 
-def turned(values):
-    extent = values.shape[1]
+def identity(extent):
     row = lax.broadcasted_iota(jnp.int32, (extent, extent), 0)
     col = lax.broadcasted_iota(jnp.int32, (extent, extent), 1)
-    return dot_back((row == col).astype(BF), values)
-
-
-def product_kernel(at_ref, packed_ref, w1_ref, w2_ref, out_ref, bias_ref):
+    return (row == col).astype(BF)
+
+
+def turned(values):
+    return dot_back(identity(values.shape[1]), values)
+
+
+def turned_wide(values):
+    return dot_across(values, identity(values.shape[0]))
+
+
+def product_kernel(at_ref, packed_ref, w1_ref, w2_ref, out, bias_ref, out_ref, sems):
     blocks, columns, _ = packed_ref.shape
     rows, hidden = w1_ref.shape
     cells = out_ref.shape[0] // STEPS
@@ -136,60 +143,132 @@
     out_ref[:, :hidden] = dot_across(left_in.astype(BF), w1_ref[...]).astype(BF)
     out_ref[:, hidden : hidden + gap] = jnp.zeros((cells * STEPS, gap), BF)
     out_ref[:, hidden + gap :] = dot_across(left_out.astype(BF), w2_ref[...]).astype(BF)
+    send = pltpu.make_async_copy(out_ref, out, sems.at[0])
+    send.start()
     bias_ref[...] = dot_across(shift, w1_ref[...]).astype(BF)
-
-
-def select_kernel(parts_ref, pick_ref, pick_bias_ref, bias_ref, out_ref):
+    send.wait()
+
+
+def select_kernel(step_ref, parts_ref, bias_ref, out, out_ref, sems):
+    samples, piece, _ = parts_ref.shape
     hidden = bias_ref.shape[1]
+    chunk = piece // STEPS
+
+    def at_step(extent):
+        row = lax.broadcasted_iota(jnp.int32, (samples * 8, extent), 0)
+        step = jnp.zeros((samples * 8, extent), jnp.int32)
+        for sample in range(samples):
+            step = jnp.where(row // 8 == sample, step_ref[sample] - 1, step)
+        return row % 8, lax.broadcasted_iota(jnp.int32, (samples * 8, extent), 1), step
+
     total = parts_ref[0].astype(F32)
-    for source in range(1, parts_ref.shape[0]):
+    for source in range(1, samples):
         total = total + parts_ref[source].astype(F32)
-    chosen = dot(pick_ref[...], total.astype(BF))
+    place, col, step = at_step(piece)
+    pick = ((col == place * STEPS + step) & (place < chunk)).astype(BF)
+    chosen = dot(pick, total.astype(BF))
     out_ref[...] = chosen.astype(BF)
-    out_ref[:, :hidden] = (chosen[:, :hidden] + dot(pick_bias_ref[...], bias_ref[...])).astype(BF)
-
-
-def student_kernel(x_ref, inverse_ref, mat_ref, out_ref):
-    cells = x_ref.shape[1]
+    place, col, step = at_step(8)
+    pick = ((col == step) & (place == chunk)).astype(BF)
+    out_ref[:, :hidden] = (chosen[:, :hidden] + dot(pick, bias_ref[...])).astype(BF)
+    send = pltpu.make_async_copy(out_ref, out, sems.at[0])
+    send.start()
+    send.wait()
+
+
+def student_kernel(where_ref, x_ref, packed_ref, mat_ref, mine_ref, other_ref, all_ref):
+    cells, seq = x_ref.shape
+    width = packed_ref.shape[0]
     lanes, wide = mat_ref.shape
     hidden = wide // 2 - (wide // 2) % 64
     gap = wide - 2 * hidden
     group = lanes * 4 // cells
+    x = turned_wide(x_ref[...]).astype(BF)
+    proj = packed_ref[:, :cells]
+    centered = proj.astype(F32)
+    centered = centered - jnp.mean(centered, axis=0, keepdims=True)
+    high, low = split(centered)
+    gram = dot_across(high, high) + (dot_across(high, low) + dot_across(low, high))
+    direct = dot_across(proj, packed_ref[:, 2 * cells : 3 * cells])
+
+    def times(matrix):
+        first, second = split(matrix)
+        return dot(x, first) + dot(x, second)
+
+    var = jnp.sum(times(gram) * x.astype(F32), axis=1, keepdims=True) / width
+    inverse = lax.rsqrt(jnp.maximum(var, 0.0) + 1e-06)
     row = lax.broadcasted_iota(jnp.int32, (cells, lanes), 0)
     col = lax.broadcasted_iota(jnp.int32, (cells, lanes), 1)
     spread = (col == group * (row // 4) + row % 4).astype(BF)
     bias_col = lax.broadcasted_iota(jnp.int32, (8, lanes), 1)
     bias = dot((bias_col % group == 4).astype(BF), mat_ref[:, :hidden])[:1]
-    x = dot(x_ref[...], spread).astype(BF)
-    z = inverse_ref[...] * dot(x, mat_ref[:, :hidden]) + bias
+    z = inverse * dot(dot(x, spread).astype(BF), mat_ref[:, :hidden]) + bias
     active = gelu_both(z)[0].astype(BF)
     high, low = split(dot_back(active, mat_ref[:, hidden + gap :]))
-    out_ref[...] = dot_back(high, spread) + dot_back(low, spread)
-
-
-def first_product_kernel(proj_ref, scale_ref, shift_ref, up, out_ref, up_ref, sems):
-    cells = proj_ref.shape[1]
+    all_ref[...] = dot_back(high, spread) + dot_back(low, spread) + 0.125 * times(direct)
+    half = seq // 2
+    core = where_ref[2]
+    mine_ref[...] = all_ref[pl.ds(pl.multiple_of(core * half, half), half), :]
+    other_ref[...] = all_ref[pl.ds(pl.multiple_of((1 - core) * half, half), half), :]
+
+
+def first_product_kernel(packed_ref, up, out_ref, vector_ref, up_ref, left_ref, sems):
+    blocks, columns, _ = packed_ref.shape
+    cells = out_ref.shape[0] - 8
     stream = Stream(matrices(0, (up,), up_ref), sems)
-    proj = turned(proj_ref[...])
-    centered = proj - jnp.mean(proj, axis=1, keepdims=True)
-    left = (centered * (1.0 + scale_ref[...])).astype(BF)
-    shift = jnp.broadcast_to(shift_ref[...], (16, shift_ref.shape[1])).astype(BF)
-    left = jnp.concatenate([left, shift], axis=0)
-    stream.next()
-    out_ref[...] = dot_back(left, up_ref[0])[: cells + 8]
+    total = jnp.zeros((columns, cells), F32)
+    for block in range(blocks):
+        total = total + packed_ref[block, :, cells : 2 * cells].astype(F32)
+    mean = jnp.sum(total, axis=0, keepdims=True) / (blocks * columns)
+
+    def vector(kind, block):
+        at = kind * blocks + block
+        return packed_ref[at // 3, :, 3 * cells + at % 3 : 3 * cells + at % 3 + 1].astype(F32)
+
+    for block in range(blocks):
+        centered = packed_ref[block, :, cells : 2 * cells].astype(F32) - mean
+        scaled = centered * (1.0 + vector(1, block))
+        shift = jnp.broadcast_to(vector(0, block), (columns, 8))
+        left_ref[block * columns : (block + 1) * columns, :] = jnp.concatenate(
+            [scaled, shift], axis=1
+        ).astype(BF)
+    for source in range(blocks):
+        rows = turned(packed_ref[source, :, 3 * cells : 3 * cells + 3 * LAYERS])
+        for third in range(3):
+            kind, block = divmod(source * 3 + third, blocks)
+            for layer in range(LAYERS):
+                vector_ref[
+                    3 * layer + kind : 3 * layer + kind + 1, block * columns : (block + 1) * columns
+                ] = rows[3 * layer + third : 3 * layer + third + 1]
+    left = turned(left_ref[...]).astype(BF)
+    stream.next()
+    out_ref[...] = dot_back(left, up_ref[0])
 
 
 def first_forward_kernel(
-    x_ref, proj_ref, mat_own, mat_sib, own, sib, y_out, slope_out, g_ref, back_ref, w_ref, y_ref, slope_ref, sems
+    where_ref, student_ref, teacher_ref, velocity_ref, x_ref, noise_ref, packed_ref, mat_own, mat_sib, own, sib,
+    y_out, slope_out, latents_ref, noised_ref, g_ref, back_ref,
+    w_ref, y_ref, slope_ref, both_ref, sems
 ):
-    cells = x_ref.shape[1]
+    cells, seq = x_ref.shape
+    half = seq // 2
     stream = Stream(matrices(0, (own, sib), w_ref), sems)
-    x = x_ref[...]
-    g_0 = dot_back(x, proj_ref[...]).astype(BF)
+    sample = where_ref[0]
+    sigma_s = student_ref[sample].astype(F32) * 0.25
+    sigma_t = teacher_ref[sample].astype(F32) * 0.001
+    both_ref[0] = turned_wide(x_ref[...])
+    both_ref[1] = turned_wide(noise_ref[...])
+    mine = pl.ds(pl.multiple_of(where_ref[2] * half, half), half)
+    latents = (both_ref[0, mine, :] - sigma_s * velocity_ref[...]).astype(BF)
+    latents_ref[...] = latents
+    x = ((1.0 - sigma_t) * latents.astype(F32) + sigma_t * both_ref[1, mine, :]).astype(BF)
+    noised_ref[...] = x
+    proj = packed_ref[:, cells : 2 * cells]
+    g_0 = dot_back(x, proj).astype(BF)
     g_ref[...] = g_0
     normed, inverse = normalize(g_0.astype(F32))
-    back_ref[:, :cells] = dot(normed.astype(BF), proj_ref[...])
-    back_ref[:, cells:] = jnp.broadcast_to(inverse, (x.shape[0], cells))
+    back_ref[:, :cells] = dot(normed.astype(BF), proj)
+    back_ref[:, cells:] = jnp.broadcast_to(inverse, (half, cells))
     twice = jnp.concatenate([x, x], axis=1)
     actives = []
     for side, mat_ref in enumerate((mat_own, mat_sib)):
@@ -211,14 +290,14 @@
 
 
 def forward_kernel(
-    g_ref, scale_ref, shift_ref, up_own, up_sib, down_own, down_sib, y_out, slope_out,
+    g_ref, vector_ref, up_own, up_sib, down_own, down_sib, y_out, slope_out,
     up_ref, down_ref, y_ref, slope_ref, sems
 ):
     stream = Stream(
         matrices(1, (up_own, up_sib), up_ref) + matrices(1, (down_own, down_sib), down_ref), sems
     )
     normed, _ = normalize(g_ref[...].astype(F32))
-    u = (normed * (1.0 + scale_ref[...]) + shift_ref[...]).astype(BF)
+    u = (normed * (1.0 + vector_ref[4:5]) + vector_ref[3:4]).astype(BF)
     actives = []
     for side in range(2):
         stream.next()
@@ -238,7 +317,7 @@
 
 
 def backward_kernel(
-    dy_ref, scale_ref, slope, head, up_own, up_sib, down_own, down_sib, out,
+    dy_ref, vector_ref, slope, head, up_own, up_sib, down_own, down_sib, out,
     up_ref, down_ref, slope_ref, head_ref, out_ref, sems
 ):
     stream = Stream(
@@ -259,15 +338,15 @@
     stream.next()
     du = du + dot(dz[1], up_ref[1])
     stream.next()
-    out_ref[...] = (du * (1.0 + scale_ref[...]) + head_ref[...].astype(F32)).astype(BF)
+    out_ref[...] = (du * (1.0 + vector_ref[4:5]) + head_ref[...].astype(F32)).astype(BF)
     send = pltpu.make_async_copy(out_ref, out, sems.at[6])
     send.start()
     send.wait()
 
 
 def first_backward_kernel(
-    at_ref, rest_ref, dy_ref, x_ref, back_ref, score_ref, direct_ref, mat_own, mat_sib, slope, own, sib,
-    out_ref, w_ref, slope_ref, sems
+    where_ref, teacher_ref, dy_ref, x_ref, back_ref, score_1, score_2, direct_ref, mat_own, mat_sib, slope, own, sib,
+    out_ref, w_ref, slope_ref, all_ref, sems
 ):
     cells = x_ref.shape[1]
     stream = Stream([(slope, slope_ref)] + matrices(0, (own, sib), w_ref), sems)
@@ -282,15 +361,16 @@
         total = part if total is None else total + part
     inverse = back_ref[:, cells : cells + 1]
     cross = inverse * jnp.sum(x_ref[...].astype(F32) * total, axis=1, keepdims=True) / dy.shape[1]
-    rest = rest_ref[0]
-    out_ref[:, :cells] = rest * (inverse * (total - back_ref[:, :cells] * cross))
-    out_ref[:, cells:] = score_ref[:, :cells]
+    rest = 1.0 - teacher_ref[where_ref[0]].astype(F32) * 0.001
+    all_ref[:, :cells] = rest * (inverse * (total - back_ref[:, :cells] * cross))
+    all_ref[:, cells:] = score_1[:, :cells] + score_2[:, :cells]
     rows = direct_ref.shape[0]
-    mine = pl.ds(pl.multiple_of(at_ref[0] * rows, rows), rows)
-    out_ref[mine, :cells] += rest * direct_ref[...]
-
-
-def modulation_kernel(cond_s_ref, cond_t_ref, s_ref, t_ref, out_ref):
+    mine = pl.ds(pl.multiple_of(where_ref[1] * rows, rows), rows)
+    all_ref[mine, :cells] += rest * direct_ref[...]
+    out_ref[...] = all_ref[...].T[: out_ref.shape[0]]
+
+
+def modulation_kernel(cond_s_ref, cond_t_ref, s_ref, t_ref, in_s, in_t, out_proj, out_ref, proj_ref):
     samples = cond_t_ref.shape[0]
 
     def product(cond, weight):
@@ -313,6 +393,8 @@
         part = product(cond_t_ref[...], t_ref[layer])
         total = total + dot(place(samples, layer, False), part)
     out_ref[...] = total.astype(BF)
+    stacked = jnp.concatenate([in_s[...], in_t[...], out_proj[...]], axis=0)
+    proj_ref[...] = turned_wide(stacked).astype(BF)
 
 
 def sum_parts(parts_ref):
@@ -327,36 +409,42 @@
         all_ref[target] = values
 
 
-def first_middle_kernel(at_ref, parts_ref, g_ref, gate_ref, mine_ref, all_ref):
+def first_middle_kernel(where_ref, parts_ref, g_ref, vector_ref, mine_ref, all_ref):
     rows = mine_ref.shape[0]
-    before = g_ref[pl.ds(pl.multiple_of(at_ref[0] * rows, rows), rows), :].astype(F32)
-    after = (before + gate_ref[...] * sum_parts(parts_ref)).astype(BF)
+    before = g_ref[pl.ds(pl.multiple_of(where_ref[1] * rows, rows), rows), :].astype(F32)
+    after = (before + vector_ref[2:3] * sum_parts(parts_ref)).astype(BF)
     mine_ref[...] = after
     share(after, all_ref)
 
 
-def last_middle_kernel(parts_ref, g_ref, gate_ref, mine_ref, all_ref):
-    after = (g_ref[...].astype(F32) + gate_ref[...] * sum_parts(parts_ref)).astype(BF)
+def last_middle_kernel(parts_ref, g_ref, vector_ref, mine_ref, all_ref):
+    after = (g_ref[...].astype(F32) + vector_ref[5:6] * sum_parts(parts_ref)).astype(BF)
     mine_ref[...] = after
     share(after, all_ref)
 
 
-def last_back_kernel(parts_ref, g_ref, gate_ref, grad_ref, all_ref):
+def last_back_kernel(parts_ref, g_ref, vector_ref, grad_ref, all_ref):
     normed, inverse = normalize(g_ref[...].astype(F32))
     grad = ln_back(sum_parts(parts_ref), normed, inverse)
     grad_ref[...] = grad
-    share((gate_ref[...] * grad).astype(BF), all_ref)
-
-
-def first_back_kernel(parts_ref, g_ref, old_ref, gate_ref, proj_ref, direct_ref, all_ref):
+    share((vector_ref[5:6] * grad).astype(BF), all_ref)
+
+
+def first_back_kernel(parts_ref, g_ref, old_ref, vector_ref, packed_ref, direct_ref, all_ref):
     normed, inverse = normalize(g_ref[...].astype(F32))
     grad = old_ref[...] + ln_back(sum_parts(parts_ref), normed, inverse)
-    direct_ref[...] = dot(grad.astype(BF), proj_ref[...])
-    share((gate_ref[...] * grad).astype(BF), all_ref)
-
-
-def head_kernel(g_ref, use_ref, own, sib, back_out, score_ref, weight_ref, back_ref, sems):
+    cells = direct_ref.shape[1]
+    direct_ref[...] = dot(grad.astype(BF), packed_ref[:, cells : 2 * cells])
+    share((vector_ref[2:3] * grad).astype(BF), all_ref)
+
+
+def head_kernel(layer, pick_ref, g_ref, out_own, out_sib, own, sib, back_out, score_ref, weight_ref, back_ref, use_ref, sems):
     stream = Stream([(own, weight_ref.at[0]), (sib, weight_ref.at[1])], sems)
+    use_ref[...] = jnp.zeros(use_ref.shape, F32)
+    for side, outs in enumerate((out_own, out_sib)):
+        for head in range(2):
+            use = jnp.where(pick_ref[head] == layer, 1.0, 0.0)
+            use_ref[side, head : head + 1, : outs.shape[1]] = use * outs[head : head + 1, :]
     normed, _ = normalize(g_ref[...].astype(F32))
     quantised = normed.astype(BF)
     back = None
@@ -451,22 +539,39 @@
     sig_steps = (1 + jnp.arange(STEPS)).astype(F32) * 0.25
     cond_s = jax.nn.silu(embed_block(1000.0 * sig_steps, width, rows, start))
     cond_t = jax.nn.silu(embed_block(1000.0 * sig_all_t, width, rows, start))
-    mod_part = here(
+    where = jnp.stack([sample, at_y, at_core]).astype(jnp.int32)
+    block = sample * rows // columns
+    places = [block, sample * rows // rows % (columns // rows)]
+    for offset in (0, 8, 16):
+        places += [(block + offset) // 3, (block + offset) % 3]
+    places = jnp.stack(places).astype(jnp.int32)
+    spare = -columns % 128
+    head_block = jnp.pad(d_w1, ((0, 0), (0, spare)))
+    picks = layer_pick[0]
+    mod_part, projections = here(
         modulation_kernel,
         "modulation",
-        array((samples * 8, s_mod.shape[1]), BF),
-        (jnp.pad(cond_s, ((0, 16 - STEPS), (0, 0))), cond_t, s_mod, t_mod),
-    ).reshape(samples, 8, s_mod.shape[1])
+        (array((samples * 8, s_mod.shape[1]), BF), array((columns, 3 * cells), BF)),
+        (
+            jnp.pad(cond_s, ((0, 16 - STEPS), (0, 0))),
+            cond_t,
+            s_mod,
+            t_mod,
+            in_proj_s,
+            in_proj_t,
+            out_proj,
+        ),
+    )
+    mod_part, projections, where, places, head_block, picks = lax.optimization_barrier(
+        (mod_part, projections, where, places, head_block, picks)
+    )
+    mod_part = mod_part.reshape(samples, 8, s_mod.shape[1])
     mods = jnp.sum(lax.all_to_all(mod_part, SAMPLE, 0, 0).astype(F32), axis=0)
     kinds = layers + STEPS
     mods = mods[:kinds].reshape(kinds * 3, columns).astype(BF)
-    packed = jnp.concatenate([in_proj_s, in_proj_t, out_proj, mods], axis=0).T
+    packed = jnp.concatenate([projections, mods.T], axis=1)
     gathered = lax.all_gather(packed, TP, axis=0, tiled=False)
 
-    block = lax.axis_index(SAMPLE) * rows // columns
-    places = [block, sample * rows // rows % (columns // rows)]
-    for offset in (0, 8, 16):
-        places += [(block + offset) // 3, (block + offset) % 3]
     gap = -hidden % 128
     both_wide = 2 * hidden + gap
     parts, part_bias = here(
@@ -476,109 +581,107 @@
             jax.ShapeDtypeStruct((cells * STEPS, both_wide), BF),
             jax.ShapeDtypeStruct((8, hidden), BF),
         ),
-        (jnp.stack(places).astype(jnp.int32), gathered, s_w1, s_w2.T),
+        (places, gathered, s_w1, s_w2.T),
         scalars=1,
+        far_out=(0,),
+        scratch=(pltpu.VMEM((cells * STEPS, both_wide), BF), pltpu.SemaphoreType.DMA((1,))),
     )
     piece = cells * STEPS // samples
     chunk = cells // samples
     t_w1 = jnp.swapaxes(t_w1, 1, 2)
-    parts, gathered, t_w1, t_w2 = lax.optimization_barrier((parts, gathered, t_w1, t_w2))
-    received = lax.all_to_all(parts.reshape(samples, piece, both_wide), SAMPLE, 0, 0)
-
-    mods = gathered[:, :, 3 * cells :].astype(F32).reshape(8, columns, kinds, 3)
-    mod_teacher = mods[:, :, :layers].transpose(2, 0, 3, 1).reshape(layers, 1, 3 * width)
-    packed = gathered.reshape(width, -1)
-    proj_s, proj_t, proj_out = (packed[:, at * cells : (at + 1) * cells] for at in range(3))
-    shifts = [mod_teacher[l, :, :width] for l in range(layers)]
-    scales = [mod_teacher[l, :, width : 2 * width] for l in range(layers)]
-    gates = [mod_teacher[l, :, 2 * width :] for l in range(layers)]
-    first_own = here(
-        first_product_kernel,
-        "first_product",
-        array((cells + 8, hidden), F32),
-        (proj_t, scales[0], shifts[0], t_w1),
-        far=1,
-        scratch=(pltpu.VMEM((1, hidden, width), BF), pltpu.SemaphoreType.DMA((1,))),
-        limit=44,
-    )
-    latent_in = noisy_latents[0]
-    h0 = dot_back(latent_in, proj_s).astype(BF)
-    _, inverse_s = normalize(h0.astype(F32))
-    received, first_own, inverse_s = lax.optimization_barrier((received, first_own, inverse_s))
-
+    parts, t_w1, t_w2, d_w2 = lax.optimization_barrier((parts, t_w1, t_w2, d_w2))
     w2_sib = sibling(t_w2)
     w1_sib = sibling(t_w1)
-
-    at_row = jnp.arange(samples * 8)
-    step_at = jnp.repeat(student_step - 1, 8)
-    pick = (
-        ((at_row % 8 * STEPS + step_at)[:, None] == jnp.arange(piece)[None])
-        & (at_row % 8 < chunk)[:, None]
-    ).astype(BF)
-    pick_bias = ((step_at[:, None] == jnp.arange(8)[None]) & (at_row % 8 == chunk)[:, None]).astype(BF)
+    d_w2_sib = sibling(d_w2)
+    received = lax.all_to_all(parts.reshape(samples, piece, both_wide), SAMPLE, 0, 0)
+
     chosen = here(
         select_kernel,
         "select",
-        jax.ShapeDtypeStruct((samples * 8, both_wide), BF),
-        (received, pick, pick_bias, part_bias),
+        array((samples * 8, both_wide), BF),
+        (student_step, received, part_bias),
+        scalars=1,
+        far_out=(0,),
+        scratch=(pltpu.VMEM((samples * 8, both_wide), BF), pltpu.SemaphoreType.DMA((1,))),
     )
     mine = lax.all_to_all(chosen.reshape(samples, 8, both_wide), SAMPLE, 0, 0)
     mine = mine.reshape(samples * 8, both_wide)
-    my_step = lax.dynamic_index_in_dim(student_step, sample, keepdims=False)
-
-    spare = -columns % 128
-    head_block, _ = lax.optimization_barrier((jnp.pad(d_w1, ((0, 0), (0, spare))), mine))
-    head_own = lax.all_gather(head_block, SAMPLE, axis=0, tiled=True)
-
-    sigma_s = my_step.astype(F32) * 0.25
-    sigma_t = lax.dynamic_index_in_dim(sig_all_t, sample, keepdims=False)
-    velocity = here(
+
+    latent_in = noisy_latents[0].T
+    noise = teacher_noise[0].T
+    packed = gathered.reshape(width, -1)
+    half_out = array((half, cells), F32)
+    velocity, other = here(
         student_kernel,
         "student",
-        jax.ShapeDtypeStruct((seq, cells), F32),
-        (latent_in, inverse_s, mine),
-    )
-    mine_first = lax.dynamic_slice_in_dim(velocity, at_core * half, half, 0)
-    other = lax.dynamic_slice_in_dim(velocity, (1 - at_core) * half, half, 0)
-    velocity = mine_first + sibling(other)
+        (half_out, half_out),
+        (where, latent_in, packed, mine),
+        scalars=1,
+        scratch=(pltpu.VMEM((seq, cells), F32),),
+    )
+    velocity = velocity + sibling(other)
     velocity = velocity + lax.ppermute(velocity, "y", [(0, 1), (1, 0), (2, 3), (3, 2)])
     velocity = velocity + lax.ppermute(velocity, "y", [(0, 2), (2, 0), (1, 3), (3, 1)])
 
-    def my_half(values):
-        return lax.dynamic_slice_in_dim(values, at_core * half, half, 0)
-
-    velocity = velocity + dot(my_half(h0), proj_out)
-    latents = (my_half(latent_in).astype(F32) - sigma_s * velocity).astype(BF)
-    noised = (
-        (1.0 - sigma_t) * latents.astype(F32) + sigma_t * my_half(teacher_noise[0]).astype(F32)
-    ).astype(BF)
-
-    def both(values):
+    head_block, _ = lax.optimization_barrier((head_block, other))
+    head_own = lax.all_gather(head_block, SAMPLE, axis=0, tiled=True)
+
+    def both(values, axis):
         other = sibling(values)
         first = jnp.where(at_core == 0, values, other)
         second = jnp.where(at_core == 0, other, values)
-        return jnp.concatenate([first, second], axis=0)
-
-    latents = both(latents)
-
+        return jnp.concatenate([first, second], axis=axis)
+
+    gathered, _ = lax.optimization_barrier((gathered, other))
+    first_own, vectors = here(
+        first_product_kernel,
+        "first_product",
+        (array((cells + 8, hidden), F32), array((8, width), F32)),
+        (gathered, t_w1),
+        far=1,
+        scratch=(
+            pltpu.VMEM((1, hidden, width), BF),
+            pltpu.VMEM((width, cells + 8), BF),
+            pltpu.SemaphoreType.DMA((1,)),
+        ),
+        limit=44,
+    )
     first_sib = sibling(first_own)
+    velocity, w1_sib, w2_sib, d_w2_sib = lax.optimization_barrier((velocity, w1_sib, w2_sib, d_w2_sib))
 
     token_rows = pltpu.VMEM((half, width), BF)
     inner = pltpu.VMEM((2, half, hidden), BF)
+    matrix = pltpu.VMEM((2, hidden, width), BF)
     rows_out = array((4, quarter, width), BF)
     mine_out = array((quarter, width), BF)
+    tokens_out = array((half, width), BF)
     inner_out = array((2, half, hidden), BF)
-    y_0, slope_0, g_0, back_0 = here(
+    cells_out = array((half, cells), BF)
+    y_0, slope_0, latents, noised, g_0, back_0 = here(
         first_forward_kernel,
         "first_forward",
-        (array((half, width), BF), inner_out, array((half, width), BF), array((half, 2 * cells), F32)),
-        (noised, proj_t, first_own, first_sib, t_w2, w2_sib),
+        (tokens_out, inner_out, cells_out, cells_out, tokens_out, array((half, 2 * cells), F32)),
+        (
+            where,
+            student_step,
+            teacher_step,
+            velocity,
+            latent_in,
+            noise,
+            packed,
+            first_own,
+            first_sib,
+            t_w2,
+            w2_sib,
+        ),
+        scalars=3,
         far=2,
         far_out=(0, 1),
         scratch=(
-            pltpu.VMEM((2, hidden, width), BF),
+            matrix,
             token_rows,
             inner,
+            pltpu.VMEM((2, seq, cells), F32),
             pltpu.SemaphoreType.DMA((4,)),
         ),
         limit=44,
@@ -588,69 +691,64 @@
         return swap_y(partial.reshape(4, quarter, width))
 
     last = (t_w1, w1_sib, t_w2, w2_sib)
-    matrix = pltpu.VMEM((2, hidden, width), BF)
     g_1_mine, g_1 = here(
         first_middle_kernel,
         "first_middle",
         (mine_out, rows_out),
-        (at_y.reshape(1), sums(y_0), g_0, gates[0]),
+        (where, sums(y_0), g_0, vectors),
         scalars=1,
     )
     g_1 = swap_y(g_1).reshape(half, width)
     y_1, slope_1 = here(
         forward_kernel,
         "forward",
-        (array((half, width), BF), inner_out),
-        (g_1, scales[1], shifts[1]) + last,
+        (tokens_out, inner_out),
+        (g_1, vectors) + last,
         far=4,
         far_out=(0, 1),
         scratch=(matrix, matrix, token_rows, inner, pltpu.SemaphoreType.DMA((6,))),
         limit=44,
     )
     g_2_mine, g_2 = here(
-        last_middle_kernel,
-        "last_middle",
-        (mine_out, rows_out),
-        (sums(y_1), g_1_mine, gates[1]),
-    )
-    head_own, d_w2_late, _ = lax.optimization_barrier((head_own, d_w2, g_2_mine))
+        last_middle_kernel, "last_middle", (mine_out, rows_out), (sums(y_1), g_1_mine, vectors)
+    )
+    head_own, _ = lax.optimization_barrier((head_own, g_2_mine))
     head_sib = sibling(head_own)
-    d_w2_sib = sibling(d_w2_late)
     g_2 = swap_y(g_2).reshape(half, width)
 
-    outs = jnp.pad(jnp.stack([d_w2, d_w2_sib]), ((0, 0), (0, 0), (0, spare)))
-    use = [outs * (layer_pick[0] == layer).astype(F32)[None, :, None] for layer in range(layers)]
-
-    def head(name, g, use):
+    def head(name, layer, g):
         return here(
-            head_kernel,
+            functools.partial(head_kernel, layer),
             name,
-            (array((half, width), BF), array((half, 128), F32)),
-            (g, use, head_own, head_sib),
+            (tokens_out, array((half, 128), F32)),
+            (picks, g, d_w2, d_w2_sib, head_own, head_sib),
+            scalars=1,
             far=2,
             far_out=(0,),
             scratch=(
                 pltpu.VMEM((2,) + head_own.shape, BF),
                 token_rows,
+                pltpu.VMEM((2, 8, head_own.shape[1]), F32),
                 pltpu.SemaphoreType.DMA((3,)),
             ),
         )
 
-    head_back_2, scores_2 = head("head_last", g_2, use[1])
+    head_back_2, scores_2 = head("head_last", 1, g_2)
 
     dg_2, dy_1 = here(
         last_back_kernel,
         "last_back",
         (array((quarter, width), F32), rows_out),
-        (sums(head_back_2), g_2_mine, gates[1]),
-    )
-    g_1, _ = lax.optimization_barrier((g_1, dg_2))
-    head_back_1, scores_1 = head("head_first", g_1, use[0])
+        (sums(head_back_2), g_2_mine, vectors),
+    )
+    g_1, latents, _ = lax.optimization_barrier((g_1, latents, dg_2))
+    latents = both(latents, 0)
+    head_back_1, scores_1 = head("head_first", 0, g_1)
     du_1 = here(
         backward_kernel,
         "backward",
-        array((half, width), BF),
-        (swap_y(dy_1).reshape(half, width), scales[1], slope_1, head_back_1) + last,
+        tokens_out,
+        (swap_y(dy_1).reshape(half, width), vectors, slope_1, head_back_1) + last,
         far=6,
         far_out=(0,),
         scratch=(matrix, matrix, inner, token_rows, token_rows, pltpu.SemaphoreType.DMA((7,))),
@@ -660,19 +758,20 @@
         first_back_kernel,
         "first_back",
         (array((quarter, cells), F32), rows_out),
-        (sums(du_1), g_1_mine, dg_2, gates[0], proj_t),
+        (sums(du_1), g_1_mine, dg_2, vectors, packed),
     )
     final = here(
         first_backward_kernel,
         "first_backward",
-        array((half, 2 * cells), F32),
+        array((cells + 8, half), F32),
         (
-            at_y.reshape(1),
-            (1.0 - sigma_t).reshape(1),
+            where,
+            teacher_step,
             swap_y(dy_0).reshape(half, width),
             noised,
             back_0,
-            scores_1 + scores_2,
+            scores_1,
+            scores_2,
             direct,
             first_own,
             first_sib,
@@ -682,13 +781,13 @@
         ),
         scalars=2,
         far=3,
-        scratch=(matrix, inner, pltpu.SemaphoreType.DMA((3,))),
+        scratch=(matrix, inner, pltpu.VMEM((half, 2 * cells), F32), pltpu.SemaphoreType.DMA((3,))),
         limit=44,
     )
     final = final + lax.ppermute(final, "y", [(0, 1), (1, 0), (2, 3), (3, 2)])
     final = final + lax.ppermute(final, "y", [(0, 2), (2, 0), (1, 3), (3, 1)])
-    final = both(final)
-    return (latents[None], final[:, cells : cells + heads].T[None], final[:, :cells][None])
+    final = both(final, 1)
+    return (latents[None], final[cells : cells + heads][None], final[:cells].T[None])
 
 
 def solution(mesh):

time: 281 us -> 285 us (1.014)
  blocking collectives: 51.6 us -> 151 us
  waiting for transfers between devices: 75.3 us -> 10.2 us
  starting transfers between devices: 60 us -> 28.3 us
  Pallas kernels: 61.4 us -> 65.5 us
    all_to_all x0 -> x3, blocking collectives: none -> 54.8 us  [the longest x1 23.4 us: body(): lax.all_to_all(parts.reshape(samples, piece, both_wide), SAMPLE, 0, 0)]
    all_to_all x3 -> x7, blocking collectives: 35.1 us -> 79.9 us  [swap_y(): return lax.all_to_all(values, 'y', 0, 0)]
    all_to_all x5 -> x1, waiting for transfers between devices: 37.6 us -> 1.91 us  [swap_y(): return lax.all_to_all(values, 'y', 0, 0)]
    all_to_all x3 -> x0, waiting for transfers between devices: 31.5 us -> none  [the longest x1 13.8 us: body(): lax.all_to_all(parts.reshape(samples, piece, both_wide), SAMPLE, 0, 0)]
    all_to_all x3 -> x0, starting transfers between devices: 16.6 us -> none  [the longest x1 8.56 us: body(): mods = jnp.sum(lax.all_to_all(mod_part, SAMPLE, 0, 0).astype(F32), axis=0)]
    all_to_all x5 -> x1, starting transfers between devices: 18.2 us -> 3.48 us  [swap_y(): return lax.all_to_all(values, 'y', 0, 0)]
    pallas_call x15, Pallas kernels: 61.4 us -> 65.5 us  [here(): pl.pallas_call(kernel, name=name, out_shape=shapes if many else shapes[0]...]
    unnamed x48 -> x55, local copies, waits for them, and re-layouts: 7.5 us -> 9.93 us
  transfers between devices with their start and end apart: 21 -> 14, of which waited for: 13 -> 6; matrix products, arithmetic and copies ran while one was open for 3% -> 0% of each run, Pallas kernels for 11% -> 12%
where the time goes in v2:
time: 285 us; the launch traced here: 284 us
  blocking collectives  151 us (53%)
  Pallas kernels  65.5 us (23%)
  starting transfers between devices  28.3 us (10%)
  between operations  14.6 us (5%)
  local copies, waits for them, and re-layouts  11.8 us (4%)
  waiting for transfers between devices  10.2 us (4%)
    all_to_all x7, blocking collectives, swap_y(): return lax.all_to_all(values, 'y', 0, 0)  79.9 us
    pallas_call x15, Pallas kernels, here(): pl.pallas_call(kernel, name=name, out_shape=shapes if many else shapes[0]...  65.5 us
    all_to_all x1, blocking collectives, body(): lax.all_to_all(parts.reshape(samples, piece, both_wide), SAMPLE, 0, 0)  23.4 us
    ppermute x8, starting transfers between devices, sibling(): return lax.ppermute(values, 'core', [(0, 1), (1, 0)])  19.2 us
    all_gather x1, blocking collectives, body(): gathered = lax.all_gather(packed, TP, axis=0, tiled=False)  16.5 us
    all_to_all x1, blocking collectives, body(): mods = jnp.sum(lax.all_to_all(mod_part, SAMPLE, 0, 0).astype(F32), axis=0)  15.9 us
    all_to_all x1, blocking collectives, body(): mine = lax.all_to_all(chosen.reshape(samples, 8, both_wide), SAMPLE, 0, 0)  15.5 us
    unnamed x55, local copies, waits for them, and re-layouts  9.93 us
  transfers between devices with their start and end apart: 14, of which 6 were waited for; matrix products, arithmetic and copies ran while one was open for 0% of the time, Pallas kernels for 12%

profile of v2, /device:TPU:1, one launch (start us, length us, event | category | flops | bytes accessed | tf_op | source)
XLA Modules:
  0.0 284.1 jit_solution(17948623025089421020)
XLA Ops:
  7.4 0.7 convert_element_type.31
  8.1 0.1 divide_multiply_fusion
  8.2 0.2 fusion.2.cond_t_ref
  8.4 1.6 pad.9
  10.1 1.1 copy-done
  11.1 1.0 copy-done.4
  12.1 0.8 copy-done.14
  12.9 0.8 copy-done.15
  13.7 0.8 copy-done.16
  14.5 0.7 modulation.1
  15.3 15.9 %all_to_all.55 = bf16[16,8,912]{2,1,0:T(8,128)(2,1)S(1)} all-to-all(bf16[16,8,912]{2,1,0:T(8,128)(2,1)S(1)} %bitcast.52), channel_id=1, replica_groups=mesh['fsdp'=8,'y'=4,'core'=2,'grp'=2] {'fsdp','grp'}, dimensions={0} | all-to-all | bytes 466944 | tf_op jit(solution)/shard_map/all_to_all | solution.py:569
  31.3 0.1 convert_element_type.33
  31.4 0.1 copy.20
  31.7 16.5 %all-gather.packed_ref = bf16[2432,210]{1,0:T(8,128)(2,1)S(1)} all-gather(bf16[304,210]{1,0:T(8,128)(2,1)S(1)} %pad_maximum_fusion), channel_id=2, replica_groups=mesh['fsdp'=8,'y'=4,'core'=2,'grp'=2] {'y','core'}, dimensions={0}, use_global_device_ids=true | all-gather | bytes 1149120 | tf_op jit(solution)/shard_map/all_gather | solution.py:573
  48.2 3.1 %product.1 = (bf16[256,2496]{1,0:T(8,128)(2,1)}, bf16[8,1216]{1,0:T(8,128)(2,1)S(1)}) custom-call(s32[8]{0:T(128)S(1)} %stack.51.at_ref, bf16[8,304,210]{2,1,0:T(8,128)(2,1)S(1)} %bitcast.43, bf16[152,1216]{1,0:T(8,128)(2,1)S(1)} %copy-done.2, bf16[152,1216]{1,0:T(8,128)(2,1)S(1)} %bitcast.51), custom_call_target="tpu_custom_call" | custom-call | tf_op jit(solution)/shard_map/product/pallas_call | solution.py:489
  51.3 0.2 collective-permute-start.3
  51.5 0.4 collective-permute-start.4
  51.9 23.4 %all_to_all.56.parts_ref = bf16[16,16,2496]{2,1,0:T(8,128)(2,1)S(1)} all-to-all(bf16[16,16,2496]{2,1,0:T(8,128)(2,1)} %bitcast.64), channel_id=1, replica_groups=mesh['fsdp'=8,'y'=4,'core'=2,'grp'=2] {'fsdp','grp'}, dimensions={0} | all-to-all | bytes 2555904 | tf_op jit(solution)/shard_map/all_to_all | solution.py:596
  75.3 1.9 select.5
  77.2 15.5 %all_to_all.57 = bf16[16,8,2496]{2,1,0:T(8,128)(2,1)S(1)} all-to-all(bf16[16,8,2496]{2,1,0:T(8,128)(2,1)} %bitcast.62), channel_id=1, replica_groups=mesh['fsdp'=8,'y'=4,'core'=2,'grp'=2] {'fsdp','grp'}, dimensions={0} | all-to-all | bytes 1277952 | tf_op jit(solution)/shard_map/all_to_all | solution.py:607
  92.7 2.7 student.1
  95.4 5.8 %first_product.1 = (f32[72,1216]{1,0:T(8,128)S(1)}, f32[8,2432]{1,0:T(8,128)S(1)}) custom-call(bf16[8,304,210]{2,1,0:T(8,128)(2,1)S(1)} %bitcast.44, bf16[2,1216,2432]{2,1,0:T(8,128)(2,1)} %bitcast.59), custom_call_target="tpu_custom_call" | custom-call | tf_op jit(solution)/shard_map/first_product/pallas_call | solution.py:489
  101.3 2.1 collective-permute-start.6
  103.4 1.3 collective-permute-done
  104.7 1.1 collective-permute-start.1
  105.8 2.5 collective-permute-done.1
  108.3 2.2 collective-permute-start.2
  110.6 1.1 collective-permute-start.5
  111.6 1.8 collective-permute-done.2
  113.5 8.0 %first_forward.1 = (bf16[128,2432]{1,0:T(8,128)(2,1)}, bf16[2,128,1216]{2,1,0:T(8,128)(2,1)}, bf16[128,64]{1,0:T(8,128)(2,1)S(1)}, bf16[128,64]{1,0:T(8,128)(2,1...) custom-call(s32[3]{0:T(128)S(1)} %pad_add_fusion.where_ref, s32[16]{0:T(128)S(1)} %copy-done.23, ...), custom_call_target="tpu_custom_call" | custom-call | tf_op jit(solution)/shard_map/first_forward/pallas_call | solution.py:489
  121.5 11.9 %all_to_all.58.parts_ref = bf16[4,32,2432]{2,1,0:T(8,128)(2,1)S(1)} all-to-all(bf16[4,32,2432]{2,1,0:T(8,128)(2,1)} %bitcast.65), channel_id=1, replica_groups=mesh['fsdp'=8,'y'=4,'core'=2,'grp'=2] {'y'}, dimensions={0} | all-to-all | bytes 1245184 | tf_op jit(solution)/shard_map/all_to_all | solution.py:75
  133.4 0.7 first_middle.1
  134.1 10.3 %all_to_all.59 = bf16[4,32,2432]{2,1,0:T(8,128)(2,1)S(1)} all-to-all(bf16[4,32,2432]{2,1,0:T(8,128)(2,1)S(1)} %get-tuple-element.71), channel_id=1, replica_groups=mesh['fsdp'=8,'y'=4,'core'=2,'grp'=2] {'y'}, dimensions={0} | all-to-all | bytes 1245184 | tf_op jit(solution)/shard_map/all_to_all | solution.py:75
  144.4 10.7 %forward.1 = (bf16[128,2432]{1,0:T(8,128)(2,1)}, bf16[2,128,1216]{2,1,0:T(8,128)(2,1)}) custom-call(bf16[128,2432]{1,0:T(8,128)(2,1)S(1)} %bitcast.45, f32[8,2432]{1,0:T(8,128)S(1)} %get-tuple-element.70.vector_ref, bf16[2,1216,2432]{2,1,0:T(8,128)(2,1)} %bitcast.60, bf16[2,1216,2432]{2,1,0:T(8,128)(2,1)} %collective-permute-done.3.up_sib, ...), custom_call_target="tpu_custom_call" | custom-call | tf_op jit(solution)/shard_map/forward/pallas_call | solution.py:489
  155.1 11.3 %all_to_all.60.parts_ref = bf16[4,32,2432]{2,1,0:T(8,128)(2,1)S(1)} all-to-all(bf16[4,32,2432]{2,1,0:T(8,128)(2,1)} %bitcast.67), channel_id=1, replica_groups=mesh['fsdp'=8,'y'=4,'core'=2,'grp'=2] {'y'}, dimensions={0} | all-to-all | bytes 1245184 | tf_op jit(solution)/shard_map/all_to_all | solution.py:75
  166.4 0.1 last_middle.1
  166.6 0.7 copy-done.7
  167.2 4.5 %collective-permute-start.7 = (bf16[2432,384]{1,0:T(8,128)(2,1)}, bf16[2432,384]{1,0:T(8,128)(2,1)S(1)}, u32[]{:S(2)}, u32[]{:S(2)}) collective-permute-start(bf16[2432,384]{1,0:T(8,128)(2,1)} %all-gather.3.cloned.1.call-done.own), channel_id=1, source_target_pairs={{0,2},{2,0},{1,3},{3,1},{4,6},{6,4},{5,7},{7,5},{8,10},{10,8},{9,1... | collective-permute-start | bytes 5603336 | tf_op jit(solution)/shard_map/ppermute | solution.py:71
  171.8 13.1 %all_to_all.61 = bf16[4,32,2432]{2,1,0:T(8,128)(2,1)S(1)} all-to-all(bf16[4,32,2432]{2,1,0:T(8,128)(2,1)S(1)} %get-tuple-element.77), channel_id=1, replica_groups=mesh['fsdp'=8,'y'=4,'core'=2,'grp'=2] {'y'}, dimensions={0} | all-to-all | bytes 1245184 | tf_op jit(solution)/shard_map/all_to_all | solution.py:75
  184.8 1.2 copy-done.26
  186.1 5.4 %head_last.1 = (bf16[128,2432]{1,0:T(8,128)(2,1)}, f32[128,128]{1,0:T(8,128)S(1)}) custom-call(s32[2]{0:T(128)S(1)} %bitcast.56, bf16[128,2432]{1,0:T(8,128)(2,1)S(1)} %bitcast.50, f32[2,304]{1,0:T(2,128)S(1)} %copy-done.22, f32[2,304]{1,0:T(2,128)S(1)} %collective-permute-done.5.out_sib, bf16[2432,384]{1,0:T(8,128)(2,1)} %all-gather.3.cloned.1.call-done.own, ...), custom_call_target="tpu_custom_call" | custom-call | tf_op jit(solution)/shard_map/head_last/pallas_call | solution.py:489
  191.5 0.6 copy-done.10
  192.1 12.6 %all_to_all.62.parts_ref = bf16[4,32,2432]{2,1,0:T(8,128)(2,1)S(1)} all-to-all(bf16[4,32,2432]{2,1,0:T(8,128)(2,1)} %bitcast.66), channel_id=1, replica_groups=mesh['fsdp'=8,'y'=4,'core'=2,'grp'=2] {'y'}, dimensions={0} | all-to-all | bytes 1245184 | tf_op jit(solution)/shard_map/all_to_all | solution.py:75
  204.7 0.4 last_back.1
  205.1 0.8 copy-done.1
  206.0 0.7 copy-done.5
  206.7 3.5 %all-to-all-start.8 = ((bf16[4,32,2432]{2,1,0:T(8,128)(2,1)}), bf16[4,32,2432]{2,1,0:T(8,128)(2,1)S(1)}, u32[]{:S(2)}, u32[]{:S(2)}) async-start(bf16[4,32,2432]{2,1,0:T(8,128)(2,1)} %copy-done.1), calls=%async_computation.8 | async-start | bytes 1245184 | tf_op jit(solution)/shard_map/all_to_all | solution.py:75
  210.2 5.4 %head_first.1 = (bf16[128,2432]{1,0:T(8,128)(2,1)}, f32[128,128]{1,0:T(8,128)S(1)}) custom-call(s32[2]{0:T(128)S(1)} %bitcast.57, bf16[128,2432]{1,0:T(8,128)(2,1)S(1)} %bitcast.46, f32[2,304]{1,0:T(2,128)S(1)} %copy-done.22, f32[2,304]{1,0:T(2,128)S(1)} %collective-permute-done.5.out_sib, bf16[2432,384]{1,0:T(8,128)(2,1)} %all-gather.3.cloned.1.call-done.own, ...), custom_call_target="tpu_custom_call" | custom-call | tf_op jit(solution)/shard_map/head_first/pallas_call | solution.py:489
  215.6 0.6 copy-done.12
  216.2 1.9 all-to-all-done.8
  218.1 10.9 %backward.1 = bf16[128,2432]{1,0:T(8,128)(2,1)} custom-call(bf16[128,2432]{1,0:T(8,128)(2,1)S(1)} %bitcast.48, f32[8,2432]{1,0:T(8,128)S(1)} %get-tuple-element.70.vector_ref, bf16[2,128,1216]{2,1,0:T(8,128)(2,1)} %get-tuple-element.87.slope, bf16[128,2432]{1,0:T(8,128)(2,1)} %get-tuple-element.89.head, bf16[2,1216,2432]{2,1,0:T(8,128)(2,1)} %bitcast.61, ...), custom_call_target="tpu_custom_call" | custom-call | tf_op jit(solution)/shard_map/backward/pallas_call | solution.py:489
  229.0 10.9 %all_to_all.63.parts_ref = bf16[4,32,2432]{2,1,0:T(8,128)(2,1)S(1)} all-to-all(bf16[4,32,2432]{2,1,0:T(8,128)(2,1)} %bitcast.63), channel_id=1, replica_groups=mesh['fsdp'=8,'y'=4,'core'=2,'grp'=2] {'y'}, dimensions={0} | all-to-all | bytes 1245184 | tf_op jit(solution)/shard_map/all_to_all | solution.py:75
  240.0 0.6 first_back.1
  240.6 9.9 %all_to_all.64 = bf16[4,32,2432]{2,1,0:T(8,128)(2,1)S(1)} all-to-all(bf16[4,32,2432]{2,1,0:T(8,128)(2,1)S(1)} %get-tuple-element.90), channel_id=1, replica_groups=mesh['fsdp'=8,'y'=4,'core'=2,'grp'=2] {'y'}, dimensions={0} | all-to-all | bytes 1245184 | tf_op jit(solution)/shard_map/all_to_all | solution.py:75
  250.5 9.0 %first_backward.1 = f32[72,128]{1,0:T(8,128)S(1)} custom-call(s32[3]{0:T(128)S(1)} %pad_add_fusion.where_ref, s32[16]{0:T(128)S(1)} %copy-done.24, bf16[128,2432]{1,0:T(8,128)(2,1)S(1)} %bitcast.49, bf16[128,64]{1,0:T(8,128)(2,1)S(1)} %copy-done.19, f32[128,128]{1,0:T(8,128)S(1)} %get-tuple-element.92.back_ref, f32[128,128]{1,0:T(8,128)S(1)} %copy-done.13, ...), custom_call_target="tpu_custom_call" | custom-call | tf_op jit(solution)/shard_map/first_backward/pallas_call | solution.py:489
  259.5 0.4 collective-permute-start.9
  259.8 6.1 %collective-permute-start.8 = (bf16[128,64]{1,0:T(8,128)(2,1)S(1)}, bf16[128,64]{1,0:T(8,128)(2,1)S(1)}, u32[]{:S(2)}, u32[]{:S(2)}) collective-permute-start(bf16[128,64]{1,0:T(8,128)(2,1)S(1)} %copy-done.21), channel_id=1, source_target_pairs={{0,2},{2,0},{1,3},{3,1},{4,6},{6,4},{5,7},{7,5},{8,10},{10,8},{9,1... | collective-permute-start | bytes 49160 | tf_op jit(solution)/shard_map/ppermute | solution.py:71
  266.0 1.9 collective-permute-start.10
  267.9 2.5 collective-permute-done.10
  270.4 4.8 %collective-permute-start.11 = (f32[72,128]{1,0:T(8,128)S(1)}, f32[72,128]{1,0:T(8,128)S(1)}, u32[]{:S(2)}, u32[]{:S(2)}) collective-permute-start(f32[72,128]{1,0:T(8,128)S(1)} %add.99), channel_id=1, source_target_pairs={{0,2},{2,0},{1,3},{3,1},{4,6},{6,4},{5,7},{7,5},{8,10},{10,8},{9,1... | collective-permute-start | bytes 110600 | tf_op jit(solution)/shard_map/ppermute | solution.py:71
  275.2 0.7 copy.21
  275.9 0.1 collective-permute-done.11
  276.0 0.6 maximum_bitcast_fusion.1
  276.6 0.6 fusion
  (70 shorter events, 0.7 us)
Async XLA Ops:
  7.2 160.1 %all-gather.3.cloned.1.call-start = ((), (), s32[]{:S(2)}) async-start(), calls=%async_computation.11 | async-start | bytes 1984512 | tf_op jit(solution)/shard_map/all_gather | solution.py:627
  10.1 1.1 copy-start
  11.1 1.0 copy-start.4
  12.1 0.8 copy-start.14
  12.9 0.8 copy-start.15
  13.7 0.8 copy-start.16
  14.5 33.7 %copy-start.2 = (bf16[152,1216]{1,0:T(8,128)(2,1)S(1)}, bf16[152,1216]{1,0:T(8,128)(2,1)}, u32[]{:S(2)}) copy-start(bf16[152,1216]{1,0:T(8,128)(2,1)} %w1_ref.1) | copy-start | bytes 1108996
  14.5 33.7 %copy-start.3 = (bf16[1216,152]{0,1:T(8,128)(2,1)S(1)}, bf16[1216,152]{0,1:T(8,128)(2,1)}, u32[]{:S(2)}) copy-start(bf16[1216,152]{0,1:T(8,128)(2,1)} %param.26) | copy-start | bytes 1108996
  48.2 27.1 %copy-start.23 = (s32[16]{0:T(128)S(1)}, s32[16]{0:T(128)}, u32[]{:S(2)}) copy-start(s32[16]{0:T(128)} %student_ref.1) | copy-start | bytes 196
  51.3 62.1 %collective-permute-start.3 = (bf16[2,1216,2432]{2,1,0:T(8,128)(2,1)}, bf16[2,1216,2432]{2,1,0:T(8,128)(2,1)}, u32[]{:S(2)}, u32[]{:S(2)}) collective-permute-start(bf16[2,1216,2432]{2,1,0:T(8,128)(2,1)} %bitcast.58), channel_id=1, source_target_pairs={{0,2},{2,0},{1,3},{3,1},{4,6},{6,4},{5,7},{7,5},{8,10},{10,8},{9,1... | collective-permute-start | bytes 35487752 | tf_op jit(solution)/shard_map/ppermute | solution.py:71
  51.5 61.9 %collective-permute-start.4 = (bf16[2,1216,2432]{2,1,0:T(8,128)(2,1)}, bf16[2,1216,2432]{2,1,0:T(8,128)(2,1)}, u32[]{:S(2)}, u32[]{:S(2)}) collective-permute-start(bf16[2,1216,2432]{2,1,0:T(8,128)(2,1)} %own.1), channel_id=1, source_target_pairs={{0,2},{2,0},{1,3},{3,1},{4,6},{6,4},{5,7},{7,5},{8,10},{10,8},{9,1... | collective-permute-start | bytes 35487752 | tf_op jit(solution)/shard_map/ppermute | solution.py:71
  75.3 17.4 %copy-start.9 = (bf16[1,256,64]{1,2,0:T(8,128)(2,1)S(1)}, bf16[1,256,64]{1,2,0:T(8,128)(2,1)}, u32[]{:S(2)}) copy-start(bf16[1,256,64]{1,2,0:T(8,128)(2,1)} %param.16) | copy-start | bytes 98308
  95.4 15.2 %copy-start.22 = (f32[2,304]{1,0:T(2,128)S(1)}, f32[2,304]{1,0:T(2,128)}, u32[]{:S(2)}) copy-start(f32[2,304]{1,0:T(2,128)} %out_own.1) | copy-start | bytes 7300
  95.4 18.1 %copy-start.17 = (bf16[1,256,64]{1,2,0:T(8,128)(2,1)S(1)}, bf16[1,256,64]{1,2,0:T(8,128)(2,1)}, u32[]{:S(2)}) copy-start(bf16[1,256,64]{1,2,0:T(8,128)(2,1)} %param.19) | copy-start | bytes 98308
  95.4 18.1 %copy-start.24 = (s32[16]{0:T(128)S(1)}, s32[16]{0:T(128)}, u32[]{:S(2)}) copy-start(s32[16]{0:T(128)} %teacher_ref.3) | copy-start | bytes 196
  101.3 12.2 %collective-permute-start.6 = (f32[72,1216]{1,0:T(8,128)S(1)}, f32[72,1216]{1,0:T(8,128)S(1)}, u32[]{:S(2)}, u32[]{:S(2)}) collective-permute-start(f32[72,1216]{1,0:T(8,128)S(1)} %get-tuple-element.66.mat_own), channel_id=1, source_target_pairs={{0,2},{2,0},{1,3},{3,1},{4,6},{6,4},{5,7},{7,5},{8,10},{10,8},{9,1... | collective-permute-start | bytes 1050632 | tf_op jit(solution)/shard_map/ppermute | solution.py:71
  103.3 1.4 collective-permute-start
  104.7 3.6 %collective-permute-start.1 = (f32[128,64]{1,0:T(8,128)S(1)}, f32[128,64]{1,0:T(8,128)S(1)}, u32[]{:S(2)}, u32[]{:S(2)}) collective-permute-start(f32[128,64]{1,0:T(8,128)S(1)} %add.95), channel_id=1, source_target_pairs={{0,4},{4,0},{8,12},{12,8},{1,5},{5,1},{9,13},{13,9},{2,6},{6,2},{1... | collective-permute-start | bytes 98312 | tf_op jit(solution)/shard_map/ppermute | solution.py:623
  108.3 5.1 %collective-permute-start.2 = (f32[128,64]{1,0:T(8,128)S(1)}, f32[128,64]{1,0:T(8,128)S(1)}, u32[]{:S(2)}, u32[]{:S(2)}) collective-permute-start(f32[128,64]{1,0:T(8,128)S(1)} %add.96), channel_id=1, source_target_pairs={{0,8},{8,0},{4,12},{12,4},{1,9},{9,1},{5,13},{13,5},{2,10},{10,2},... | collective-permute-start | bytes 98312 | tf_op jit(solution)/shard_map/ppermute | solution.py:624
  110.6 2.9 %collective-permute-start.5 = (f32[2,304]{1,0:T(2,128)S(1)}, f32[2,304]{1,0:T(2,128)S(1)}, u32[]{:S(2)}, u32[]{:S(2)}) collective-permute-start(f32[2,304]{1,0:T(2,128)S(1)} %copy-done.22), channel_id=1, source_target_pairs={{0,2},{2,0},{1,3},{3,1},{4,6},{6,4},{5,7},{7,5},{8,10},{10,8},{9,1... | collective-permute-start | bytes 7304 | tf_op jit(solution)/shard_map/ppermute | solution.py:71
  121.5 22.9 %copy-start.18 = (bf16[128,64]{1,0:T(8,128)(2,1)}, bf16[128,64]{1,0:T(8,128)(2,1)S(1)}, u32[]{:S(2)}) copy-start(bf16[128,64]{1,0:T(8,128)(2,1)S(1)} %get-tuple-element.91.x_ref) | copy-start | bytes 49156
  121.5 22.9 %copy-start.20 = (bf16[128,64]{1,0:T(8,128)(2,1)}, bf16[128,64]{1,0:T(8,128)(2,1)S(1)}, u32[]{:S(2)}) copy-start(bf16[128,64]{1,0:T(8,128)(2,1)S(1)} %get-tuple-element.85) | copy-start | bytes 49156
  155.1 31.0 %copy-start.25 = (s32[1,2]{1,0:T(1,128)S(1)}, s32[1,2]{1,0:T(1,128)}, u32[]{:S(2)}) copy-start(s32[1,2]{1,0:T(1,128)} %param.20) | copy-start | bytes 28
  166.6 0.7 copy-start.7
  167.2 17.6 %collective-permute-start.7 = (bf16[2432,384]{1,0:T(8,128)(2,1)}, bf16[2432,384]{1,0:T(8,128)(2,1)S(1)}, u32[]{:S(2)}, u32[]{:S(2)}) collective-permute-start(bf16[2432,384]{1,0:T(8,128)(2,1)} %all-gather.3.cloned.1.call-done.own), channel_id=1, source_target_pairs={{0,2},{2,0},{1,3},{3,1},{4,6},{6,4},{5,7},{7,5},{8,10},{10,8},{9,1... | collective-permute-start | bytes 5603336 | tf_op jit(solution)/shard_map/ppermute | solution.py:71
  184.8 1.2 copy-start.26
  186.1 18.6 %copy-start.8 = (bf16[32,2432]{1,0:T(8,128)(2,1)S(1)}, bf16[32,2432]{1,0:T(8,128)(2,1)}, u32[]{:S(2)}) copy-start(bf16[32,2432]{1,0:T(8,128)(2,1)} %copy-done.7) | copy-start | bytes 466948
  191.4 0.6 copy-start.10
  205.1 0.8 copy-start.1
  206.0 0.7 copy-start.5
  206.7 11.4 %all-to-all-start.8 = ((bf16[4,32,2432]{2,1,0:T(8,128)(2,1)}), bf16[4,32,2432]{2,1,0:T(8,128)(2,1)S(1)}, u32[]{:S(2)}, u32[]{:S(2)}) async-start(bf16[4,32,2432]{2,1,0:T(8,128)(2,1)} %copy-done.1), calls=%async_computation.8 | async-start | bytes 1245184 | tf_op jit(solution)/shard_map/all_to_all | solution.py:75
  215.5 0.6 copy-start.12
  218.1 21.9 %copy-start.6 = (f32[32,2432]{1,0:T(8,128)S(1)}, f32[32,2432]{1,0:T(8,128)}, u32[]{:S(2)}) copy-start(f32[32,2432]{1,0:T(8,128)} %copy-done.5) | copy-start | bytes 933892
  239.9 10.5 %copy-start.11 = (f32[128,128]{1,0:T(8,128)S(1)}, f32[128,128]{1,0:T(8,128)}, u32[]{:S(2)}) copy-start(f32[128,128]{1,0:T(8,128)} %copy-done.10) | copy-start | bytes 196612
  239.9 10.5 %copy-start.13 = (f32[128,128]{1,0:T(8,128)S(1)}, f32[128,128]{1,0:T(8,128)}, u32[]{:S(2)}) copy-start(f32[128,128]{1,0:T(8,128)} %copy-done.12) | copy-start | bytes 196612
  239.9 10.5 %copy-start.19 = (bf16[128,64]{1,0:T(8,128)(2,1)S(1)}, bf16[128,64]{1,0:T(8,128)(2,1)}, u32[]{:S(2)}) copy-start(bf16[128,64]{1,0:T(8,128)(2,1)} %copy-done.18) | copy-start | bytes 49156
  250.4 9.4 %copy-start.21 = (bf16[128,64]{1,0:T(8,128)(2,1)S(1)}, bf16[128,64]{1,0:T(8,128)(2,1)}, u32[]{:S(2)}) copy-start(bf16[128,64]{1,0:T(8,128)(2,1)} %copy-done.20) | copy-start | bytes 49156
  259.5 6.5 %collective-permute-start.9 = (f32[72,128]{1,0:T(8,128)S(1)}, f32[72,128]{1,0:T(8,128)S(1)}, u32[]{:S(2)}, u32[]{:S(2)}) collective-permute-start(f32[72,128]{1,0:T(8,128)S(1)} %first_backward.1), channel_id=1, source_target_pairs={{0,4},{4,0},{8,12},{12,8},{1,5},{5,1},{9,13},{13,9},{2,6},{6,2},{1... | collective-permute-start | bytes 110600 | tf_op jit(solution)/shard_map/ppermute | solution.py:787
  259.8 8.0 %collective-permute-start.8 = (bf16[128,64]{1,0:T(8,128)(2,1)S(1)}, bf16[128,64]{1,0:T(8,128)(2,1)S(1)}, u32[]{:S(2)}, u32[]{:S(2)}) collective-permute-start(bf16[128,64]{1,0:T(8,128)(2,1)S(1)} %copy-done.21), channel_id=1, source_target_pairs={{0,2},{2,0},{1,3},{3,1},{4,6},{6,4},{5,7},{7,5},{8,10},{10,8},{9,1... | collective-permute-start | bytes 49160 | tf_op jit(solution)/shard_map/ppermute | solution.py:71
  266.0 4.4 %collective-permute-start.10 = (f32[72,128]{1,0:T(8,128)S(1)}, f32[72,128]{1,0:T(8,128)S(1)}, u32[]{:S(2)}, u32[]{:S(2)}) collective-permute-start(f32[72,128]{1,0:T(8,128)S(1)} %add.98), channel_id=1, source_target_pairs={{0,8},{8,0},{4,12},{12,4},{1,9},{9,1},{5,13},{13,5},{2,10},{10,2},... | collective-permute-start | bytes 110600 | tf_op jit(solution)/shard_map/ppermute | solution.py:788
  270.4 5.7 %collective-permute-start.11 = (f32[72,128]{1,0:T(8,128)S(1)}, f32[72,128]{1,0:T(8,128)S(1)}, u32[]{:S(2)}, u32[]{:S(2)}) collective-permute-start(f32[72,128]{1,0:T(8,128)S(1)} %add.99), channel_id=1, source_target_pairs={{0,2},{2,0},{1,3},{3,1},{4,6},{6,4},{5,7},{7,5},{8,10},{10,8},{9,1... | collective-permute-start | bytes 110600 | tf_op jit(solution)/shard_map/ppermute | solution.py:71
Sparse Core Ops, SparseCore 0:
  95.5 65.2 all-gather.2

commit v3 on v2

--- a/solution.py
+++ b/solution.py
@@ -142,7 +142,8 @@
     gap = -hidden % 128
     out_ref[:, :hidden] = dot_across(left_in.astype(BF), w1_ref[...]).astype(BF)
     out_ref[:, hidden : hidden + gap] = jnp.zeros((cells * STEPS, gap), BF)
-    out_ref[:, hidden + gap :] = dot_across(left_out.astype(BF), w2_ref[...]).astype(BF)
+    out_ref[:, hidden + gap : 2 * hidden + gap] = dot_across(left_out.astype(BF), w2_ref[...]).astype(BF)
+    out_ref[:, 2 * hidden + gap :] = jnp.zeros((cells * STEPS, gap), BF)
     send = pltpu.make_async_copy(out_ref, out, sems.at[0])
     send.start()
     bias_ref[...] = dot_across(shift, w1_ref[...]).astype(BF)
@@ -176,12 +177,11 @@
     send.wait()
 
 
-def student_kernel(where_ref, x_ref, packed_ref, mat_ref, mine_ref, other_ref, all_ref):
+def student_kernel(hidden, where_ref, x_ref, packed_ref, mat_ref, mine_ref, other_ref, all_ref):
     cells, seq = x_ref.shape
     width = packed_ref.shape[0]
     lanes, wide = mat_ref.shape
-    hidden = wide // 2 - (wide // 2) % 64
-    gap = wide - 2 * hidden
+    second_at = wide // 2
     group = lanes * 4 // cells
     x = turned_wide(x_ref[...]).astype(BF)
     proj = packed_ref[:, :cells]
@@ -204,7 +204,7 @@
     bias = dot((bias_col % group == 4).astype(BF), mat_ref[:, :hidden])[:1]
     z = inverse * dot(dot(x, spread).astype(BF), mat_ref[:, :hidden]) + bias
     active = gelu_both(z)[0].astype(BF)
-    high, low = split(dot_back(active, mat_ref[:, hidden + gap :]))
+    high, low = split(dot_back(active, mat_ref[:, second_at : second_at + hidden]))
     all_ref[...] = dot_back(high, spread) + dot_back(low, spread) + 0.125 * times(direct)
     half = seq // 2
     core = where_ref[2]
@@ -259,7 +259,7 @@
     both_ref[0] = turned_wide(x_ref[...])
     both_ref[1] = turned_wide(noise_ref[...])
     mine = pl.ds(pl.multiple_of(where_ref[2] * half, half), half)
-    latents = (both_ref[0, mine, :] - sigma_s * velocity_ref[...]).astype(BF)
+    latents = (both_ref[0, mine, :] - sigma_s * sum_parts(velocity_ref)).astype(BF)
     latents_ref[...] = latents
     x = ((1.0 - sigma_t) * latents.astype(F32) + sigma_t * both_ref[1, mine, :]).astype(BF)
     noised_ref[...] = x
@@ -367,11 +367,34 @@
     rows = direct_ref.shape[0]
     mine = pl.ds(pl.multiple_of(where_ref[1] * rows, rows), rows)
     all_ref[mine, :cells] += rest * direct_ref[...]
-    out_ref[...] = all_ref[...].T[: out_ref.shape[0]]
-
-
-def modulation_kernel(cond_s_ref, cond_t_ref, s_ref, t_ref, in_s, in_t, out_proj, out_ref, proj_ref):
+    final = all_ref[...].T[: out_ref.shape[1]]
+    for target in range(out_ref.shape[0]):
+        out_ref[target] = final
+
+
+def modulation_kernel(
+    cond_s_ref, cond_t_ref, s_mod, t_mod, in_s, in_t, out_proj, head, out, proj_ref, head_out,
+    s_ref, t_ref, stack_ref, head_ref, out_ref, head_all, sems
+):
     samples = cond_t_ref.shape[0]
+    cells = in_s.shape[0]
+    hidden = s_mod.shape[1]
+    stream = Stream(
+        [(head, head_ref), (s_mod, s_ref), (t_mod, t_ref)]
+        + [
+            (source, stack_ref.at[pl.ds(index * cells, cells)])
+            for index, source in enumerate((in_s, in_t, out_proj))
+        ],
+        sems,
+    )
+    stream.next()
+    head_all[:, : head_ref.shape[1]] = head_ref[...]
+    head_all[:, head_ref.shape[1] :] = jnp.zeros(
+        (head_ref.shape[0], head_all.shape[1] - head_ref.shape[1]), BF
+    )
+    keep = pltpu.make_async_copy(head_all, head_out, sems.at[6])
+    keep.start()
+    stream.next()
 
     def product(cond, weight):
         extent = cond.shape[0]
@@ -389,12 +412,19 @@
         return ((row // 8 == col) & (row % 8 == first)).astype(BF)
 
     total = dot(place(16, LAYERS, True), product(cond_s_ref[...], s_ref[...]))
+    stream.next()
     for layer in range(LAYERS):
         part = product(cond_t_ref[...], t_ref[layer])
         total = total + dot(place(samples, layer, False), part)
-    out_ref[...] = total.astype(BF)
-    stacked = jnp.concatenate([in_s[...], in_t[...], out_proj[...]], axis=0)
-    proj_ref[...] = turned_wide(stacked).astype(BF)
+    out_ref[:, :hidden] = total.astype(BF)
+    out_ref[:, hidden:] = jnp.zeros((samples * 8, out_ref.shape[1] - hidden), BF)
+    send = pltpu.make_async_copy(out_ref, out, sems.at[7])
+    send.start()
+    for _ in range(3):
+        stream.next()
+    proj_ref[...] = turned_wide(stack_ref[...]).astype(BF)
+    keep.wait()
+    send.wait()
 
 
 def sum_parts(parts_ref):
@@ -404,42 +434,69 @@
     return total
 
 
-def share(values, all_ref):
-    for target in range(all_ref.shape[0]):
-        all_ref[target] = values
-
-
-def first_middle_kernel(where_ref, parts_ref, g_ref, vector_ref, mine_ref, all_ref):
+def share(values_ref, everyone, sems):
+    copies = [
+        pltpu.make_async_copy(values_ref, everyone.at[target], sems.at[target])
+        for target in range(everyone.shape[0])
+    ]
+    for copy in copies:
+        copy.start()
+    for copy in copies:
+        copy.wait()
+
+
+def first_middle_kernel(where_ref, parts_ref, g_ref, vector_ref, mine_ref, everyone, sems):
     rows = mine_ref.shape[0]
     before = g_ref[pl.ds(pl.multiple_of(where_ref[1] * rows, rows), rows), :].astype(F32)
     after = (before + vector_ref[2:3] * sum_parts(parts_ref)).astype(BF)
     mine_ref[...] = after
-    share(after, all_ref)
-
-
-def last_middle_kernel(parts_ref, g_ref, vector_ref, mine_ref, all_ref):
+    share(mine_ref, everyone, sems)
+
+
+def last_middle_kernel(parts_ref, g_ref, vector_ref, mine_ref, everyone, sems):
     after = (g_ref[...].astype(F32) + vector_ref[5:6] * sum_parts(parts_ref)).astype(BF)
     mine_ref[...] = after
-    share(after, all_ref)
-
-
-def last_back_kernel(parts_ref, g_ref, vector_ref, grad_ref, all_ref):
+    share(mine_ref, everyone, sems)
+
+
+def last_back_kernel(parts_ref, g_ref, vector_ref, grad_ref, everyone, share_ref, sems):
     normed, inverse = normalize(g_ref[...].astype(F32))
     grad = ln_back(sum_parts(parts_ref), normed, inverse)
     grad_ref[...] = grad
-    share((vector_ref[5:6] * grad).astype(BF), all_ref)
-
-
-def first_back_kernel(parts_ref, g_ref, old_ref, vector_ref, packed_ref, direct_ref, all_ref):
+    share_ref[...] = (vector_ref[5:6] * grad).astype(BF)
+    share(share_ref, everyone, sems)
+
+
+def first_back_kernel(parts_ref, g_ref, old_ref, vector_ref, packed_ref, direct_ref, everyone, share_ref, sems):
     normed, inverse = normalize(g_ref[...].astype(F32))
     grad = old_ref[...] + ln_back(sum_parts(parts_ref), normed, inverse)
     cells = direct_ref.shape[1]
     direct_ref[...] = dot(grad.astype(BF), packed_ref[:, cells : 2 * cells])
-    share((vector_ref[2:3] * grad).astype(BF), all_ref)
-
-
-def head_kernel(layer, pick_ref, g_ref, out_own, out_sib, own, sib, back_out, score_ref, weight_ref, back_ref, use_ref, sems):
-    stream = Stream([(own, weight_ref.at[0]), (sib, weight_ref.at[1])], sems)
+    share_ref[...] = (vector_ref[2:3] * grad).astype(BF)
+    share(share_ref, everyone, sems)
+
+
+def block_owner(fsdp, block):
+    x_hi, z = fsdp // 4, fsdp % 4
+    return (x_hi ^ (block & 1)) * 4 + (z ^ ((block >> 1 & 1) ^ (block >> 2 & 1) * 3))
+
+
+def swap_fsdp(values, pattern):
+    other = lax.ppermute(values, "fsdp", [(at, at ^ pattern) for at in range(8)])
+    return jnp.concatenate([values, other], axis=0)
+
+
+def head_kernel(layer, pick_ref, where_ref, g_ref, out_own, out_sib, own, sib, back_out, score_ref, weight_ref, back_ref, use_ref, sems):
+    blocks = 8
+    size = own.shape[0] // blocks
+    plan = []
+    for side, source in enumerate((own, sib)):
+        for block in range(blocks):
+            row = pl.multiple_of(block_owner(where_ref[3], block) * size, size)
+            plan.append(
+                (source.at[pl.ds(block * size, size)], weight_ref.at[side, pl.ds(row, size)])
+            )
+    stream = Stream(plan, sems)
     use_ref[...] = jnp.zeros(use_ref.shape, F32)
     for side, outs in enumerate((out_own, out_sib)):
         for head in range(2):
@@ -450,7 +507,8 @@
     back = None
     scores = None
     for side in range(2):
-        stream.next()
+        for _ in range(blocks):
+            stream.next()
         weight = weight_ref[side]
         e = dot(quantised, weight)
         sigm = 1.0 / (1.0 + jnp.exp(-e))
@@ -462,7 +520,7 @@
         part = [jnp.sum(active * outs[head : head + 1], axis=1, keepdims=True) for head in range(2)]
         scores = part if scores is None else [old + new for old, new in zip(scores, part)]
     back_ref[...] = back.astype(BF)
-    send = pltpu.make_async_copy(back_ref, back_out, sems.at[2])
+    send = pltpu.make_async_copy(back_ref, back_out, sems.at[2 * blocks])
     send.start()
     lane = lax.broadcasted_iota(jnp.int32, score_ref.shape, 1)
     score_ref[...] = jnp.where(lane == 0, scores[0], 0.0) + jnp.where(lane == 1, scores[1], 0.0)
@@ -539,19 +597,24 @@
     sig_steps = (1 + jnp.arange(STEPS)).astype(F32) * 0.25
     cond_s = jax.nn.silu(embed_block(1000.0 * sig_steps, width, rows, start))
     cond_t = jax.nn.silu(embed_block(1000.0 * sig_all_t, width, rows, start))
-    where = jnp.stack([sample, at_y, at_core]).astype(jnp.int32)
+    at_grp = lax.axis_index("grp")
+    where = jnp.stack([sample, at_y, at_core, lax.axis_index("fsdp")]).astype(jnp.int32)
     block = sample * rows // columns
     places = [block, sample * rows // rows % (columns // rows)]
     for offset in (0, 8, 16):
         places += [(block + offset) // 3, (block + offset) % 3]
     places = jnp.stack(places).astype(jnp.int32)
-    spare = -columns % 128
-    head_block = jnp.pad(d_w1, ((0, 0), (0, spare)))
+    head_wide = columns + -columns % 128
+    mod_wide = s_mod.shape[1] + -s_mod.shape[1] % 128
     picks = layer_pick[0]
-    mod_part, projections = here(
+    mod_part, projections, head_block = here(
         modulation_kernel,
         "modulation",
-        (array((samples * 8, s_mod.shape[1]), BF), array((columns, 3 * cells), BF)),
+        (
+            array((samples * 8, mod_wide), BF),
+            array((columns, 3 * cells), BF),
+            array((rows, head_wide), BF),
+        ),
         (
             jnp.pad(cond_s, ((0, 16 - STEPS), (0, 0))),
             cond_t,
@@ -560,20 +623,32 @@
             in_proj_s,
             in_proj_t,
             out_proj,
+            d_w1,
+        ),
+        far=6,
+        far_out=(0, 2),
+        scratch=(
+            pltpu.VMEM(s_mod.shape, BF),
+            pltpu.VMEM(t_mod.shape, BF),
+            pltpu.VMEM((3 * cells, columns), BF),
+            pltpu.VMEM(d_w1.shape, BF),
+            pltpu.VMEM((samples * 8, mod_wide), BF),
+            pltpu.VMEM((rows, head_wide), BF),
+            pltpu.SemaphoreType.DMA((8,)),
         ),
     )
     mod_part, projections, where, places, head_block, picks = lax.optimization_barrier(
         (mod_part, projections, where, places, head_block, picks)
     )
-    mod_part = mod_part.reshape(samples, 8, s_mod.shape[1])
+    mod_part = mod_part.reshape(samples, 8, mod_wide)
     mods = jnp.sum(lax.all_to_all(mod_part, SAMPLE, 0, 0).astype(F32), axis=0)
     kinds = layers + STEPS
-    mods = mods[:kinds].reshape(kinds * 3, columns).astype(BF)
+    mods = mods[:kinds, : 3 * columns].reshape(kinds * 3, columns).astype(BF)
     packed = jnp.concatenate([projections, mods.T], axis=1)
     gathered = lax.all_gather(packed, TP, axis=0, tiled=False)
 
     gap = -hidden % 128
-    both_wide = 2 * hidden + gap
+    both_wide = 2 * (hidden + gap)
     parts, part_bias = here(
         product_kernel,
         "product",
@@ -589,50 +664,12 @@
     piece = cells * STEPS // samples
     chunk = cells // samples
     t_w1 = jnp.swapaxes(t_w1, 1, 2)
-    parts, t_w1, t_w2, d_w2 = lax.optimization_barrier((parts, t_w1, t_w2, d_w2))
+    parts, gathered, t_w1, t_w2, d_w2 = lax.optimization_barrier((parts, gathered, t_w1, t_w2, d_w2))
     w2_sib = sibling(t_w2)
     w1_sib = sibling(t_w1)
     d_w2_sib = sibling(d_w2)
     received = lax.all_to_all(parts.reshape(samples, piece, both_wide), SAMPLE, 0, 0)
 
-    chosen = here(
-        select_kernel,
-        "select",
-        array((samples * 8, both_wide), BF),
-        (student_step, received, part_bias),
-        scalars=1,
-        far_out=(0,),
-        scratch=(pltpu.VMEM((samples * 8, both_wide), BF), pltpu.SemaphoreType.DMA((1,))),
-    )
-    mine = lax.all_to_all(chosen.reshape(samples, 8, both_wide), SAMPLE, 0, 0)
-    mine = mine.reshape(samples * 8, both_wide)
-
-    latent_in = noisy_latents[0].T
-    noise = teacher_noise[0].T
-    packed = gathered.reshape(width, -1)
-    half_out = array((half, cells), F32)
-    velocity, other = here(
-        student_kernel,
-        "student",
-        (half_out, half_out),
-        (where, latent_in, packed, mine),
-        scalars=1,
-        scratch=(pltpu.VMEM((seq, cells), F32),),
-    )
-    velocity = velocity + sibling(other)
-    velocity = velocity + lax.ppermute(velocity, "y", [(0, 1), (1, 0), (2, 3), (3, 2)])
-    velocity = velocity + lax.ppermute(velocity, "y", [(0, 2), (2, 0), (1, 3), (3, 1)])
-
-    head_block, _ = lax.optimization_barrier((head_block, other))
-    head_own = lax.all_gather(head_block, SAMPLE, axis=0, tiled=True)
-
-    def both(values, axis):
-        other = sibling(values)
-        first = jnp.where(at_core == 0, values, other)
-        second = jnp.where(at_core == 0, other, values)
-        return jnp.concatenate([first, second], axis=axis)
-
-    gathered, _ = lax.optimization_barrier((gathered, other))
     first_own, vectors = here(
         first_product_kernel,
         "first_product",
@@ -646,6 +683,52 @@
         ),
         limit=44,
     )
+    received, first_own, vectors = lax.optimization_barrier((received, first_own, vectors))
+
+    chosen = here(
+        select_kernel,
+        "select",
+        array((samples * 8, both_wide), BF),
+        (student_step, received, part_bias),
+        scalars=1,
+        far_out=(0,),
+        scratch=(pltpu.VMEM((samples * 8, both_wide), BF), pltpu.SemaphoreType.DMA((1,))),
+    )
+    mine = lax.all_to_all(chosen.reshape(samples, 8, both_wide), SAMPLE, 0, 0)
+    mine = mine.reshape(samples * 8, both_wide)
+
+    latent_in = noisy_latents[0].T
+    noise = teacher_noise[0].T
+    packed = gathered.reshape(width, -1)
+    half_out = array((half, cells), F32)
+    velocity, other = here(
+        functools.partial(student_kernel, hidden),
+        "student",
+        (half_out, half_out),
+        (where, latent_in, packed, mine),
+        scalars=1,
+        scratch=(pltpu.VMEM((seq, cells), F32),),
+    )
+    velocity = velocity + sibling(other)
+    head_block, _ = lax.optimization_barrier((head_block, mine))
+    head_other = lax.ppermute(head_block, "grp", [(0, 1), (1, 0)])
+    head_other, _ = lax.optimization_barrier((head_other, velocity))
+    head_pair = jnp.concatenate(
+        [
+            jnp.where(at_grp == 0, head_block, head_other),
+            jnp.where(at_grp == 0, head_other, head_block),
+        ],
+        axis=0,
+    )
+    head_two = swap_fsdp(head_pair, 4)
+    velocity = swap_y(jnp.broadcast_to(velocity[None], (4,) + velocity.shape))
+
+    def both(values, axis):
+        other = sibling(values)
+        first = jnp.where(at_core == 0, values, other)
+        second = jnp.where(at_core == 0, other, values)
+        return jnp.concatenate([first, second], axis=axis)
+
     first_sib = sibling(first_own)
     velocity, w1_sib, w2_sib, d_w2_sib = lax.optimization_barrier((velocity, w1_sib, w2_sib, d_w2_sib))
 
@@ -691,13 +774,21 @@
         return swap_y(partial.reshape(4, quarter, width))
 
     last = (t_w1, w1_sib, t_w2, w2_sib)
+    four = pltpu.SemaphoreType.DMA((4,))
+    quarter_rows = pltpu.VMEM((quarter, width), BF)
     g_1_mine, g_1 = here(
         first_middle_kernel,
         "first_middle",
         (mine_out, rows_out),
         (where, sums(y_0), g_0, vectors),
         scalars=1,
-    )
+        far_out=(1,),
+        scratch=(four,),
+    )
+    head_two, _ = lax.optimization_barrier((head_two, y_0))
+    head_four = swap_fsdp(head_two, 1)
+    head_four, _ = lax.optimization_barrier((head_four, g_1_mine))
+    head_own = swap_fsdp(head_four, 3)
     g_1 = swap_y(g_1).reshape(half, width)
     y_1, slope_1 = here(
         forward_kernel,
@@ -710,7 +801,12 @@
         limit=44,
     )
     g_2_mine, g_2 = here(
-        last_middle_kernel, "last_middle", (mine_out, rows_out), (sums(y_1), g_1_mine, vectors)
+        last_middle_kernel,
+        "last_middle",
+        (mine_out, rows_out),
+        (sums(y_1), g_1_mine, vectors),
+        far_out=(1,),
+        scratch=(four,),
     )
     head_own, _ = lax.optimization_barrier((head_own, g_2_mine))
     head_sib = sibling(head_own)
@@ -721,15 +817,15 @@
             functools.partial(head_kernel, layer),
             name,
             (tokens_out, array((half, 128), F32)),
-            (picks, g, d_w2, d_w2_sib, head_own, head_sib),
-            scalars=1,
+            (picks, where, g, d_w2, d_w2_sib, head_own, head_sib),
+            scalars=2,
             far=2,
             far_out=(0,),
             scratch=(
                 pltpu.VMEM((2,) + head_own.shape, BF),
                 token_rows,
                 pltpu.VMEM((2, 8, head_own.shape[1]), F32),
-                pltpu.SemaphoreType.DMA((3,)),
+                pltpu.SemaphoreType.DMA((17,)),
             ),
         )
 
@@ -740,6 +836,8 @@
         "last_back",
         (array((quarter, width), F32), rows_out),
         (sums(head_back_2), g_2_mine, vectors),
+        far_out=(1,),
+        scratch=(quarter_rows, four),
     )
     g_1, latents, _ = lax.optimization_barrier((g_1, latents, dg_2))
     latents = both(latents, 0)
@@ -759,11 +857,13 @@
         "first_back",
         (array((quarter, cells), F32), rows_out),
         (sums(du_1), g_1_mine, dg_2, vectors, packed),
+        far_out=(1,),
+        scratch=(quarter_rows, four),
     )
     final = here(
         first_backward_kernel,
         "first_backward",
-        array((cells + 8, half), F32),
+        array((4, cells + 8, half), F32),
         (
             where,
             teacher_step,
@@ -784,9 +884,7 @@
         scratch=(matrix, inner, pltpu.VMEM((half, 2 * cells), F32), pltpu.SemaphoreType.DMA((3,))),
         limit=44,
     )
-    final = final + lax.ppermute(final, "y", [(0, 1), (1, 0), (2, 3), (3, 2)])
-    final = final + lax.ppermute(final, "y", [(0, 2), (2, 0), (1, 3), (3, 1)])
-    final = both(final, 1)
+    final = both(jnp.sum(swap_y(final), axis=0), 1)
     return (latents[None], final[cells : cells + heads][None], final[:cells].T[None])
 
 

time: 285 us -> 276 us (0.968)
  blocking collectives: 151 us -> 97.2 us
  waiting for transfers between devices: 10.2 us -> 41.6 us
  starting transfers between devices: 28.3 us -> 48.3 us
  between operations: 14.6 us -> 1.29 us
  Pallas kernels: 65.5 us -> 71.9 us
  other arithmetic: 2.47 us -> 8.52 us
  local copies, waits for them, and re-layouts: 11.8 us -> 6.44 us
    all_to_all x7 -> x4, blocking collectives: 79.9 us -> 48.7 us  [swap_y(): return lax.all_to_all(values, 'y', 0, 0)]
    all_to_all x1 -> x0, blocking collectives: 23.4 us -> none  [body(): lax.all_to_all(parts.reshape(samples, piece, both_wide), SAMPLE, 0, 0)]
    all_to_all x1 -> x6, starting transfers between devices: 3.48 us -> 20.8 us  [swap_y(): return lax.all_to_all(values, 'y', 0, 0)]
    all_to_all x0 -> x1, waiting for transfers between devices: none -> 15.5 us  [body(): lax.all_to_all(parts.reshape(samples, piece, both_wide), SAMPLE, 0, 0)]
    all_to_all x1 -> x6, waiting for transfers between devices: 1.91 us -> 16.4 us  [swap_y(): return lax.all_to_all(values, 'y', 0, 0)]
    pallas_call x15, Pallas kernels: 65.5 us -> 71.9 us  [here(): pl.pallas_call(kernel, name=name, out_shape=shapes if many else shapes[0]...]
    concatenate x0 -> x4, other arithmetic: none -> 6.03 us  [the longest x3 6 us: swap_fsdp(): return jnp.concatenate([values, other], axis=0)]
    unnamed x55 -> x41, local copies, waits for them, and re-layouts: 9.93 us -> 5.21 us
  transfers between devices with their start and end apart: 14 -> 19, of which waited for: 6 -> 10; matrix products, arithmetic and copies ran while one was open for 0% -> 3% of each run, Pallas kernels for 12% -> 13%
where the time goes in v3:
time: 276 us; the launch traced here: 275 us
  blocking collectives  97.2 us (35%)
  Pallas kernels  71.9 us (26%)
  starting transfers between devices  48.3 us (18%)
  waiting for transfers between devices  41.6 us (15%)
  other arithmetic  8.52 us (3%)
  local copies, waits for them, and re-layouts  6.44 us (2%)
    pallas_call x15, Pallas kernels, here(): pl.pallas_call(kernel, name=name, out_shape=shapes if many else shapes[0]...  71.9 us
    all_to_all x4, blocking collectives, swap_y(): return lax.all_to_all(values, 'y', 0, 0)  48.7 us
    ppermute x8, starting transfers between devices, sibling(): return lax.ppermute(values, 'core', [(0, 1), (1, 0)])  21.1 us
    all_to_all x6, starting transfers between devices, swap_y(): return lax.all_to_all(values, 'y', 0, 0)  20.8 us
    all_gather x1, blocking collectives, body(): gathered = lax.all_gather(packed, TP, axis=0, tiled=False)  16.5 us
    all_to_all x6, waiting for transfers between devices, swap_y(): return lax.all_to_all(values, 'y', 0, 0)  16.4 us
    all_to_all x1, blocking collectives, body(): mods = jnp.sum(lax.all_to_all(mod_part, SAMPLE, 0, 0).astype(F32), axis=0)  16.2 us
    all_to_all x1, blocking collectives, body(): mine = lax.all_to_all(chosen.reshape(samples, 8, both_wide), SAMPLE, 0, 0)  15.9 us
  transfers between devices with their start and end apart: 19, of which 10 were waited for; matrix products, arithmetic and copies ran while one was open for 3% of the time, Pallas kernels for 13%

profile of v3, /device:TPU:1, one launch (start us, length us, event | category | flops | bytes accessed | tf_op | source)
XLA Modules:
  0.0 275.2 jit_solution(16766763813519711374)
XLA Ops:
  0.8 0.7 convert_element_type.29
  1.6 0.2 fusion.2.cond_t_ref
  2.0 2.7 modulation.1
  4.7 16.2 %all_to_all.65 = bf16[16,8,1024]{2,1,0:T(8,128)(2,1)S(1)} all-to-all(bf16[16,8,1024]{2,1,0:T(8,128)(2,1)} %bitcast.70), channel_id=1, replica_groups=mesh['fsdp'=8,'y'=4,'core'=2,'grp'=2] {'fsdp','grp'}, dimensions={0} | all-to-all | bytes 524288 | tf_op jit(solution)/shard_map/all_to_all | solution.py:644
  21.0 0.1 copy.22
  21.3 16.5 %all-gather = bf16[2432,210]{1,0:T(8,128)(2,1)S(1)} all-gather(bf16[304,210]{1,0:T(8,128)(2,1)S(1)} %pad_maximum_fusion.4), channel_id=2, replica_groups=mesh['fsdp'=8,'y'=4,'core'=2,'grp'=2] {'y','core'}, dimensions={0}, use_global_device_ids=true | all-gather | bytes 1149120 | tf_op jit(solution)/shard_map/all_gather | solution.py:648
  37.8 3.1 %product.1 = (bf16[256,2560]{1,0:T(8,128)(2,1)}, bf16[8,1216]{1,0:T(8,128)(2,1)S(1)}) custom-call(s32[8]{0:T(128)S(1)} %stack.55.at_ref, bf16[8,304,210]{2,1,0:T(8,128)(2,1)S(1)} %bitcast.45, bf16[152,1216]{1,0:T(8,128)(2,1)S(1)} %copy-done, bf16[152,1216]{1,0:T(8,128)(2,1)S(1)} %bitcast.53), custom_call_target="tpu_custom_call" | custom-call | tf_op jit(solution)/shard_map/product/pallas_call | solution.py:547
  40.9 0.2 collective-permute-start.1
  41.2 0.4 collective-permute-start.2
  41.5 3.7 %all-to-all-start.1 = ((bf16[16,16,2560]{2,1,0:T(8,128)(2,1)}), bf16[16,16,2560]{2,1,0:T(8,128)(2,1)S(1)}, u32[]{:S(2)}, u32[]{:S(2)}) async-start(bf16[16,16,2560]{2,1,0:T(8,128)(2,1)} %bitcast.65), calls=%async_computation.1 | async-start | bytes 2621440 | tf_op jit(solution)/shard_map/all_to_all | solution.py:671
  45.2 5.8 %first_product.1 = (f32[72,1216]{1,0:T(8,128)S(1)}, f32[8,2432]{1,0:T(8,128)S(1)}) custom-call(bf16[8,304,210]{2,1,0:T(8,128)(2,1)S(1)} %bitcast.46, bf16[2,1216,2432]{2,1,0:T(8,128)(2,1)} %bitcast.60), custom_call_target="tpu_custom_call" | custom-call | tf_op jit(solution)/shard_map/first_product/pallas_call | solution.py:547
  51.1 15.5 %all-to-all-done.1.parts_ref = bf16[16,16,2560]{2,1,0:T(8,128)(2,1)S(1)} async-done(((bf16[16,16,2560]{2,1,0:T(8,128)(2,1)}), bf16[16,16,2560]{2,1,0:T(8,128)(2,1)S(1)}, u32[]{:S(2)}, u32[]{:S(2)}) %all-to-all-start.1) | async-done | bytes 1310752 | tf_op jit(solution)/shard_map/all_to_all | solution.py:671
  66.6 1.9 select.4
  68.5 15.9 %all_to_all.66 = bf16[16,8,2560]{2,1,0:T(8,128)(2,1)S(1)} all-to-all(bf16[16,8,2560]{2,1,0:T(8,128)(2,1)} %bitcast.63), channel_id=1, replica_groups=mesh['fsdp'=8,'y'=4,'core'=2,'grp'=2] {'fsdp','grp'}, dimensions={0} | all-to-all | bytes 1310720 | tf_op jit(solution)/shard_map/all_to_all | solution.py:697
  84.3 2.7 student.1
  87.0 2.9 %collective-permute-start = (f32[128,64]{1,0:T(8,128)S(1)}, f32[128,64]{1,0:T(8,128)S(1)}, u32[]{:S(2)}, u32[]{:S(2)}) collective-permute-start(f32[128,64]{1,0:T(8,128)S(1)} %get-tuple-element.73), channel_id=1, source_target_pairs={{0,2},{2,0},{1,3},{3,1},{4,6},{6,4},{5,7},{7,5},{8,10},{10,8},{9,1... | collective-permute-start | bytes 98312 | tf_op jit(solution)/shard_map/ppermute | solution.py:71
  90.0 0.9 collective-permute-done
  91.0 1.8 collective-permute-start.6
  92.8 0.6 collective-permute-start.4
  93.5 0.7 broadcast_in_dim.39
  94.2 3.5 %all-to-all-start.3 = ((f32[4,128,64]{1,2,0:T(8,128)}), f32[4,128,64]{1,2,0:T(8,128)S(1)}, u32[]{:S(2)}, u32[]{:S(2)}) async-start(f32[4,128,64]{1,2,0:T(8,128)} %broadcast_in_dim.39), calls=%async_computation.3 | async-start | bytes 262144 | tf_op jit(solution)/shard_map/all_to_all | solution.py:75
  97.7 1.6 collective-permute-done.6
  99.3 0.8 pad_maximum_fusion.2
  100.1 2.4 all-to-all-done.3
  102.7 8.0 %first_forward.1 = (bf16[128,2432]{1,0:T(8,128)(2,1)}, bf16[2,128,1216]{2,1,0:T(8,128)(2,1)}, bf16[128,64]{1,0:T(8,128)(2,1)S(1)}, bf16[128,64]{1,0:T(8,128)(2,1...) custom-call(s32[4]{0:T(128)S(1)} %pad_add_fusion.where_ref, s32[16]{0:T(128)S(1)} %copy-done.15, ...), custom_call_target="tpu_custom_call" | custom-call | tf_op jit(solution)/shard_map/first_forward/pallas_call | solution.py:547
  110.7 0.6 copy-done.10
  111.3 0.6 copy-done.12
  111.9 3.5 %all-to-all-start.4 = ((bf16[4,32,2432]{2,1,0:T(8,128)(2,1)}), bf16[4,32,2432]{2,1,0:T(8,128)(2,1)S(1)}, u32[]{:S(2)}, u32[]{:S(2)}) async-start(bf16[4,32,2432]{2,1,0:T(8,128)(2,1)} %bitcast.66), calls=%async_computation.4 | async-start | bytes 1245184 | tf_op jit(solution)/shard_map/all_to_all | solution.py:75
  115.4 7.1 %collective-permute-done.7 = bf16[608,384]{1,0:T(8,128)(2,1)} collective-permute-done((bf16[608,384]{1,0:T(8,128)(2,1)}, bf16[608,384]{1,0:T(8,128)(2,1)}, u32[]{:S(2)}, u32[]{:S(2)}) %collective-permute-start.7) | collective-permute-done | bytes 466976 | tf_op jit(solution)/shard_map/ppermute | solution.py:485
  122.5 2.2 pad_maximum_fusion.1
  124.7 1.5 first_middle.1
  126.2 0.9 collective-permute-start.8
  127.1 10.9 %all_to_all.67 = bf16[4,32,2432]{2,1,0:T(8,128)(2,1)S(1)} all-to-all(bf16[4,32,2432]{2,1,0:T(8,128)(2,1)} %get-tuple-element.82), channel_id=1, replica_groups=mesh['fsdp'=8,'y'=4,'core'=2,'grp'=2] {'y'}, dimensions={0} | all-to-all | bytes 1245184 | tf_op jit(solution)/shard_map/all_to_all | solution.py:75
  138.0 10.7 %forward.1 = (bf16[128,2432]{1,0:T(8,128)(2,1)}, bf16[2,128,1216]{2,1,0:T(8,128)(2,1)}) custom-call(bf16[128,2432]{1,0:T(8,128)(2,1)S(1)} %bitcast.47, f32[8,2432]{1,0:T(8,128)S(1)} %get-tuple-element.81.vector_ref, bf16[2,1216,2432]{2,1,0:T(8,128)(2,1)} %bitcast.61, bf16[2,1216,2432]{2,1,0:T(8,128)(2,1)} %collective-permute-done.1.up_sib, ...), custom_call_target="tpu_custom_call" | custom-call | tf_op jit(solution)/shard_map/forward/pallas_call | solution.py:547
  148.8 3.5 %all-to-all-start.6 = ((bf16[4,32,2432]{2,1,0:T(8,128)(2,1)}), bf16[4,32,2432]{2,1,0:T(8,128)(2,1)S(1)}, u32[]{:S(2)}, u32[]{:S(2)}) async-start(bf16[4,32,2432]{2,1,0:T(8,128)(2,1)} %bitcast.67), calls=%async_computation.6 | async-start | bytes 1245184 | tf_op jit(solution)/shard_map/all_to_all | solution.py:75
  152.3 3.0 %pad_maximum_fusion.own = bf16[2432,384]{1,0:T(8,128)(2,1)} fusion(bf16[1216,384]{1,0:T(8,128)(2,1)} %collective-permute-done.8, bf16[1216,384]{1,0:T(8,128)(2,1)} %pad_maximum_fusion.1), kind=kLoop, calls=%fused_computation | loop fusion | flops 3735552 | bytes 3735552 | tf_op jit(solution)/shard_map/concatenate | solution.py:486
  155.3 4.4 %all-to-all-done.6.parts_ref = bf16[4,32,2432]{2,1,0:T(8,128)(2,1)S(1)} async-done(((bf16[4,32,2432]{2,1,0:T(8,128)(2,1)}), bf16[4,32,2432]{2,1,0:T(8,128)(2,1)S(1)}, u32[]{:S(2)}, u32[]{:S(2)}) %all-to-all-start.6) | async-done | bytes 622624 | tf_op jit(solution)/shard_map/all_to_all | solution.py:75
  159.7 1.0 last_middle.1
  160.7 5.5 %collective-permute-start.9 = (bf16[2432,384]{1,0:T(8,128)(2,1)}, bf16[2432,384]{1,0:T(8,128)(2,1)S(1)}, u32[]{:S(2)}, u32[]{:S(2)}) collective-permute-start(bf16[2432,384]{1,0:T(8,128)(2,1)} %pad_maximum_fusion.own), channel_id=1, source_target_pairs={{0,2},{2,0},{1,3},{3,1},{4,6},{6,4},{5,7},{7,5},{8,10},{10,8},{9,1... | collective-permute-start | bytes 5603336 | tf_op jit(solution)/shard_map/ppermute | solution.py:71
  166.2 13.9 %all_to_all.68 = bf16[4,32,2432]{2,1,0:T(8,128)(2,1)S(1)} all-to-all(bf16[4,32,2432]{2,1,0:T(8,128)(2,1)} %get-tuple-element.88), channel_id=1, replica_groups=mesh['fsdp'=8,'y'=4,'core'=2,'grp'=2] {'y'}, dimensions={0} | all-to-all | bytes 1245184 | tf_op jit(solution)/shard_map/all_to_all | solution.py:75
  180.1 1.2 copy-done.18
  181.3 5.6 %head_last.1 = (bf16[128,2432]{1,0:T(8,128)(2,1)}, f32[128,128]{1,0:T(8,128)S(1)}) custom-call(s32[2]{0:T(128)S(1)} %bitcast.57, s32[4]{0:T(128)S(1)} %pad_add_fusion.where_ref, bf16[128,2432]{1,0:T(8,128)(2,1)S(1)} %bitcast.52, f32[2,304]{1,0:T(2,128)S(1)} %copy-done.14, f32[2,304]{1,0:T(2,128)S(1)} %collective-permute-done.3.out_sib, ...), custom_call_target="tpu_custom_call" | custom-call | tf_op jit(solution)/shard_map/head_last/pallas_call | solution.py:547
  187.0 0.6 copy-done.5
  187.6 13.0 %all_to_all.69.parts_ref = bf16[4,32,2432]{2,1,0:T(8,128)(2,1)S(1)} all-to-all(bf16[4,32,2432]{2,1,0:T(8,128)(2,1)} %bitcast.68), channel_id=1, replica_groups=mesh['fsdp'=8,'y'=4,'core'=2,'grp'=2] {'y'}, dimensions={0} | all-to-all | bytes 1245184 | tf_op jit(solution)/shard_map/all_to_all | solution.py:75
  200.6 1.3 last_back.1
  201.9 0.7 copy-done.2
  202.6 3.5 %all-to-all-start.9 = ((bf16[4,32,2432]{2,1,0:T(8,128)(2,1)}), bf16[4,32,2432]{2,1,0:T(8,128)(2,1)S(1)}, u32[]{:S(2)}, u32[]{:S(2)}) async-start(bf16[4,32,2432]{2,1,0:T(8,128)(2,1)} %get-tuple-element.100), calls=%async_computation.9 | async-start | bytes 1245184 | tf_op jit(solution)/shard_map/all_to_all | solution.py:75
  206.1 5.7 %head_first.1 = (bf16[128,2432]{1,0:T(8,128)(2,1)}, f32[128,128]{1,0:T(8,128)S(1)}) custom-call(s32[2]{0:T(128)S(1)} %bitcast.58, s32[4]{0:T(128)S(1)} %pad_add_fusion.where_ref, bf16[128,2432]{1,0:T(8,128)(2,1)S(1)} %bitcast.48, f32[2,304]{1,0:T(2,128)S(1)} %copy-done.14, f32[2,304]{1,0:T(2,128)S(1)} %collective-permute-done.3.out_sib, ...), custom_call_target="tpu_custom_call" | custom-call | tf_op jit(solution)/shard_map/head_first/pallas_call | solution.py:547
  211.7 0.6 copy-done.7
  212.4 2.0 all-to-all-done.9
  214.3 10.9 %backward.1 = bf16[128,2432]{1,0:T(8,128)(2,1)} custom-call(bf16[128,2432]{1,0:T(8,128)(2,1)S(1)} %bitcast.50, f32[8,2432]{1,0:T(8,128)S(1)} %get-tuple-element.81.vector_ref, bf16[2,128,1216]{2,1,0:T(8,128)(2,1)} %get-tuple-element.101.slope, bf16[128,2432]{1,0:T(8,128)(2,1)} %get-tuple-element.103.head, bf16[2,1216,2432]{2,1,0:T(8,128)(2,1)} %bitcast.62, ...), custom_call_target="tpu_custom_call" | custom-call | tf_op jit(solution)/shard_map/backward/pallas_call | solution.py:547
  225.3 10.9 %all_to_all.70.parts_ref = bf16[4,32,2432]{2,1,0:T(8,128)(2,1)S(1)} all-to-all(bf16[4,32,2432]{2,1,0:T(8,128)(2,1)} %bitcast.64), channel_id=1, replica_groups=mesh['fsdp'=8,'y'=4,'core'=2,'grp'=2] {'y'}, dimensions={0} | all-to-all | bytes 1245184 | tf_op jit(solution)/shard_map/all_to_all | solution.py:75
  236.2 1.3 first_back.1
  237.6 3.5 %all-to-all-start.11 = ((bf16[4,32,2432]{2,1,0:T(8,128)(2,1)}), bf16[4,32,2432]{2,1,0:T(8,128)(2,1)S(1)}, u32[]{:S(2)}, u32[]{:S(2)}) async-start(bf16[4,32,2432]{2,1,0:T(8,128)(2,1)} %get-tuple-element.104), calls=%async_computation.11 | async-start | bytes 1245184 | tf_op jit(solution)/shard_map/all_to_all | solution.py:75
  241.1 4.7 %collective-permute-start.10 = (bf16[128,64]{1,0:T(8,128)(2,1)S(1)}, bf16[128,64]{1,0:T(8,128)(2,1)S(1)}, u32[]{:S(2)}, u32[]{:S(2)}) collective-permute-start(bf16[128,64]{1,0:T(8,128)(2,1)S(1)} %copy-done.13), channel_id=1, source_target_pairs={{0,2},{2,0},{1,3},{3,1},{4,6},{6,4},{5,7},{7,5},{8,10},{10,8},{9,1... | collective-permute-start | bytes 49160 | tf_op jit(solution)/shard_map/ppermute | solution.py:71
  245.7 2.7 all-to-all-done.11
  248.5 9.7 %first_backward.1 = f32[4,72,128]{2,1,0:T(8,128)} custom-call(s32[4]{0:T(128)S(1)} %pad_add_fusion.where_ref, s32[16]{0:T(128)S(1)} %copy-done.16, bf16[128,2432]{1,0:T(8,128)(2,1)S(1)} %bitcast.51, bf16[128,64]{1,0:T(8,128)(2,1)S(1)} %copy-done.11, f32[128,128]{1,0:T(8,128)S(1)} %get-tuple-element.106.back_ref, f32[128,128]{1,0:T(8,128)S(1)} %copy-done.8, ...), custom_call_target="tpu_custom_call" | custom-call | tf_op jit(solution)/shard_map/first_backward/pallas_call | solution.py:547
  258.2 3.3 %all-to-all-start.12 = ((f32[4,72,128]{2,1,0:T(8,128)}), f32[4,72,128]{2,1,0:T(8,128)S(1)}, u32[]{:S(2)}, u32[]{:S(2)}) async-start(f32[4,72,128]{2,1,0:T(8,128)} %first_backward.1), calls=%async_computation.12 | async-start | bytes 294912 | tf_op jit(solution)/shard_map/all_to_all | solution.py:75
  261.5 4.8 %all-to-all-done.12 = f32[4,72,128]{2,1,0:T(8,128)S(1)} async-done(((f32[4,72,128]{2,1,0:T(8,128)}), f32[4,72,128]{2,1,0:T(8,128)S(1)}, u32[]{:S(2)}, u32[]{:S(2)}) %all-to-all-start.12) | async-done | bytes 147488 | tf_op jit(solution)/shard_map/all_to_all | solution.py:75
  266.4 6.7 %collective-permute-start.11 = (f32[72,128]{1,0:T(8,128)S(1)}, f32[72,128]{1,0:T(8,128)S(1)}, u32[]{:S(2)}, u32[]{:S(2)}) collective-permute-start(f32[72,128]{1,0:T(8,128)S(1)} %reduce_sum.19), channel_id=1, source_target_pairs={{0,2},{2,0},{1,3},{3,1},{4,6},{6,4},{5,7},{7,5},{8,10},{10,8},{9,1... | collective-permute-start | bytes 110600 | tf_op jit(solution)/shard_map/ppermute | solution.py:71
  273.2 0.7 copy.25
  273.9 0.1 collective-permute-done.11
  274.0 0.6 maximum_bitcast_fusion.1
  274.6 0.6 fusion
  (65 shorter events, 1.0 us)
Async XLA Ops:
  2.0 35.8 %copy-start = (bf16[152,1216]{1,0:T(8,128)(2,1)S(1)}, bf16[152,1216]{1,0:T(8,128)(2,1)}, u32[]{:S(2)}) copy-start(bf16[152,1216]{1,0:T(8,128)(2,1)} %w1_ref.1) | copy-start | bytes 1108996
  2.0 35.8 %copy-start.1 = (bf16[1216,152]{0,1:T(8,128)(2,1)S(1)}, bf16[1216,152]{0,1:T(8,128)(2,1)}, u32[]{:S(2)}) copy-start(bf16[1216,152]{0,1:T(8,128)(2,1)} %param.26) | copy-start | bytes 1108996
  40.9 61.6 %collective-permute-start.1 = (bf16[2,1216,2432]{2,1,0:T(8,128)(2,1)}, bf16[2,1216,2432]{2,1,0:T(8,128)(2,1)}, u32[]{:S(2)}, u32[]{:S(2)}) collective-permute-start(bf16[2,1216,2432]{2,1,0:T(8,128)(2,1)} %bitcast.59), channel_id=1, source_target_pairs={{0,2},{2,0},{1,3},{3,1},{4,6},{6,4},{5,7},{7,5},{8,10},{10,8},{9,1... | collective-permute-start | bytes 35487752 | tf_op jit(solution)/shard_map/ppermute | solution.py:71
  41.2 61.4 %collective-permute-start.2 = (bf16[2,1216,2432]{2,1,0:T(8,128)(2,1)}, bf16[2,1216,2432]{2,1,0:T(8,128)(2,1)}, u32[]{:S(2)}, u32[]{:S(2)}) collective-permute-start(bf16[2,1216,2432]{2,1,0:T(8,128)(2,1)} %own.1), channel_id=1, source_target_pairs={{0,2},{2,0},{1,3},{3,1},{4,6},{6,4},{5,7},{7,5},{8,10},{10,8},{9,1... | collective-permute-start | bytes 35487752 | tf_op jit(solution)/shard_map/ppermute | solution.py:71
  41.5 25.0 %all-to-all-start.1 = ((bf16[16,16,2560]{2,1,0:T(8,128)(2,1)}), bf16[16,16,2560]{2,1,0:T(8,128)(2,1)S(1)}, u32[]{:S(2)}, u32[]{:S(2)}) async-start(bf16[16,16,2560]{2,1,0:T(8,128)(2,1)} %bitcast.65), calls=%async_computation.1 | async-start | bytes 2621440 | tf_op jit(solution)/shard_map/all_to_all | solution.py:671
  45.2 21.3 %copy-start.15 = (s32[16]{0:T(128)S(1)}, s32[16]{0:T(128)}, u32[]{:S(2)}) copy-start(s32[16]{0:T(128)} %student_ref.1) | copy-start | bytes 196
  51.1 33.3 %copy-start.19 = (bf16[152,384]{1,0:T(8,128)(2,1)S(1)}, bf16[152,384]{1,0:T(8,128)(2,1)}, u32[]{:S(2)}) copy-start(bf16[152,384]{1,0:T(8,128)(2,1)} %get-tuple-element.91) | copy-start | bytes 350212
  51.1 33.3 %copy-start.4 = (bf16[1,256,64]{1,2,0:T(8,128)(2,1)S(1)}, bf16[1,256,64]{1,2,0:T(8,128)(2,1)}, u32[]{:S(2)}) copy-start(bf16[1,256,64]{1,2,0:T(8,128)(2,1)} %param.16) | copy-start | bytes 98308
  84.3 9.1 %copy-start.14 = (f32[2,304]{1,0:T(2,128)S(1)}, f32[2,304]{1,0:T(2,128)}, u32[]{:S(2)}) copy-start(f32[2,304]{1,0:T(2,128)} %out_own.1) | copy-start | bytes 7300
  84.3 6.6 %collective-permute-start.5 = (bf16[152,384]{1,0:T(8,128)(2,1)S(1)}, bf16[152,384]{1,0:T(8,128)(2,1)S(1)}, u32[]{:S(2)}, u32[]{:S(2)}) collective-permute-start(bf16[152,384]{1,0:T(8,128)(2,1)S(1)} %copy-done.19), channel_id=1, source_target_pairs={{0,1},{1,0},{2,3},{3,2},{4,5},{5,4},{6,7},{7,6},{8,9},{9,8},{10,11... | collective-permute-start | bytes 350216 | tf_op jit(solution)/shard_map/ppermute | solution.py:714
  87.0 15.7 %copy-start.9 = (bf16[1,256,64]{1,2,0:T(8,128)(2,1)S(1)}, bf16[1,256,64]{1,2,0:T(8,128)(2,1)}, u32[]{:S(2)}) copy-start(bf16[1,256,64]{1,2,0:T(8,128)(2,1)} %param.19) | copy-start | bytes 98308
  87.0 15.7 %copy-start.16 = (s32[16]{0:T(128)S(1)}, s32[16]{0:T(128)}, u32[]{:S(2)}) copy-start(s32[16]{0:T(128)} %teacher_ref.3) | copy-start | bytes 196
  87.0 3.8 %collective-permute-start = (f32[128,64]{1,0:T(8,128)S(1)}, f32[128,64]{1,0:T(8,128)S(1)}, u32[]{:S(2)}, u32[]{:S(2)}) collective-permute-start(f32[128,64]{1,0:T(8,128)S(1)} %get-tuple-element.73), channel_id=1, source_target_pairs={{0,2},{2,0},{1,3},{3,1},{4,6},{6,4},{5,7},{7,5},{8,10},{10,8},{9,1... | collective-permute-start | bytes 98312 | tf_op jit(solution)/shard_map/ppermute | solution.py:71
  91.0 8.3 %collective-permute-start.6 = (bf16[304,384]{1,0:T(8,128)(2,1)S(1)}, bf16[304,384]{1,0:T(8,128)(2,1)S(1)}, u32[]{:S(2)}, u32[]{:S(2)}) collective-permute-start(bf16[304,384]{1,0:T(8,128)(2,1)S(1)} %pad_maximum_fusion.3), channel_id=1, source_target_pairs={{0,64},{16,80},{32,96},{48,112},{64,0},{80,16},{96,32},{112,48},{1... | collective-permute-start | bytes 700424 | tf_op jit(solution)/shard_map/ppermute | solution.py:485
  92.8 9.9 %collective-permute-start.4 = (f32[72,1216]{1,0:T(8,128)S(1)}, f32[72,1216]{1,0:T(8,128)S(1)}, u32[]{:S(2)}, u32[]{:S(2)}) collective-permute-start(f32[72,1216]{1,0:T(8,128)S(1)} %get-tuple-element.77.mat_own), channel_id=1, source_target_pairs={{0,2},{2,0},{1,3},{3,1},{4,6},{6,4},{5,7},{7,5},{8,10},{10,8},{9,1... | collective-permute-start | bytes 1050632 | tf_op jit(solution)/shard_map/ppermute | solution.py:71
  93.4 6.7 %collective-permute-start.3 = (f32[2,304]{1,0:T(2,128)S(1)}, f32[2,304]{1,0:T(2,128)S(1)}, u32[]{:S(2)}, u32[]{:S(2)}) collective-permute-start(f32[2,304]{1,0:T(2,128)S(1)} %copy-done.14), channel_id=1, source_target_pairs={{0,2},{2,0},{1,3},{3,1},{4,6},{6,4},{5,7},{7,5},{8,10},{10,8},{9,1... | collective-permute-start | bytes 7304 | tf_op jit(solution)/shard_map/ppermute | solution.py:71
  94.2 8.3 %all-to-all-start.3 = ((f32[4,128,64]{1,2,0:T(8,128)}), f32[4,128,64]{1,2,0:T(8,128)S(1)}, u32[]{:S(2)}, u32[]{:S(2)}) async-start(f32[4,128,64]{1,2,0:T(8,128)} %broadcast_in_dim.39), calls=%async_computation.3 | async-start | bytes 262144 | tf_op jit(solution)/shard_map/all_to_all | solution.py:75
  110.7 0.6 copy-start.10
  111.3 0.6 copy-start.12
  111.9 10.6 %collective-permute-start.7 = (bf16[608,384]{1,0:T(8,128)(2,1)}, bf16[608,384]{1,0:T(8,128)(2,1)}, u32[]{:S(2)}, u32[]{:S(2)}) collective-permute-start(bf16[608,384]{1,0:T(8,128)(2,1)} %pad_maximum_fusion.2), channel_id=1, source_target_pairs={{0,16},{16,0},{32,48},{48,32},{64,80},{80,64},{96,112},{112,96},{1... | collective-permute-start | bytes 1400840 | tf_op jit(solution)/shard_map/ppermute | solution.py:485
  111.9 12.8 %all-to-all-start.4 = ((bf16[4,32,2432]{2,1,0:T(8,128)(2,1)}), bf16[4,32,2432]{2,1,0:T(8,128)(2,1)S(1)}, u32[]{:S(2)}, u32[]{:S(2)}) async-start(bf16[4,32,2432]{2,1,0:T(8,128)(2,1)} %bitcast.66), calls=%async_computation.4 | async-start | bytes 1245184 | tf_op jit(solution)/shard_map/all_to_all | solution.py:75
  126.2 26.1 %collective-permute-start.8 = (bf16[1216,384]{1,0:T(8,128)(2,1)}, bf16[1216,384]{1,0:T(8,128)(2,1)}, u32[]{:S(2)}, u32[]{:S(2)}) collective-permute-start(bf16[1216,384]{1,0:T(8,128)(2,1)} %pad_maximum_fusion.1), channel_id=1, source_target_pairs={{0,48},{16,32},{32,16},{48,0},{64,112},{80,96},{96,80},{112,64},{1... | collective-permute-start | bytes 2801672 | tf_op jit(solution)/shard_map/ppermute | solution.py:485
  148.8 10.9 %all-to-all-start.6 = ((bf16[4,32,2432]{2,1,0:T(8,128)(2,1)}), bf16[4,32,2432]{2,1,0:T(8,128)(2,1)S(1)}, u32[]{:S(2)}, u32[]{:S(2)}) async-start(bf16[4,32,2432]{2,1,0:T(8,128)(2,1)} %bitcast.67), calls=%async_computation.6 | async-start | bytes 1245184 | tf_op jit(solution)/shard_map/all_to_all | solution.py:75
  155.3 26.1 %copy-start.17 = (s32[1,2]{1,0:T(1,128)S(1)}, s32[1,2]{1,0:T(1,128)}, u32[]{:S(2)}) copy-start(s32[1,2]{1,0:T(1,128)} %param.20) | copy-start | bytes 28
  160.7 19.4 %collective-permute-start.9 = (bf16[2432,384]{1,0:T(8,128)(2,1)}, bf16[2432,384]{1,0:T(8,128)(2,1)S(1)}, u32[]{:S(2)}, u32[]{:S(2)}) collective-permute-start(bf16[2432,384]{1,0:T(8,128)(2,1)} %pad_maximum_fusion.own), channel_id=1, source_target_pairs={{0,2},{2,0},{1,3},{3,1},{4,6},{6,4},{5,7},{7,5},{8,10},{10,8},{9,1... | collective-permute-start | bytes 5603336 | tf_op jit(solution)/shard_map/ppermute | solution.py:71
  180.1 1.2 copy-start.18
  187.0 0.6 copy-start.5
  201.9 0.7 copy-start.2
  202.6 11.8 %all-to-all-start.9 = ((bf16[4,32,2432]{2,1,0:T(8,128)(2,1)}), bf16[4,32,2432]{2,1,0:T(8,128)(2,1)S(1)}, u32[]{:S(2)}, u32[]{:S(2)}) async-start(bf16[4,32,2432]{2,1,0:T(8,128)(2,1)} %get-tuple-element.100), calls=%async_computation.9 | async-start | bytes 1245184 | tf_op jit(solution)/shard_map/all_to_all | solution.py:75
  211.7 0.6 copy-start.7
  214.3 21.9 %copy-start.3 = (f32[32,2432]{1,0:T(8,128)S(1)}, f32[32,2432]{1,0:T(8,128)}, u32[]{:S(2)}) copy-start(f32[32,2432]{1,0:T(8,128)} %copy-done.2) | copy-start | bytes 933892
  236.2 4.9 %copy-start.13 = (bf16[128,64]{1,0:T(8,128)(2,1)S(1)}, bf16[128,64]{1,0:T(8,128)(2,1)}, u32[]{:S(2)}) copy-start(bf16[128,64]{1,0:T(8,128)(2,1)} %copy-done.12) | copy-start | bytes 49156
  236.2 12.3 %copy-start.6 = (f32[128,128]{1,0:T(8,128)S(1)}, f32[128,128]{1,0:T(8,128)}, u32[]{:S(2)}) copy-start(f32[128,128]{1,0:T(8,128)} %copy-done.5) | copy-start | bytes 196612
  236.2 12.3 %copy-start.8 = (f32[128,128]{1,0:T(8,128)S(1)}, f32[128,128]{1,0:T(8,128)}, u32[]{:S(2)}) copy-start(f32[128,128]{1,0:T(8,128)} %copy-done.7) | copy-start | bytes 196612
  236.2 12.3 %copy-start.11 = (bf16[128,64]{1,0:T(8,128)(2,1)S(1)}, bf16[128,64]{1,0:T(8,128)(2,1)}, u32[]{:S(2)}) copy-start(bf16[128,64]{1,0:T(8,128)(2,1)} %copy-done.10) | copy-start | bytes 49156
  237.6 10.9 %all-to-all-start.11 = ((bf16[4,32,2432]{2,1,0:T(8,128)(2,1)}), bf16[4,32,2432]{2,1,0:T(8,128)(2,1)S(1)}, u32[]{:S(2)}, u32[]{:S(2)}) async-start(bf16[4,32,2432]{2,1,0:T(8,128)(2,1)} %get-tuple-element.104), calls=%async_computation.11 | async-start | bytes 1245184 | tf_op jit(solution)/shard_map/all_to_all | solution.py:75
  241.1 20.5 %collective-permute-start.10 = (bf16[128,64]{1,0:T(8,128)(2,1)S(1)}, bf16[128,64]{1,0:T(8,128)(2,1)S(1)}, u32[]{:S(2)}, u32[]{:S(2)}) collective-permute-start(bf16[128,64]{1,0:T(8,128)(2,1)S(1)} %copy-done.13), channel_id=1, source_target_pairs={{0,2},{2,0},{1,3},{3,1},{4,6},{6,4},{5,7},{7,5},{8,10},{10,8},{9,1... | collective-permute-start | bytes 49160 | tf_op jit(solution)/shard_map/ppermute | solution.py:71
  258.2 8.2 %all-to-all-start.12 = ((f32[4,72,128]{2,1,0:T(8,128)}), f32[4,72,128]{2,1,0:T(8,128)S(1)}, u32[]{:S(2)}, u32[]{:S(2)}) async-start(f32[4,72,128]{2,1,0:T(8,128)} %first_backward.1), calls=%async_computation.12 | async-start | bytes 294912 | tf_op jit(solution)/shard_map/all_to_all | solution.py:75
  266.4 7.6 %collective-permute-start.11 = (f32[72,128]{1,0:T(8,128)S(1)}, f32[72,128]{1,0:T(8,128)S(1)}, u32[]{:S(2)}, u32[]{:S(2)}) collective-permute-start(f32[72,128]{1,0:T(8,128)S(1)} %reduce_sum.19), channel_id=1, source_target_pairs={{0,2},{2,0},{1,3},{3,1},{4,6},{6,4},{5,7},{7,5},{8,10},{10,8},{9,1... | collective-permute-start | bytes 110600 | tf_op jit(solution)/shard_map/ppermute | solution.py:71

commit v4 on v3

--- a/solution.py
+++ b/solution.py
@@ -92,6 +92,37 @@
 
 def matrices(layer, sources, target):
     return [(source.at[layer], target.at[side]) for side, source in enumerate(sources)]
+
+
+def halves(extent):
+    cut = extent // 2 // 128 * 128 + 128
+    return ((0, cut), (cut, extent - cut))
+
+
+def matrix_halves(layer, source, target, side):
+    return [
+        (source.at[layer, pl.ds(at, size)], target.at[side, pl.ds(at, size)])
+        for at, size in halves(target.shape[1])
+    ]
+
+
+def finish(total, stream, left, right_ref, last, out_ref, out, sems):
+    (first_at, first_size), (next_at, next_size) = halves(right_ref.shape[1])
+    stream.next()
+    total = total + dot(left[:, :first_size], right_ref[1, :first_size, :])
+    stream.next()
+    sends = []
+    for index, (at, size) in enumerate(halves(right_ref.shape[2])):
+        columns = slice(at, at + size)
+        part = total[:, columns] + dot(left[:, next_at:], right_ref[1, next_at:, columns])
+        out_ref[:, columns] = last(part, columns).astype(BF)
+        send = pltpu.make_async_copy(
+            out_ref.at[:, pl.ds(at, size)], out.at[:, pl.ds(at, size)], sems.at[index]
+        )
+        send.start()
+        sends.append(send)
+    for send in sends:
+        send.wait()
 
 
 def identity(extent):
@@ -177,7 +208,7 @@
     send.wait()
 
 
-def student_kernel(hidden, where_ref, x_ref, packed_ref, mat_ref, mine_ref, other_ref, all_ref):
+def student_kernel(hidden, x_ref, packed_ref, mat_ref, out_ref):
     cells, seq = x_ref.shape
     width = packed_ref.shape[0]
     lanes, wide = mat_ref.shape
@@ -205,11 +236,11 @@
     z = inverse * dot(dot(x, spread).astype(BF), mat_ref[:, :hidden]) + bias
     active = gelu_both(z)[0].astype(BF)
     high, low = split(dot_back(active, mat_ref[:, second_at : second_at + hidden]))
-    all_ref[...] = dot_back(high, spread) + dot_back(low, spread) + 0.125 * times(direct)
+    velocity = dot_back(high, spread) + dot_back(low, spread) + 0.125 * times(direct)
     half = seq // 2
-    core = where_ref[2]
-    mine_ref[...] = all_ref[pl.ds(pl.multiple_of(core * half, half), half), :]
-    other_ref[...] = all_ref[pl.ds(pl.multiple_of((1 - core) * half, half), half), :]
+    for target in range(out_ref.shape[0]):
+        at = target % 2 * half
+        out_ref[target] = velocity[at : at + half]
 
 
 def first_product_kernel(packed_ref, up, out_ref, vector_ref, up_ref, left_ref, sems):
@@ -252,7 +283,9 @@
 ):
     cells, seq = x_ref.shape
     half = seq // 2
-    stream = Stream(matrices(0, (own, sib), w_ref), sems)
+    stream = Stream(
+        matrices(0, (own,), w_ref) + matrix_halves(0, sib, w_ref, 1), sems
+    )
     sample = where_ref[0]
     sigma_s = student_ref[sample].astype(F32) * 0.25
     sigma_t = teacher_ref[sample].astype(F32) * 0.001
@@ -277,16 +310,12 @@
         active, slope = gelu_both(z)
         slope_ref[side] = slope.astype(BF)
         actives.append(active.astype(BF))
-    keep = pltpu.make_async_copy(slope_ref, slope_out, sems.at[2])
+    keep = pltpu.make_async_copy(slope_ref, slope_out, sems.at[3])
     keep.start()
     stream.next()
     y = dot(actives[0], w_ref[0])
-    stream.next()
-    y_ref[...] = (y + dot(actives[1], w_ref[1])).astype(BF)
-    send = pltpu.make_async_copy(y_ref, y_out, sems.at[3])
-    send.start()
+    finish(y, stream, actives[1], w_ref, lambda part, _: part, y_ref, y_out, sems.at[pl.ds(4, 2)])
     keep.wait()
-    send.wait()
 
 
 def forward_kernel(
@@ -294,7 +323,10 @@
     up_ref, down_ref, y_ref, slope_ref, sems
 ):
     stream = Stream(
-        matrices(1, (up_own, up_sib), up_ref) + matrices(1, (down_own, down_sib), down_ref), sems
+        matrices(1, (up_own, up_sib), up_ref)
+        + matrices(1, (down_own,), down_ref)
+        + matrix_halves(1, down_sib, down_ref, 1),
+        sems,
     )
     normed, _ = normalize(g_ref[...].astype(F32))
     u = (normed * (1.0 + vector_ref[4:5]) + vector_ref[3:4]).astype(BF)
@@ -304,16 +336,12 @@
         active, slope = gelu_both(dot_back(u, up_ref[side]))
         slope_ref[side] = slope.astype(BF)
         actives.append(active.astype(BF))
-    keep = pltpu.make_async_copy(slope_ref, slope_out, sems.at[4])
+    keep = pltpu.make_async_copy(slope_ref, slope_out, sems.at[5])
     keep.start()
     stream.next()
     y = dot(actives[0], down_ref[0])
-    stream.next()
-    y_ref[...] = (y + dot(actives[1], down_ref[1])).astype(BF)
-    send = pltpu.make_async_copy(y_ref, y_out, sems.at[5])
-    send.start()
+    finish(y, stream, actives[1], down_ref, lambda part, _: part, y_ref, y_out, sems.at[pl.ds(6, 2)])
     keep.wait()
-    send.wait()
 
 
 def backward_kernel(
@@ -323,8 +351,9 @@
     stream = Stream(
         [(slope, slope_ref)]
         + matrices(1, (down_own, down_sib), down_ref)
-        + matrices(1, (up_own, up_sib), up_ref)
-        + [(head, head_ref)],
+        + [(head, head_ref)]
+        + matrices(1, (up_own,), up_ref)
+        + matrix_halves(1, up_sib, up_ref, 1),
         sems,
     )
     dy = dy_ref[...]
@@ -334,14 +363,13 @@
         stream.next()
         dz.append((dot_back(dy, down_ref[side]) * slope_ref[side].astype(F32)).astype(BF))
     stream.next()
+    stream.next()
     du = dot(dz[0], up_ref[0])
-    stream.next()
-    du = du + dot(dz[1], up_ref[1])
-    stream.next()
-    out_ref[...] = (du * (1.0 + vector_ref[4:5]) + head_ref[...].astype(F32)).astype(BF)
-    send = pltpu.make_async_copy(out_ref, out, sems.at[6])
-    send.start()
-    send.wait()
+
+    def last(part, columns):
+        return part * (1.0 + vector_ref[4:5, columns]) + head_ref[:, columns].astype(F32)
+
+    finish(du, stream, dz[1], up_ref, last, out_ref, out, sems.at[pl.ds(7, 2)])
 
 
 def first_backward_kernel(
@@ -349,16 +377,20 @@
     out_ref, w_ref, slope_ref, all_ref, sems
 ):
     cells = x_ref.shape[1]
-    stream = Stream([(slope, slope_ref)] + matrices(0, (own, sib), w_ref), sems)
+    ranges = halves(w_ref.shape[1])
+    plan = matrix_halves(0, own, w_ref, 0) + matrix_halves(0, sib, w_ref, 1)
+    stream = Stream([(slope, slope_ref)] + plan, sems)
     dy = dy_ref[...]
     stream.next()
     total = None
     for side, mat_ref in enumerate((mat_own, mat_sib)):
         high, low = split(mat_ref[:cells])
-        stream.next()
-        dz = (dot_back(dy, w_ref[side]) * slope_ref[side].astype(F32)).astype(BF)
-        part = dot_back(dz, high) + dot_back(dz, low)
-        total = part if total is None else total + part
+        for at, size in ranges:
+            stream.next()
+            da = dot_back(dy, w_ref[side, at : at + size, :])
+            dz = (da * slope_ref[side, :, at : at + size].astype(F32)).astype(BF)
+            part = dot_back(dz, high[:, at : at + size]) + dot_back(dz, low[:, at : at + size])
+            total = part if total is None else total + part
     inverse = back_ref[:, cells : cells + 1]
     cross = inverse * jnp.sum(x_ref[...].astype(F32) * total, axis=1, keepdims=True) / dy.shape[1]
     rest = 1.0 - teacher_ref[where_ref[0]].astype(F32) * 0.001
@@ -445,6 +477,18 @@
         copy.wait()
 
 
+def output_kernel(parts_ref, grad_ref, score_ref):
+    cells = grad_ref.shape[0]
+    half = parts_ref.shape[2]
+    for core in range(2):
+        total = parts_ref[core]
+        for source in range(core + 2, parts_ref.shape[0], 2):
+            total = total + parts_ref[source]
+        columns = slice(core * half, (core + 1) * half)
+        grad_ref[:, columns] = total[:cells]
+        score_ref[:, columns] = total[cells : cells + score_ref.shape[0]]
+
+
 def first_middle_kernel(where_ref, parts_ref, g_ref, vector_ref, mine_ref, everyone, sems):
     rows = mine_ref.shape[0]
     before = g_ref[pl.ds(pl.multiple_of(where_ref[1] * rows, rows), rows), :].astype(F32)
@@ -486,42 +530,39 @@
     return jnp.concatenate([values, other], axis=0)
 
 
-def head_kernel(layer, pick_ref, where_ref, g_ref, out_own, out_sib, own, sib, back_out, score_ref, weight_ref, back_ref, use_ref, sems):
+def head_kernel(layer, pick_ref, where_ref, g_ref, out_own, out_sib, near, rest, back_out, score_ref, weight_ref, back_ref, use_ref, sems):
     blocks = 8
-    size = own.shape[0] // blocks
+    size = near.shape[0] * 2 // blocks
+    wide = near.shape[1] // 2
     plan = []
-    for side, source in enumerate((own, sib)):
-        for block in range(blocks):
-            row = pl.multiple_of(block_owner(where_ref[3], block) * size, size)
-            plan.append(
-                (source.at[pl.ds(block * size, size)], weight_ref.at[side, pl.ds(row, size)])
-            )
+    for block in range(blocks):
+        row = pl.multiple_of(block_owner(where_ref[3], block) * size, size)
+        source = near if block < blocks // 2 else rest
+        plan.append(
+            (source.at[pl.ds(block % (blocks // 2) * size, size)], weight_ref.at[pl.ds(row, size)])
+        )
     stream = Stream(plan, sems)
     use_ref[...] = jnp.zeros(use_ref.shape, F32)
     for side, outs in enumerate((out_own, out_sib)):
         for head in range(2):
             use = jnp.where(pick_ref[head] == layer, 1.0, 0.0)
-            use_ref[side, head : head + 1, : outs.shape[1]] = use * outs[head : head + 1, :]
+            use_ref[head : head + 1, side * wide : side * wide + outs.shape[1]] = (
+                use * outs[head : head + 1, :]
+            )
     normed, _ = normalize(g_ref[...].astype(F32))
     quantised = normed.astype(BF)
-    back = None
-    scores = None
-    for side in range(2):
-        for _ in range(blocks):
-            stream.next()
-        weight = weight_ref[side]
-        e = dot(quantised, weight)
-        sigm = 1.0 / (1.0 + jnp.exp(-e))
-        active = e * sigm
-        outs = use_ref[side]
-        slope = sigm * (1.0 + e * (1.0 - sigm))
-        part = dot_back((-(outs[0:1] + outs[1:2]) * slope).astype(BF), weight)
-        back = part if back is None else back + part
-        part = [jnp.sum(active * outs[head : head + 1], axis=1, keepdims=True) for head in range(2)]
-        scores = part if scores is None else [old + new for old, new in zip(scores, part)]
-    back_ref[...] = back.astype(BF)
-    send = pltpu.make_async_copy(back_ref, back_out, sems.at[2 * blocks])
+    for _ in plan:
+        stream.next()
+    weight = weight_ref[...]
+    e = dot(quantised, weight)
+    sigm = 1.0 / (1.0 + jnp.exp(-e))
+    active = e * sigm
+    outs = use_ref[...]
+    slope = sigm * (1.0 + e * (1.0 - sigm))
+    back_ref[...] = dot_back((-(outs[0:1] + outs[1:2]) * slope).astype(BF), weight).astype(BF)
+    send = pltpu.make_async_copy(back_ref, back_out, sems.at[blocks])
     send.start()
+    scores = [jnp.sum(active * outs[head : head + 1], axis=1, keepdims=True) for head in range(2)]
     lane = lax.broadcasted_iota(jnp.int32, score_ref.shape, 1)
     score_ref[...] = jnp.where(lane == 0, scores[0], 0.0) + jnp.where(lane == 1, scores[1], 0.0)
     send.wait()
@@ -645,7 +686,10 @@
     kinds = layers + STEPS
     mods = mods[:kinds, : 3 * columns].reshape(kinds * 3, columns).astype(BF)
     packed = jnp.concatenate([projections, mods.T], axis=1)
+    head_block = jnp.concatenate([head_block, sibling(head_block)], axis=1)
+    head_other = lax.ppermute(head_block, "grp", [(0, 1), (1, 0)])
     gathered = lax.all_gather(packed, TP, axis=0, tiled=False)
+    gathered, head_other = lax.optimization_barrier((gathered, head_other))
 
     gap = -hidden % 128
     both_wide = 2 * (hidden + gap)
@@ -669,6 +713,14 @@
     w1_sib = sibling(t_w1)
     d_w2_sib = sibling(d_w2)
     received = lax.all_to_all(parts.reshape(samples, piece, both_wide), SAMPLE, 0, 0)
+    head_block, head_other, _ = lax.optimization_barrier((head_block, head_other, parts))
+    head_pair = jnp.concatenate(
+        [
+            jnp.where(at_grp == 0, head_block, head_other),
+            jnp.where(at_grp == 0, head_other, head_block),
+        ],
+        axis=0,
+    )
 
     first_own, vectors = here(
         first_product_kernel,
@@ -700,28 +752,18 @@
     latent_in = noisy_latents[0].T
     noise = teacher_noise[0].T
     packed = gathered.reshape(width, -1)
-    half_out = array((half, cells), F32)
-    velocity, other = here(
+    velocity = here(
         functools.partial(student_kernel, hidden),
         "student",
-        (half_out, half_out),
-        (where, latent_in, packed, mine),
-        scalars=1,
-        scratch=(pltpu.VMEM((seq, cells), F32),),
-    )
-    velocity = velocity + sibling(other)
-    head_block, _ = lax.optimization_barrier((head_block, mine))
-    head_other = lax.ppermute(head_block, "grp", [(0, 1), (1, 0)])
-    head_other, _ = lax.optimization_barrier((head_other, velocity))
-    head_pair = jnp.concatenate(
-        [
-            jnp.where(at_grp == 0, head_block, head_other),
-            jnp.where(at_grp == 0, head_other, head_block),
-        ],
-        axis=0,
-    )
-    head_two = swap_fsdp(head_pair, 4)
-    velocity = swap_y(jnp.broadcast_to(velocity[None], (4,) + velocity.shape))
+        array((8, half, cells), F32),
+        (latent_in, packed, mine),
+    )
+    head_pair, _ = lax.optimization_barrier((head_pair, mine))
+    head_other = lax.ppermute(head_pair, "fsdp", [(at, at ^ 4) for at in range(8)])
+    velocity = lax.all_to_all(velocity, TP, 0, 0)
+    head_pair, head_other, _ = lax.optimization_barrier((head_pair, head_other, velocity))
+    head_two = jnp.concatenate([head_pair, head_other], axis=0)
+    head_four = swap_fsdp(head_two, 1)
 
     def both(values, axis):
         other = sibling(values)
@@ -765,7 +807,7 @@
             token_rows,
             inner,
             pltpu.VMEM((2, seq, cells), F32),
-            pltpu.SemaphoreType.DMA((4,)),
+            pltpu.SemaphoreType.DMA((6,)),
         ),
         limit=44,
     )
@@ -785,10 +827,8 @@
         far_out=(1,),
         scratch=(four,),
     )
-    head_two, _ = lax.optimization_barrier((head_two, y_0))
-    head_four = swap_fsdp(head_two, 1)
-    head_four, _ = lax.optimization_barrier((head_four, g_1_mine))
-    head_own = swap_fsdp(head_four, 3)
+    head_four, _ = lax.optimization_barrier((head_four, y_0))
+    head_rest = lax.ppermute(head_four, "fsdp", [(at, at ^ 3) for at in range(8)])
     g_1 = swap_y(g_1).reshape(half, width)
     y_1, slope_1 = here(
         forward_kernel,
@@ -797,7 +837,7 @@
         (g_1, vectors) + last,
         far=4,
         far_out=(0, 1),
-        scratch=(matrix, matrix, token_rows, inner, pltpu.SemaphoreType.DMA((6,))),
+        scratch=(matrix, matrix, token_rows, inner, pltpu.SemaphoreType.DMA((8,))),
         limit=44,
     )
     g_2_mine, g_2 = here(
@@ -808,8 +848,6 @@
         far_out=(1,),
         scratch=(four,),
     )
-    head_own, _ = lax.optimization_barrier((head_own, g_2_mine))
-    head_sib = sibling(head_own)
     g_2 = swap_y(g_2).reshape(half, width)
 
     def head(name, layer, g):
@@ -817,15 +855,15 @@
             functools.partial(head_kernel, layer),
             name,
             (tokens_out, array((half, 128), F32)),
-            (picks, where, g, d_w2, d_w2_sib, head_own, head_sib),
+            (picks, where, g, d_w2, d_w2_sib, head_four, head_rest),
             scalars=2,
             far=2,
             far_out=(0,),
             scratch=(
-                pltpu.VMEM((2,) + head_own.shape, BF),
+                pltpu.VMEM((width, 2 * head_wide), BF),
                 token_rows,
-                pltpu.VMEM((2, 8, head_own.shape[1]), F32),
-                pltpu.SemaphoreType.DMA((17,)),
+                pltpu.VMEM((8, 2 * head_wide), F32),
+                pltpu.SemaphoreType.DMA((9,)),
             ),
         )
 
@@ -849,7 +887,7 @@
         (swap_y(dy_1).reshape(half, width), vectors, slope_1, head_back_1) + last,
         far=6,
         far_out=(0,),
-        scratch=(matrix, matrix, inner, token_rows, token_rows, pltpu.SemaphoreType.DMA((7,))),
+        scratch=(matrix, matrix, inner, token_rows, token_rows, pltpu.SemaphoreType.DMA((9,))),
         limit=44,
     )
     direct, dy_0 = here(
@@ -860,14 +898,15 @@
         far_out=(1,),
         scratch=(quarter_rows, four),
     )
+    dy_0, latents = lax.optimization_barrier((swap_y(dy_0).reshape(half, width), latents))
     final = here(
         first_backward_kernel,
         "first_backward",
-        array((4, cells + 8, half), F32),
+        array((8, cells + 8, half), F32),
         (
             where,
             teacher_step,
-            swap_y(dy_0).reshape(half, width),
+            dy_0,
             noised,
             back_0,
             scores_1,
@@ -881,11 +920,16 @@
         ),
         scalars=2,
         far=3,
-        scratch=(matrix, inner, pltpu.VMEM((half, 2 * cells), F32), pltpu.SemaphoreType.DMA((3,))),
+        scratch=(matrix, inner, pltpu.VMEM((half, 2 * cells), F32), pltpu.SemaphoreType.DMA((5,))),
         limit=44,
     )
-    final = both(jnp.sum(swap_y(final), axis=0), 1)
-    return (latents[None], final[cells : cells + heads][None], final[:cells].T[None])
+    grad, scores = here(
+        output_kernel,
+        "output",
+        (array((cells, seq), F32), array((heads, seq), F32)),
+        (lax.all_to_all(final, TP, 0, 0),),
+    )
+    return (latents[None], scores[None], grad.T[None])
 
 
 def solution(mesh):

time: 276 us -> 271 us (0.982)
  blocking collectives: 97.2 us -> 74.4 us
  waiting for transfers between devices: 41.6 us -> 51.9 us
  starting transfers between devices: 48.3 us -> 56.8 us
    all_to_all x0 -> x3, starting transfers between devices: none -> 23.5 us  [the longest x1 10.6 us: body(): lax.all_to_all(final, TP, 0, 0)]
    all_to_all x0 -> x3, waiting for transfers between devices: none -> 19.4 us  [the longest x1 9.44 us: body(): mine = lax.all_to_all(chosen.reshape(samples, 8, both_wide), SAMPLE, 0, 0)]
    all_to_all x2 -> x1, blocking collectives: 32 us -> 13.4 us  [body(): velocity = lax.all_to_all(velocity, TP, 0, 0)]
    ppermute x8 -> x6, starting transfers between devices: 21.1 us -> 12.2 us  [sibling(): return lax.ppermute(values, 'core', [(0, 1), (1, 0)])]
    all_to_all x6 -> x4, waiting for transfers between devices: 16.4 us -> 8.34 us  [swap_y(): return lax.all_to_all(values, 'y', 0, 0)]
    all_to_all x6 -> x4, starting transfers between devices: 20.8 us -> 14.1 us  [swap_y(): return lax.all_to_all(values, 'y', 0, 0)]
    all_to_all x4, blocking collectives: 48.7 us -> 44.5 us  [swap_y(): return lax.all_to_all(values, 'y', 0, 0)]
    concatenate x3 -> x1, other arithmetic: 6 us -> 2.88 us  [swap_fsdp(): return jnp.concatenate([values, other], axis=0)]
  transfers between devices with their start and end apart: 19 -> 18, of which waited for: 10 -> 10; matrix products, arithmetic and copies ran while one was open for 3% -> 4% of each run, Pallas kernels for 13% -> 14%
where the time goes in v4:
time: 271 us; the launch traced here: 270 us
  blocking collectives  74.4 us (27%)
  Pallas kernels  71.6 us (26%)
  starting transfers between devices  56.8 us (21%)
  waiting for transfers between devices  51.9 us (19%)
  other arithmetic  8.27 us (3%)
  local copies, waits for them, and re-layouts  5.65 us (2%)
    pallas_call x16, Pallas kernels, here(): pl.pallas_call(kernel, name=name, out_shape=shapes if many else shapes[0]...  71.6 us
    all_to_all x4, blocking collectives, swap_y(): return lax.all_to_all(values, 'y', 0, 0)  44.5 us
    all_gather x1, blocking collectives, body(): gathered = lax.all_gather(packed, TP, axis=0, tiled=False)  16.5 us
    all_to_all x1, waiting for transfers between devices, body(): lax.all_to_all(parts.reshape(samples, piece, both_wide), SAMPLE, 0, 0)  15.5 us
    all_to_all x4, starting transfers between devices, swap_y(): return lax.all_to_all(values, 'y', 0, 0)  14.1 us
    all_to_all x1, blocking collectives, body(): velocity = lax.all_to_all(velocity, TP, 0, 0)  13.4 us
    ppermute x6, starting transfers between devices, sibling(): return lax.ppermute(values, 'core', [(0, 1), (1, 0)])  12.2 us
    all_to_all x1, starting transfers between devices, body(): lax.all_to_all(final, TP, 0, 0)  10.6 us
  transfers between devices with their start and end apart: 18, of which 10 were waited for; matrix products, arithmetic and copies ran while one was open for 4% of the time, Pallas kernels for 14%

profile of v4, /device:TPU:1, one launch (start us, length us, event | category | flops | bytes accessed | tf_op | source)
XLA Modules:
  0.0 270.0 jit_solution(8746831633720355961)
XLA Ops:
  0.8 0.7 convert_element_type.29
  1.6 0.2 fusion.1.cond_t_ref
  2.0 2.6 modulation.1
  4.7 8.6 %all-to-all-start = ((bf16[16,8,1024]{2,1,0:T(8,128)(2,1)}), bf16[16,8,1024]{2,1,0:T(8,128)(2,1)S(1)}, u32[]{:S(2)}, u32[]{:S(2)}) async-start(bf16[16,8,1024]{2,1,0:T(8,128)(2,1)} %bitcast.67), calls=%async_computation | async-start | bytes 524288 | tf_op jit(solution)/shard_map/all_to_all | solution.py:685
  13.3 1.0 collective-permute-start
  14.3 0.9 constant_dynamic-update-slice_fusion.1
  15.2 0.3 collective-permute-done
  15.5 1.6 collective-permute-start.1
  17.2 3.8 %all-to-all-done = bf16[16,8,1024]{2,1,0:T(8,128)(2,1)S(1)} async-done(((bf16[16,8,1024]{2,1,0:T(8,128)(2,1)}), bf16[16,8,1024]{2,1,0:T(8,128)(2,1)S(1)}, u32[]{:S(2)}, u32[]{:S(2)}) %all-to-all-start) | async-done | bytes 262176 | tf_op jit(solution)/shard_map/all_to_all | solution.py:685
  21.4 16.5 %all-gather = bf16[2432,210]{1,0:T(8,128)(2,1)S(1)} all-gather(bf16[304,210]{1,0:T(8,128)(2,1)S(1)} %pad_maximum_fusion.3), channel_id=2, replica_groups=mesh['fsdp'=8,'y'=4,'core'=2,'grp'=2] {'y','core'}, dimensions={0}, use_global_device_ids=true | all-gather | bytes 1149120 | tf_op jit(solution)/shard_map/all_gather | solution.py:691
  37.9 3.1 %product.1 = (bf16[256,2560]{1,0:T(8,128)(2,1)}, bf16[8,1216]{1,0:T(8,128)(2,1)S(1)}) custom-call(s32[8]{0:T(128)S(1)} %stack.55.at_ref, bf16[8,304,210]{2,1,0:T(8,128)(2,1)S(1)} %bitcast.42, bf16[152,1216]{1,0:T(8,128)(2,1)S(1)} %copy-done, bf16[152,1216]{1,0:T(8,128)(2,1)S(1)} %bitcast.50), custom_call_target="tpu_custom_call" | custom-call | tf_op jit(solution)/shard_map/product/pallas_call | solution.py:588
  41.1 0.2 collective-permute-start.2
  41.3 0.4 collective-permute-start.3
  41.7 3.7 %all-to-all-start.1 = ((bf16[16,16,2560]{2,1,0:T(8,128)(2,1)}), bf16[16,16,2560]{2,1,0:T(8,128)(2,1)S(1)}, u32[]{:S(2)}, u32[]{:S(2)}) async-start(bf16[16,16,2560]{2,1,0:T(8,128)(2,1)} %bitcast.62), calls=%async_computation.1 | async-start | bytes 2621440 | tf_op jit(solution)/shard_map/all_to_all | solution.py:715
  45.4 5.8 %first_product.1 = (f32[72,1216]{1,0:T(8,128)S(1)}, f32[8,2432]{1,0:T(8,128)S(1)}) custom-call(bf16[8,304,210]{2,1,0:T(8,128)(2,1)S(1)} %bitcast.43, bf16[2,1216,2432]{2,1,0:T(8,128)(2,1)} %bitcast.57), custom_call_target="tpu_custom_call" | custom-call | tf_op jit(solution)/shard_map/first_product/pallas_call | solution.py:588
  51.2 15.5 %all-to-all-done.1.parts_ref = bf16[16,16,2560]{2,1,0:T(8,128)(2,1)S(1)} async-done(((bf16[16,16,2560]{2,1,0:T(8,128)(2,1)}), bf16[16,16,2560]{2,1,0:T(8,128)(2,1)S(1)}, u32[]{:S(2)}, u32[]{:S(2)}) %all-to-all-start.1) | async-done | bytes 1310752 | tf_op jit(solution)/shard_map/all_to_all | solution.py:715
  66.7 1.9 select.4
  68.6 4.2 %all-to-all-start.2 = ((bf16[16,8,2560]{2,1,0:T(8,128)(2,1)}), bf16[16,8,2560]{2,1,0:T(8,128)(2,1)S(1)}, u32[]{:S(2)}, u32[]{:S(2)}) async-start(bf16[16,8,2560]{2,1,0:T(8,128)(2,1)} %bitcast.60), calls=%async_computation.2 | async-start | bytes 1310720 | tf_op jit(solution)/shard_map/all_to_all | solution.py:749
  72.9 1.1 broadcast_select_fusion.1
  74.0 0.8 pad_maximum_fusion.2
  74.8 9.4 %all-to-all-done.2 = bf16[16,8,2560]{2,1,0:T(8,128)(2,1)S(1)} async-done(((bf16[16,8,2560]{2,1,0:T(8,128)(2,1)}), bf16[16,8,2560]{2,1,0:T(8,128)(2,1)S(1)}, u32[]{:S(2)}, u32[]{:S(2)}) %all-to-all-start.2) | async-done | bytes 655392 | tf_op jit(solution)/shard_map/all_to_all | solution.py:749
  84.2 0.4 collective-permute-start.6
  84.7 2.1 student.1
  86.8 0.2 copy.23
  87.0 13.4 %all_to_all.65 = f32[8,128,64]{1,2,0:T(8,128)S(1)} all-to-all(f32[8,128,64]{1,2,0:T(8,128)S(1)} %copy.23), channel_id=1, replica_groups=mesh['fsdp'=8,'y'=4,'core'=2,'grp'=2] {'y','core'}, dimensions={0} | all-to-all | bytes 524288 | tf_op jit(solution)/shard_map/all_to_all | solution.py:763
  100.4 2.2 pad_maximum_fusion.1
  102.6 1.1 collective-permute-start.5
  103.7 0.2 collective-permute-start.4
  103.9 1.1 collective-permute-done.4.out_sib
  105.0 0.2 copy.24.velocity_ref
  105.3 7.6 %first_forward.1 = (bf16[128,2432]{1,0:T(8,128)(2,1)}, bf16[2,128,1216]{2,1,0:T(8,128)(2,1)}, bf16[128,64]{1,0:T(8,128)(2,1)S(1)}, bf16[128,64]{1,0:T(8,128)(2,1...) custom-call(s32[4]{0:T(128)S(1)} %pad_add_fusion.where_ref, s32[16]{0:T(128)S(1)} %copy-done.18, ...), custom_call_target="tpu_custom_call" | custom-call | tf_op jit(solution)/shard_map/first_forward/pallas_call | solution.py:588
  112.9 0.6 copy-done.7
  113.6 0.6 copy-done.14
  114.2 3.5 %all-to-all-start.4 = ((bf16[4,32,2432]{2,1,0:T(8,128)(2,1)}), bf16[4,32,2432]{2,1,0:T(8,128)(2,1)S(1)}, u32[]{:S(2)}, u32[]{:S(2)}) async-start(bf16[4,32,2432]{2,1,0:T(8,128)(2,1)} %bitcast.63), calls=%async_computation.4 | async-start | bytes 1245184 | tf_op jit(solution)/shard_map/all_to_all | solution.py:75
  117.7 6.4 %collective-permute-done.7 = bf16[608,768]{1,0:T(8,128)(2,1)} collective-permute-done((bf16[608,768]{1,0:T(8,128)(2,1)}, bf16[608,768]{1,0:T(8,128)(2,1)}, u32[]{:S(2)}, u32[]{:S(2)}) %collective-permute-start.7) | collective-permute-done | bytes 933920 | tf_op jit(solution)/shard_map/ppermute | solution.py:529
  124.1 2.9 %pad_maximum_fusion.near = bf16[1216,768]{1,0:T(8,128)(2,1)} fusion(bf16[608,768]{1,0:T(8,128)(2,1)} %collective-permute-done.7, bf16[304,768]{1,0:T(8,128)(2,1)} %collective-permute-done.6, bf16[304,768]{1,0:T(8,128)(2,1)} %pad_maximum_fusion.2), kind=kLoop, calls=%fused_computation | loop fusion | flops 5603328 | bytes 3735552 | tf_op jit(solution)/shard_map/concatenate | solution.py:530
  127.0 1.3 collective-permute-start.8
  128.2 1.5 first_middle.1
  129.8 11.8 %all_to_all.66 = bf16[4,32,2432]{2,1,0:T(8,128)(2,1)S(1)} all-to-all(bf16[4,32,2432]{2,1,0:T(8,128)(2,1)} %get-tuple-element.88), channel_id=1, replica_groups=mesh['fsdp'=8,'y'=4,'core'=2,'grp'=2] {'y'}, dimensions={0} | all-to-all | bytes 1245184 | tf_op jit(solution)/shard_map/all_to_all | solution.py:75
  141.5 11.0 %forward.1 = (bf16[128,2432]{1,0:T(8,128)(2,1)}, bf16[2,128,1216]{2,1,0:T(8,128)(2,1)}) custom-call(bf16[128,2432]{1,0:T(8,128)(2,1)S(1)} %bitcast.44, f32[8,2432]{1,0:T(8,128)S(1)} %get-tuple-element.87.vector_ref, bf16[2,1216,2432]{2,1,0:T(8,128)(2,1)} %bitcast.58, bf16[2,1216,2432]{2,1,0:T(8,128)(2,1)} %collective-permute-done.2.up_sib, ...), custom_call_target="tpu_custom_call" | custom-call | tf_op jit(solution)/shard_map/forward/pallas_call | solution.py:588
  152.5 10.9 %all_to_all.67.parts_ref = bf16[4,32,2432]{2,1,0:T(8,128)(2,1)S(1)} all-to-all(bf16[4,32,2432]{2,1,0:T(8,128)(2,1)} %bitcast.65), channel_id=1, replica_groups=mesh['fsdp'=8,'y'=4,'core'=2,'grp'=2] {'y'}, dimensions={0} | all-to-all | bytes 1245184 | tf_op jit(solution)/shard_map/all_to_all | solution.py:75
  163.4 1.1 last_middle.1
  164.5 0.6 copy-done.4
  165.2 3.7 %all-to-all-start.7 = ((bf16[4,32,2432]{2,1,0:T(8,128)(2,1)}), bf16[4,32,2432]{2,1,0:T(8,128)(2,1)S(1)}, u32[]{:S(2)}, u32[]{:S(2)}) async-start(bf16[4,32,2432]{2,1,0:T(8,128)(2,1)} %get-tuple-element.92), calls=%async_computation.7 | async-start | bytes 1245184 | tf_op jit(solution)/shard_map/all_to_all | solution.py:75
  168.9 7.2 %all-to-all-done.7 = bf16[4,32,2432]{2,1,0:T(8,128)(2,1)S(1)} async-done(((bf16[4,32,2432]{2,1,0:T(8,128)(2,1)}), bf16[4,32,2432]{2,1,0:T(8,128)(2,1)S(1)}, u32[]{:S(2)}, u32[]{:S(2)}) %all-to-all-start.7) | async-done | bytes 622624 | tf_op jit(solution)/shard_map/all_to_all | solution.py:75
  176.1 5.7 %head_last.1 = (bf16[128,2432]{1,0:T(8,128)(2,1)}, f32[128,128]{1,0:T(8,128)S(1)}) custom-call(s32[2]{0:T(128)S(1)} %bitcast.54, s32[4]{0:T(128)S(1)} %pad_add_fusion.where_ref, bf16[128,2432]{1,0:T(8,128)(2,1)S(1)} %bitcast.49, f32[2,304]{1,0:T(2,128)S(1)} %copy-done.16, f32[2,304]{1,0:T(2,128)S(1)} %collective-permute-done.4.out_sib, ...), custom_call_target="tpu_custom_call" | custom-call | tf_op jit(solution)/shard_map/head_last/pallas_call | solution.py:588
  181.8 10.9 %all_to_all.68.parts_ref = bf16[4,32,2432]{2,1,0:T(8,128)(2,1)S(1)} all-to-all(bf16[4,32,2432]{2,1,0:T(8,128)(2,1)} %bitcast.64), channel_id=1, replica_groups=mesh['fsdp'=8,'y'=4,'core'=2,'grp'=2] {'y'}, dimensions={0} | all-to-all | bytes 1245184 | tf_op jit(solution)/shard_map/all_to_all | solution.py:75
  192.7 1.2 last_back.1
  193.9 0.7 copy-done.2
  194.6 3.5 %all-to-all-start.9 = ((bf16[4,32,2432]{2,1,0:T(8,128)(2,1)}), bf16[4,32,2432]{2,1,0:T(8,128)(2,1)S(1)}, u32[]{:S(2)}, u32[]{:S(2)}) async-start(bf16[4,32,2432]{2,1,0:T(8,128)(2,1)} %get-tuple-element.103), calls=%async_computation.9 | async-start | bytes 1245184 | tf_op jit(solution)/shard_map/all_to_all | solution.py:75
  198.1 5.7 %head_first.1 = (bf16[128,2432]{1,0:T(8,128)(2,1)}, f32[128,128]{1,0:T(8,128)S(1)}) custom-call(s32[2]{0:T(128)S(1)} %bitcast.55, s32[4]{0:T(128)S(1)} %pad_add_fusion.where_ref, bf16[128,2432]{1,0:T(8,128)(2,1)S(1)} %bitcast.45, f32[2,304]{1,0:T(2,128)S(1)} %copy-done.16, f32[2,304]{1,0:T(2,128)S(1)} %collective-permute-done.4.out_sib, ...), custom_call_target="tpu_custom_call" | custom-call | tf_op jit(solution)/shard_map/head_first/pallas_call | solution.py:588
  203.8 0.6 copy-done.9
  204.4 1.1 all-to-all-done.9
  205.6 10.9 %backward.1 = bf16[128,2432]{1,0:T(8,128)(2,1)} custom-call(bf16[128,2432]{1,0:T(8,128)(2,1)S(1)} %bitcast.47, f32[8,2432]{1,0:T(8,128)S(1)} %get-tuple-element.87.vector_ref, bf16[2,128,1216]{2,1,0:T(8,128)(2,1)} %get-tuple-element.104.slope, bf16[128,2432]{1,0:T(8,128)(2,1)} %get-tuple-element.108.head, bf16[2,1216,2432]{2,1,0:T(8,128)(2,1)} %bitcast.59, ...), custom_call_target="tpu_custom_call" | custom-call | tf_op jit(solution)/shard_map/backward/pallas_call | solution.py:588
  216.4 10.9 %all_to_all.69.parts_ref = bf16[4,32,2432]{2,1,0:T(8,128)(2,1)S(1)} all-to-all(bf16[4,32,2432]{2,1,0:T(8,128)(2,1)} %bitcast.61), channel_id=1, replica_groups=mesh['fsdp'=8,'y'=4,'core'=2,'grp'=2] {'y'}, dimensions={0} | all-to-all | bytes 1245184 | tf_op jit(solution)/shard_map/all_to_all | solution.py:75
  227.4 1.4 first_back.1
  228.7 3.5 %all-to-all-start.11 = ((bf16[4,32,2432]{2,1,0:T(8,128)(2,1)}), bf16[4,32,2432]{2,1,0:T(8,128)(2,1)S(1)}, u32[]{:S(2)}, u32[]{:S(2)}) async-start(bf16[4,32,2432]{2,1,0:T(8,128)(2,1)} %get-tuple-element.109), calls=%async_computation.11 | async-start | bytes 1245184 | tf_op jit(solution)/shard_map/all_to_all | solution.py:75
  232.2 9.3 %collective-permute-start.9 = (bf16[128,64]{1,0:T(8,128)(2,1)S(1)}, bf16[128,64]{1,0:T(8,128)(2,1)S(1)}, u32[]{:S(2)}, u32[]{:S(2)}) collective-permute-start(bf16[128,64]{1,0:T(8,128)(2,1)S(1)} %copy-done.15), channel_id=1, source_target_pairs={{0,2},{2,0},{1,3},{3,1},{4,6},{6,4},{5,7},{7,5},{8,10},{10,8},{9,1... | collective-permute-start | bytes 49160 | tf_op jit(solution)/shard_map/ppermute | solution.py:71
  241.5 0.9 collective-permute-done.9
  242.4 9.5 %first_backward.1 = f32[8,72,128]{2,1,0:T(8,128)} custom-call(s32[4]{0:T(128)S(1)} %pad_add_fusion.where_ref, s32[16]{0:T(128)S(1)} %copy-done.17, bf16[128,2432]{1,0:T(8,128)(2,1)S(1)} %bitcast.48, bf16[128,64]{1,0:T(8,128)(2,1)S(1)} %copy-done.13, f32[128,128]{1,0:T(8,128)S(1)} %copy-done.8, f32[128,128]{1,0:T(8,128)S(1)} %copy-done.10, ...), custom_call_target="tpu_custom_call" | custom-call | tf_op jit(solution)/shard_map/first_backward/pallas_call | solution.py:588
  251.9 10.6 %all-to-all-start.12 = ((f32[8,72,128]{2,1,0:T(8,128)}), f32[8,72,128]{2,1,0:T(8,128)S(1)}, u32[]{:S(2)}, u32[]{:S(2)}) async-start(f32[8,72,128]{2,1,0:T(8,128)} %first_backward.1), calls=%async_computation.12 | async-start | bytes 589824 | tf_op jit(solution)/shard_map/all_to_all | solution.py:930
  262.6 0.7 copy.25
  263.3 6.1 %all-to-all-done.12.parts_ref = f32[8,72,128]{2,1,0:T(8,128)S(1)} async-done(((f32[8,72,128]{2,1,0:T(8,128)}), f32[8,72,128]{2,1,0:T(8,128)S(1)}, u32[]{:S(2)}, u32[]{:S(2)}) %all-to-all-start.12) | async-done | bytes 294944 | tf_op jit(solution)/shard_map/all_to_all | solution.py:930
  269.4 0.6 output.1
  (62 shorter events, 0.9 us)
Async XLA Ops:
  4.7 33.3 %copy-start = (bf16[152,1216]{1,0:T(8,128)(2,1)S(1)}, bf16[152,1216]{1,0:T(8,128)(2,1)}, u32[]{:S(2)}) copy-start(bf16[152,1216]{1,0:T(8,128)(2,1)} %w1_ref.1) | copy-start | bytes 1108996
  4.7 33.2 %copy-start.1 = (bf16[1216,152]{0,1:T(8,128)(2,1)S(1)}, bf16[1216,152]{0,1:T(8,128)(2,1)}, u32[]{:S(2)}) copy-start(bf16[1216,152]{0,1:T(8,128)(2,1)} %param.26) | copy-start | bytes 1108996
  4.7 16.3 %all-to-all-start = ((bf16[16,8,1024]{2,1,0:T(8,128)(2,1)}), bf16[16,8,1024]{2,1,0:T(8,128)(2,1)S(1)}, u32[]{:S(2)}, u32[]{:S(2)}) async-start(bf16[16,8,1024]{2,1,0:T(8,128)(2,1)} %bitcast.67), calls=%async_computation | async-start | bytes 524288 | tf_op jit(solution)/shard_map/all_to_all | solution.py:685
  13.3 2.2 collective-permute-start
  15.5 25.5 %copy-start.20 = (bf16[152,768]{1,0:T(8,128)(2,1)}, bf16[152,768]{1,0:T(8,128)(2,1)S(1)}, u32[]{:S(2)}) copy-start(bf16[152,768]{1,0:T(8,128)(2,1)S(1)} %constant_dynamic-update-slice_fusion) | copy-start | bytes 700420
  15.5 22.4 %collective-permute-start.1 = (bf16[152,768]{1,0:T(8,128)(2,1)S(1)}, bf16[152,768]{1,0:T(8,128)(2,1)S(1)}, u32[]{:S(2)}, u32[]{:S(2)}) collective-permute-start(bf16[152,768]{1,0:T(8,128)(2,1)S(1)} %constant_dynamic-update-slice_fusion), channel_id=1, source_target_pairs={{0,1},{1,0},{2,3},{3,2},{4,5},{5,4},{6,7},{7,6},{8,9},{9,8},{10,11... | collective-permute-start | bytes 700424 | tf_op jit(solution)/shard_map/ppermute | solution.py:690
  37.9 3.7 %copy-start.21 = (bf16[152,768]{1,0:T(8,128)(2,1)}, bf16[152,768]{1,0:T(8,128)(2,1)S(1)}, u32[]{:S(2)}) copy-start(bf16[152,768]{1,0:T(8,128)(2,1)S(1)} %collective-permute-done.1) | copy-start | bytes 700420
  41.1 64.0 %collective-permute-start.2 = (bf16[2,1216,2432]{2,1,0:T(8,128)(2,1)}, bf16[2,1216,2432]{2,1,0:T(8,128)(2,1)}, u32[]{:S(2)}, u32[]{:S(2)}) collective-permute-start(bf16[2,1216,2432]{2,1,0:T(8,128)(2,1)} %bitcast.56), channel_id=1, source_target_pairs={{0,2},{2,0},{1,3},{3,1},{4,6},{6,4},{5,7},{7,5},{8,10},{10,8},{9,1... | collective-permute-start | bytes 35487752 | tf_op jit(solution)/shard_map/ppermute | solution.py:71
  41.3 63.8 %collective-permute-start.3 = (bf16[2,1216,2432]{2,1,0:T(8,128)(2,1)}, bf16[2,1216,2432]{2,1,0:T(8,128)(2,1)}, u32[]{:S(2)}, u32[]{:S(2)}) collective-permute-start(bf16[2,1216,2432]{2,1,0:T(8,128)(2,1)} %own.1), channel_id=1, source_target_pairs={{0,2},{2,0},{1,3},{3,1},{4,6},{6,4},{5,7},{7,5},{8,10},{10,8},{9,1... | collective-permute-start | bytes 35487752 | tf_op jit(solution)/shard_map/ppermute | solution.py:71
  41.7 25.0 %all-to-all-start.1 = ((bf16[16,16,2560]{2,1,0:T(8,128)(2,1)}), bf16[16,16,2560]{2,1,0:T(8,128)(2,1)S(1)}, u32[]{:S(2)}, u32[]{:S(2)}) async-start(bf16[16,16,2560]{2,1,0:T(8,128)(2,1)} %bitcast.62), calls=%async_computation.1 | async-start | bytes 2621440 | tf_op jit(solution)/shard_map/all_to_all | solution.py:715
  45.4 21.3 %copy-start.18 = (s32[16]{0:T(128)S(1)}, s32[16]{0:T(128)}, u32[]{:S(2)}) copy-start(s32[16]{0:T(128)} %student_ref.1) | copy-start | bytes 196
  68.6 16.1 %copy-start.6 = (bf16[1,256,64]{1,2,0:T(8,128)(2,1)S(1)}, bf16[1,256,64]{1,2,0:T(8,128)(2,1)}, u32[]{:S(2)}) copy-start(bf16[1,256,64]{1,2,0:T(8,128)(2,1)} %param.16) | copy-start | bytes 98308
  68.6 15.6 %all-to-all-start.2 = ((bf16[16,8,2560]{2,1,0:T(8,128)(2,1)}), bf16[16,8,2560]{2,1,0:T(8,128)(2,1)S(1)}, u32[]{:S(2)}, u32[]{:S(2)}) async-start(bf16[16,8,2560]{2,1,0:T(8,128)(2,1)} %bitcast.60), calls=%async_computation.2 | async-start | bytes 1310720 | tf_op jit(solution)/shard_map/all_to_all | solution.py:749
  84.2 16.1 %collective-permute-start.6 = (bf16[304,768]{1,0:T(8,128)(2,1)}, bf16[304,768]{1,0:T(8,128)(2,1)}, u32[]{:S(2)}, u32[]{:S(2)}) collective-permute-start(bf16[304,768]{1,0:T(8,128)(2,1)} %pad_maximum_fusion.2), channel_id=1, source_target_pairs={{0,64},{16,80},{32,96},{48,112},{64,0},{80,16},{96,32},{112,48},{1... | collective-permute-start | bytes 1400840 | tf_op jit(solution)/shard_map/ppermute | solution.py:762
  86.8 16.9 %copy-start.16 = (f32[2,304]{1,0:T(2,128)S(1)}, f32[2,304]{1,0:T(2,128)}, u32[]{:S(2)}) copy-start(f32[2,304]{1,0:T(2,128)} %out_own.1) | copy-start | bytes 7300
  86.8 18.5 %copy-start.11 = (bf16[1,256,64]{1,2,0:T(8,128)(2,1)S(1)}, bf16[1,256,64]{1,2,0:T(8,128)(2,1)}, u32[]{:S(2)}) copy-start(bf16[1,256,64]{1,2,0:T(8,128)(2,1)} %param.19) | copy-start | bytes 98308
  86.8 18.5 %copy-start.17 = (s32[16]{0:T(128)S(1)}, s32[16]{0:T(128)}, u32[]{:S(2)}) copy-start(s32[16]{0:T(128)} %teacher_ref.3) | copy-start | bytes 196
  102.6 21.5 %collective-permute-start.7 = (bf16[608,768]{1,0:T(8,128)(2,1)}, bf16[608,768]{1,0:T(8,128)(2,1)}, u32[]{:S(2)}, u32[]{:S(2)}) collective-permute-start(bf16[608,768]{1,0:T(8,128)(2,1)} %pad_maximum_fusion.1), channel_id=1, source_target_pairs={{0,16},{16,0},{32,48},{48,32},{64,80},{80,64},{96,112},{112,96},{1... | collective-permute-start | bytes 2801672 | tf_op jit(solution)/shard_map/ppermute | solution.py:529
  102.6 2.6 collective-permute-start.5
  103.7 1.3 collective-permute-start.4
  112.9 0.6 copy-start.7
  113.6 0.6 copy-start.14
  114.2 12.8 %copy-start.12 = (bf16[128,64]{1,0:T(8,128)(2,1)}, bf16[128,64]{1,0:T(8,128)(2,1)S(1)}, u32[]{:S(2)}) copy-start(bf16[128,64]{1,0:T(8,128)(2,1)S(1)} %get-tuple-element.113.x_ref) | copy-start | bytes 49156
  114.2 14.1 %all-to-all-start.4 = ((bf16[4,32,2432]{2,1,0:T(8,128)(2,1)}), bf16[4,32,2432]{2,1,0:T(8,128)(2,1)S(1)}, u32[]{:S(2)}, u32[]{:S(2)}) async-start(bf16[4,32,2432]{2,1,0:T(8,128)(2,1)} %bitcast.63), calls=%async_computation.4 | async-start | bytes 1245184 | tf_op jit(solution)/shard_map/all_to_all | solution.py:75
  127.0 41.9 %collective-permute-start.8 = (bf16[1216,768]{1,0:T(8,128)(2,1)}, bf16[1216,768]{1,0:T(8,128)(2,1)}, u32[]{:S(2)}, u32[]{:S(2)}) collective-permute-start(bf16[1216,768]{1,0:T(8,128)(2,1)} %pad_maximum_fusion.near), channel_id=1, source_target_pairs={{0,48},{16,32},{32,16},{48,0},{64,112},{80,96},{96,80},{112,64},{1... | collective-permute-start | bytes 5603336 | tf_op jit(solution)/shard_map/ppermute | solution.py:831
  152.5 23.6 %copy-start.19 = (s32[1,2]{1,0:T(1,128)S(1)}, s32[1,2]{1,0:T(1,128)}, u32[]{:S(2)}) copy-start(s32[1,2]{1,0:T(1,128)} %param.20) | copy-start | bytes 28
  164.5 0.7 copy-start.4
  165.2 10.9 %all-to-all-start.7 = ((bf16[4,32,2432]{2,1,0:T(8,128)(2,1)}), bf16[4,32,2432]{2,1,0:T(8,128)(2,1)S(1)}, u32[]{:S(2)}, u32[]{:S(2)}) async-start(bf16[4,32,2432]{2,1,0:T(8,128)(2,1)} %get-tuple-element.92), calls=%async_computation.7 | async-start | bytes 1245184 | tf_op jit(solution)/shard_map/all_to_all | solution.py:75
  176.1 16.6 %copy-start.5 = (bf16[32,2432]{1,0:T(8,128)(2,1)S(1)}, bf16[32,2432]{1,0:T(8,128)(2,1)}, u32[]{:S(2)}) copy-start(bf16[32,2432]{1,0:T(8,128)(2,1)} %copy-done.4) | copy-start | bytes 466948
  193.9 0.7 copy-start.2
  194.6 10.9 %all-to-all-start.9 = ((bf16[4,32,2432]{2,1,0:T(8,128)(2,1)}), bf16[4,32,2432]{2,1,0:T(8,128)(2,1)S(1)}, u32[]{:S(2)}, u32[]{:S(2)}) async-start(bf16[4,32,2432]{2,1,0:T(8,128)(2,1)} %get-tuple-element.103), calls=%async_computation.9 | async-start | bytes 1245184 | tf_op jit(solution)/shard_map/all_to_all | solution.py:75
  203.8 0.6 copy-start.9
  205.5 21.8 %copy-start.3 = (f32[32,2432]{1,0:T(8,128)S(1)}, f32[32,2432]{1,0:T(8,128)}, u32[]{:S(2)}) copy-start(f32[32,2432]{1,0:T(8,128)} %copy-done.2) | copy-start | bytes 933892
  227.3 4.9 %copy-start.15 = (bf16[128,64]{1,0:T(8,128)(2,1)S(1)}, bf16[128,64]{1,0:T(8,128)(2,1)}, u32[]{:S(2)}) copy-start(bf16[128,64]{1,0:T(8,128)(2,1)} %copy-done.14) | copy-start | bytes 49156
  227.3 15.1 %copy-start.8 = (f32[128,128]{1,0:T(8,128)S(1)}, f32[128,128]{1,0:T(8,128)}, u32[]{:S(2)}) copy-start(f32[128,128]{1,0:T(8,128)} %copy-done.7) | copy-start | bytes 196612
  227.3 15.1 %copy-start.10 = (f32[128,128]{1,0:T(8,128)S(1)}, f32[128,128]{1,0:T(8,128)}, u32[]{:S(2)}) copy-start(f32[128,128]{1,0:T(8,128)} %copy-done.9) | copy-start | bytes 196612
  227.4 15.1 %copy-start.13 = (bf16[128,64]{1,0:T(8,128)(2,1)S(1)}, bf16[128,64]{1,0:T(8,128)(2,1)}, u32[]{:S(2)}) copy-start(bf16[128,64]{1,0:T(8,128)(2,1)} %copy-done.12) | copy-start | bytes 49156
  228.7 13.7 %all-to-all-start.11 = ((bf16[4,32,2432]{2,1,0:T(8,128)(2,1)}), bf16[4,32,2432]{2,1,0:T(8,128)(2,1)S(1)}, u32[]{:S(2)}, u32[]{:S(2)}) async-start(bf16[4,32,2432]{2,1,0:T(8,128)(2,1)} %get-tuple-element.109), calls=%async_computation.11 | async-start | bytes 1245184 | tf_op jit(solution)/shard_map/all_to_all | solution.py:75
  232.2 10.1 %collective-permute-start.9 = (bf16[128,64]{1,0:T(8,128)(2,1)S(1)}, bf16[128,64]{1,0:T(8,128)(2,1)S(1)}, u32[]{:S(2)}, u32[]{:S(2)}) collective-permute-start(bf16[128,64]{1,0:T(8,128)(2,1)S(1)} %copy-done.15), channel_id=1, source_target_pairs={{0,2},{2,0},{1,3},{3,1},{4,6},{6,4},{5,7},{7,5},{8,10},{10,8},{9,1... | collective-permute-start | bytes 49160 | tf_op jit(solution)/shard_map/ppermute | solution.py:71
  251.9 17.5 %all-to-all-start.12 = ((f32[8,72,128]{2,1,0:T(8,128)}), f32[8,72,128]{2,1,0:T(8,128)S(1)}, u32[]{:S(2)}, u32[]{:S(2)}) async-start(f32[8,72,128]{2,1,0:T(8,128)} %first_backward.1), calls=%async_computation.12 | async-start | bytes 589824 | tf_op jit(solution)/shard_map/all_to_all | solution.py:930

commit v5 on v4

--- a/solution.py
+++ b/solution.py
@@ -405,28 +405,23 @@
 
 
 def modulation_kernel(
-    cond_s_ref, cond_t_ref, s_mod, t_mod, in_s, in_t, out_proj, head, out, proj_ref, head_out,
-    s_ref, t_ref, stack_ref, head_ref, out_ref, head_all, sems
+    cond_s_ref, cond_t_ref, s_ref, t_ref, head_ref, in_s, in_t, out_proj, out, proj_ref, head_all,
+    stack_ref, out_ref, sems
 ):
     samples = cond_t_ref.shape[0]
     cells = in_s.shape[0]
-    hidden = s_mod.shape[1]
+    hidden = s_ref.shape[1]
     stream = Stream(
-        [(head, head_ref), (s_mod, s_ref), (t_mod, t_ref)]
-        + [
+        [
             (source, stack_ref.at[pl.ds(index * cells, cells)])
             for index, source in enumerate((in_s, in_t, out_proj))
         ],
         sems,
     )
-    stream.next()
     head_all[:, : head_ref.shape[1]] = head_ref[...]
     head_all[:, head_ref.shape[1] :] = jnp.zeros(
         (head_ref.shape[0], head_all.shape[1] - head_ref.shape[1]), BF
     )
-    keep = pltpu.make_async_copy(head_all, head_out, sems.at[6])
-    keep.start()
-    stream.next()
 
     def product(cond, weight):
         extent = cond.shape[0]
@@ -444,18 +439,16 @@
         return ((row // 8 == col) & (row % 8 == first)).astype(BF)
 
     total = dot(place(16, LAYERS, True), product(cond_s_ref[...], s_ref[...]))
-    stream.next()
     for layer in range(LAYERS):
         part = product(cond_t_ref[...], t_ref[layer])
         total = total + dot(place(samples, layer, False), part)
     out_ref[:, :hidden] = total.astype(BF)
     out_ref[:, hidden:] = jnp.zeros((samples * 8, out_ref.shape[1] - hidden), BF)
-    send = pltpu.make_async_copy(out_ref, out, sems.at[7])
+    send = pltpu.make_async_copy(out_ref, out, sems.at[3])
     send.start()
     for _ in range(3):
         stream.next()
     proj_ref[...] = turned_wide(stack_ref[...]).astype(BF)
-    keep.wait()
     send.wait()
 
 
@@ -661,21 +654,17 @@
             cond_t,
             s_mod,
             t_mod,
+            d_w1,
             in_proj_s,
             in_proj_t,
             out_proj,
-            d_w1,
         ),
-        far=6,
-        far_out=(0, 2),
+        far=3,
+        far_out=(0,),
         scratch=(
-            pltpu.VMEM(s_mod.shape, BF),
-            pltpu.VMEM(t_mod.shape, BF),
             pltpu.VMEM((3 * cells, columns), BF),
-            pltpu.VMEM(d_w1.shape, BF),
             pltpu.VMEM((samples * 8, mod_wide), BF),
-            pltpu.VMEM((rows, head_wide), BF),
-            pltpu.SemaphoreType.DMA((8,)),
+            pltpu.SemaphoreType.DMA((4,)),
         ),
     )
     mod_part, projections, where, places, head_block, picks = lax.optimization_barrier(

time: 271 us -> 273 us (level)
    unnamed x46 -> x52, local copies, waits for them, and re-layouts: 4.92 us -> 6.95 us
  transfers between devices with their start and end apart: 18 -> 18, of which waited for: 10 -> 10; matrix products, arithmetic and copies ran while one was open for 4% -> 3% of each run, Pallas kernels for 14% -> 13%
where the time goes in v5:
time: 273 us; the launch traced here: 272 us
  blocking collectives  74.4 us (27%)
  Pallas kernels  70.4 us (26%)
  starting transfers between devices  56.8 us (21%)
  waiting for transfers between devices  52.8 us (19%)
  other arithmetic  8.3 us (3%)
  local copies, waits for them, and re-layouts  7.68 us (3%)
    pallas_call x16, Pallas kernels, here(): pl.pallas_call(kernel, name=name, out_shape=shapes if many else shapes[0]...  70.4 us
    all_to_all x4, blocking collectives, swap_y(): return lax.all_to_all(values, 'y', 0, 0)  44.5 us
    all_gather x1, blocking collectives, body(): gathered = lax.all_gather(packed, TP, axis=0, tiled=False)  16.5 us
    all_to_all x1, waiting for transfers between devices, body(): lax.all_to_all(parts.reshape(samples, piece, both_wide), SAMPLE, 0, 0)  15.5 us
    all_to_all x4, starting transfers between devices, swap_y(): return lax.all_to_all(values, 'y', 0, 0)  14.1 us
    all_to_all x1, blocking collectives, body(): velocity = lax.all_to_all(velocity, TP, 0, 0)  13.4 us
    ppermute x6, starting transfers between devices, sibling(): return lax.ppermute(values, 'core', [(0, 1), (1, 0)])  12.2 us
    all_to_all x1, starting transfers between devices, body(): lax.all_to_all(final, TP, 0, 0)  10.6 us
  transfers between devices with their start and end apart: 18, of which 10 were waited for; matrix products, arithmetic and copies ran while one was open for 3% of the time, Pallas kernels for 13%

profile of v5, /device:TPU:1, one launch (start us, length us, event | category | flops | bytes accessed | tf_op | source)
XLA Modules:
  0.0 271.8 jit_solution(12261565480328341175)
XLA Ops:
  0.8 0.7 convert_element_type.29
  2.0 1.1 copy-done
  3.1 1.0 copy-done.3
  4.1 0.9 copy-done.9
  5.0 1.5 modulation.1
  6.5 8.6 %all-to-all-start = ((bf16[16,8,1024]{2,1,0:T(8,128)(2,1)}), bf16[16,8,1024]{2,1,0:T(8,128)(2,1)S(1)}, u32[]{:S(2)}, u32[]{:S(2)}) async-start(bf16[16,8,1024]{2,1,0:T(8,128)(2,1)} %bitcast.67), calls=%async_computation | async-start | bytes 524288 | tf_op jit(solution)/shard_map/all_to_all | solution.py:674
  15.1 1.0 collective-permute-start
  16.1 1.0 collective-permute-done
  17.1 1.6 collective-permute-start.1
  18.7 4.0 %all-to-all-done = bf16[16,8,1024]{2,1,0:T(8,128)(2,1)S(1)} async-done(((bf16[16,8,1024]{2,1,0:T(8,128)(2,1)}), bf16[16,8,1024]{2,1,0:T(8,128)(2,1)S(1)}, u32[]{:S(2)}, u32[]{:S(2)}) %all-to-all-start) | async-done | bytes 262176 | tf_op jit(solution)/shard_map/all_to_all | solution.py:674
  23.2 16.5 %all-gather = bf16[2432,210]{1,0:T(8,128)(2,1)S(1)} all-gather(bf16[304,210]{1,0:T(8,128)(2,1)S(1)} %pad_maximum_fusion.3), channel_id=2, replica_groups=mesh['fsdp'=8,'y'=4,'core'=2,'grp'=2] {'y','core'}, dimensions={0}, use_global_device_ids=true | all-gather | bytes 1149120 | tf_op jit(solution)/shard_map/all_gather | solution.py:680
  39.7 3.1 %product.1 = (bf16[256,2560]{1,0:T(8,128)(2,1)}, bf16[8,1216]{1,0:T(8,128)(2,1)S(1)}) custom-call(s32[8]{0:T(128)S(1)} %stack.55.at_ref, bf16[8,304,210]{2,1,0:T(8,128)(2,1)S(1)} %bitcast.42, bf16[152,1216]{1,0:T(8,128)(2,1)S(1)} %copy-done.1, bf16[152,1216]{1,0:T(8,128)(2,1)S(1)} %bitcast.50), custom_call_target="tpu_custom_call" | custom-call | tf_op jit(solution)/shard_map/product/pallas_call | solution.py:581
  42.8 0.2 collective-permute-start.2
  43.1 0.4 collective-permute-start.3
  43.4 3.7 %all-to-all-start.1 = ((bf16[16,16,2560]{2,1,0:T(8,128)(2,1)}), bf16[16,16,2560]{2,1,0:T(8,128)(2,1)S(1)}, u32[]{:S(2)}, u32[]{:S(2)}) async-start(bf16[16,16,2560]{2,1,0:T(8,128)(2,1)} %bitcast.62), calls=%async_computation.1 | async-start | bytes 2621440 | tf_op jit(solution)/shard_map/all_to_all | solution.py:704
  47.1 5.8 %first_product.1 = (f32[72,1216]{1,0:T(8,128)S(1)}, f32[8,2432]{1,0:T(8,128)S(1)}) custom-call(bf16[8,304,210]{2,1,0:T(8,128)(2,1)S(1)} %bitcast.43, bf16[2,1216,2432]{2,1,0:T(8,128)(2,1)} %bitcast.57), custom_call_target="tpu_custom_call" | custom-call | tf_op jit(solution)/shard_map/first_product/pallas_call | solution.py:581
  53.0 15.5 %all-to-all-done.1.parts_ref = bf16[16,16,2560]{2,1,0:T(8,128)(2,1)S(1)} async-done(((bf16[16,16,2560]{2,1,0:T(8,128)(2,1)}), bf16[16,16,2560]{2,1,0:T(8,128)(2,1)S(1)}, u32[]{:S(2)}, u32[]{:S(2)}) %all-to-all-start.1) | async-done | bytes 1310752 | tf_op jit(solution)/shard_map/all_to_all | solution.py:704
  68.5 1.9 select.4
  70.4 4.2 %all-to-all-start.2 = ((bf16[16,8,2560]{2,1,0:T(8,128)(2,1)}), bf16[16,8,2560]{2,1,0:T(8,128)(2,1)S(1)}, u32[]{:S(2)}, u32[]{:S(2)}) async-start(bf16[16,8,2560]{2,1,0:T(8,128)(2,1)} %bitcast.60), calls=%async_computation.2 | async-start | bytes 1310720 | tf_op jit(solution)/shard_map/all_to_all | solution.py:738
  74.6 1.1 broadcast_select_fusion.1
  75.7 0.8 pad_maximum_fusion.2
  76.6 9.5 %all-to-all-done.2 = bf16[16,8,2560]{2,1,0:T(8,128)(2,1)S(1)} async-done(((bf16[16,8,2560]{2,1,0:T(8,128)(2,1)}), bf16[16,8,2560]{2,1,0:T(8,128)(2,1)S(1)}, u32[]{:S(2)}, u32[]{:S(2)}) %all-to-all-start.2) | async-done | bytes 655392 | tf_op jit(solution)/shard_map/all_to_all | solution.py:738
  86.0 0.4 collective-permute-start.6
  86.5 2.1 student.1
  88.8 13.4 %all_to_all.65 = f32[8,128,64]{1,2,0:T(8,128)S(1)} all-to-all(f32[8,128,64]{1,2,0:T(8,128)S(1)} %copy.23), channel_id=1, replica_groups=mesh['fsdp'=8,'y'=4,'core'=2,'grp'=2] {'y','core'}, dimensions={0} | all-to-all | bytes 524288 | tf_op jit(solution)/shard_map/all_to_all | solution.py:752
  102.2 2.3 pad_maximum_fusion.1
  104.4 1.1 collective-permute-start.5
  105.5 0.2 collective-permute-start.4
  105.8 1.1 collective-permute-done.4.out_sib
  106.9 0.2 copy.24.velocity_ref
  107.1 7.6 %first_forward.1 = (bf16[128,2432]{1,0:T(8,128)(2,1)}, bf16[2,128,1216]{2,1,0:T(8,128)(2,1)}, bf16[128,64]{1,0:T(8,128)(2,1)S(1)}, bf16[128,64]{1,0:T(8,128)(2,1...) custom-call(s32[4]{0:T(128)S(1)} %pad_add_fusion.where_ref, s32[16]{0:T(128)S(1)} %copy-done.21, ...), custom_call_target="tpu_custom_call" | custom-call | tf_op jit(solution)/shard_map/first_forward/pallas_call | solution.py:581
  114.8 0.6 copy-done.10
  115.4 0.6 copy-done.17
  116.0 3.5 %all-to-all-start.4 = ((bf16[4,32,2432]{2,1,0:T(8,128)(2,1)}), bf16[4,32,2432]{2,1,0:T(8,128)(2,1)S(1)}, u32[]{:S(2)}, u32[]{:S(2)}) async-start(bf16[4,32,2432]{2,1,0:T(8,128)(2,1)} %bitcast.63), calls=%async_computation.4 | async-start | bytes 1245184 | tf_op jit(solution)/shard_map/all_to_all | solution.py:75
  119.5 6.4 %collective-permute-done.7 = bf16[608,768]{1,0:T(8,128)(2,1)} collective-permute-done((bf16[608,768]{1,0:T(8,128)(2,1)}, bf16[608,768]{1,0:T(8,128)(2,1)}, u32[]{:S(2)}, u32[]{:S(2)}) %collective-permute-start.7) | collective-permute-done | bytes 933920 | tf_op jit(solution)/shard_map/ppermute | solution.py:522
  125.9 2.9 %pad_maximum_fusion.near = bf16[1216,768]{1,0:T(8,128)(2,1)} fusion(bf16[608,768]{1,0:T(8,128)(2,1)} %collective-permute-done.7, bf16[304,768]{1,0:T(8,128)(2,1)} %collective-permute-done.6, bf16[304,768]{1,0:T(8,128)(2,1)} %pad_maximum_fusion.2), kind=kLoop, calls=%fused_computation | loop fusion | flops 5603328 | bytes 3735552 | tf_op jit(solution)/shard_map/concatenate | solution.py:523
  128.8 1.3 collective-permute-start.8
  130.1 1.5 first_middle.1
  131.6 11.8 %all_to_all.66 = bf16[4,32,2432]{2,1,0:T(8,128)(2,1)S(1)} all-to-all(bf16[4,32,2432]{2,1,0:T(8,128)(2,1)} %get-tuple-element.88), channel_id=1, replica_groups=mesh['fsdp'=8,'y'=4,'core'=2,'grp'=2] {'y'}, dimensions={0} | all-to-all | bytes 1245184 | tf_op jit(solution)/shard_map/all_to_all | solution.py:75
  143.4 10.9 %forward.1 = (bf16[128,2432]{1,0:T(8,128)(2,1)}, bf16[2,128,1216]{2,1,0:T(8,128)(2,1)}) custom-call(bf16[128,2432]{1,0:T(8,128)(2,1)S(1)} %bitcast.44, f32[8,2432]{1,0:T(8,128)S(1)} %get-tuple-element.87.vector_ref, bf16[2,1216,2432]{2,1,0:T(8,128)(2,1)} %bitcast.58, bf16[2,1216,2432]{2,1,0:T(8,128)(2,1)} %collective-permute-done.2.up_sib, ...), custom_call_target="tpu_custom_call" | custom-call | tf_op jit(solution)/shard_map/forward/pallas_call | solution.py:581
  154.3 10.9 %all_to_all.67.parts_ref = bf16[4,32,2432]{2,1,0:T(8,128)(2,1)S(1)} all-to-all(bf16[4,32,2432]{2,1,0:T(8,128)(2,1)} %bitcast.65), channel_id=1, replica_groups=mesh['fsdp'=8,'y'=4,'core'=2,'grp'=2] {'y'}, dimensions={0} | all-to-all | bytes 1245184 | tf_op jit(solution)/shard_map/all_to_all | solution.py:75
  165.3 1.0 last_middle.1
  166.3 0.7 copy-done.6
  167.0 3.7 %all-to-all-start.7 = ((bf16[4,32,2432]{2,1,0:T(8,128)(2,1)}), bf16[4,32,2432]{2,1,0:T(8,128)(2,1)S(1)}, u32[]{:S(2)}, u32[]{:S(2)}) async-start(bf16[4,32,2432]{2,1,0:T(8,128)(2,1)} %get-tuple-element.92), calls=%async_computation.7 | async-start | bytes 1245184 | tf_op jit(solution)/shard_map/all_to_all | solution.py:75
  170.7 7.2 %all-to-all-done.7 = bf16[4,32,2432]{2,1,0:T(8,128)(2,1)S(1)} async-done(((bf16[4,32,2432]{2,1,0:T(8,128)(2,1)}), bf16[4,32,2432]{2,1,0:T(8,128)(2,1)S(1)}, u32[]{:S(2)}, u32[]{:S(2)}) %all-to-all-start.7) | async-done | bytes 622624 | tf_op jit(solution)/shard_map/all_to_all | solution.py:75
  177.9 5.6 %head_last.1 = (bf16[128,2432]{1,0:T(8,128)(2,1)}, f32[128,128]{1,0:T(8,128)S(1)}) custom-call(s32[2]{0:T(128)S(1)} %bitcast.54, s32[4]{0:T(128)S(1)} %pad_add_fusion.where_ref, bf16[128,2432]{1,0:T(8,128)(2,1)S(1)} %bitcast.49, f32[2,304]{1,0:T(2,128)S(1)} %copy-done.19, f32[2,304]{1,0:T(2,128)S(1)} %collective-permute-done.4.out_sib, ...), custom_call_target="tpu_custom_call" | custom-call | tf_op jit(solution)/shard_map/head_last/pallas_call | solution.py:581
  183.5 10.9 %all_to_all.68.parts_ref = bf16[4,32,2432]{2,1,0:T(8,128)(2,1)S(1)} all-to-all(bf16[4,32,2432]{2,1,0:T(8,128)(2,1)} %bitcast.64), channel_id=1, replica_groups=mesh['fsdp'=8,'y'=4,'core'=2,'grp'=2] {'y'}, dimensions={0} | all-to-all | bytes 1245184 | tf_op jit(solution)/shard_map/all_to_all | solution.py:75
  194.5 1.2 last_back.1
  195.7 0.7 copy-done.4
  196.4 3.5 %all-to-all-start.9 = ((bf16[4,32,2432]{2,1,0:T(8,128)(2,1)}), bf16[4,32,2432]{2,1,0:T(8,128)(2,1)S(1)}, u32[]{:S(2)}, u32[]{:S(2)}) async-start(bf16[4,32,2432]{2,1,0:T(8,128)(2,1)} %get-tuple-element.103), calls=%async_computation.9 | async-start | bytes 1245184 | tf_op jit(solution)/shard_map/all_to_all | solution.py:75
  199.9 5.6 %head_first.1 = (bf16[128,2432]{1,0:T(8,128)(2,1)}, f32[128,128]{1,0:T(8,128)S(1)}) custom-call(s32[2]{0:T(128)S(1)} %bitcast.55, s32[4]{0:T(128)S(1)} %pad_add_fusion.where_ref, bf16[128,2432]{1,0:T(8,128)(2,1)S(1)} %bitcast.45, f32[2,304]{1,0:T(2,128)S(1)} %copy-done.19, f32[2,304]{1,0:T(2,128)S(1)} %collective-permute-done.4.out_sib, ...), custom_call_target="tpu_custom_call" | custom-call | tf_op jit(solution)/shard_map/head_first/pallas_call | solution.py:581
  205.6 0.6 copy-done.12
  206.2 1.1 all-to-all-done.9
  207.3 10.8 %backward.1 = bf16[128,2432]{1,0:T(8,128)(2,1)} custom-call(bf16[128,2432]{1,0:T(8,128)(2,1)S(1)} %bitcast.47, f32[8,2432]{1,0:T(8,128)S(1)} %get-tuple-element.87.vector_ref, bf16[2,128,1216]{2,1,0:T(8,128)(2,1)} %get-tuple-element.104.slope, bf16[128,2432]{1,0:T(8,128)(2,1)} %get-tuple-element.108.head, bf16[2,1216,2432]{2,1,0:T(8,128)(2,1)} %bitcast.59, ...), custom_call_target="tpu_custom_call" | custom-call | tf_op jit(solution)/shard_map/backward/pallas_call | solution.py:581
  218.2 10.9 %all_to_all.69.parts_ref = bf16[4,32,2432]{2,1,0:T(8,128)(2,1)S(1)} all-to-all(bf16[4,32,2432]{2,1,0:T(8,128)(2,1)} %bitcast.61), channel_id=1, replica_groups=mesh['fsdp'=8,'y'=4,'core'=2,'grp'=2] {'y'}, dimensions={0} | all-to-all | bytes 1245184 | tf_op jit(solution)/shard_map/all_to_all | solution.py:75
  229.1 1.4 first_back.1
  230.5 3.5 %all-to-all-start.11 = ((bf16[4,32,2432]{2,1,0:T(8,128)(2,1)}), bf16[4,32,2432]{2,1,0:T(8,128)(2,1)S(1)}, u32[]{:S(2)}, u32[]{:S(2)}) async-start(bf16[4,32,2432]{2,1,0:T(8,128)(2,1)} %get-tuple-element.109), calls=%async_computation.11 | async-start | bytes 1245184 | tf_op jit(solution)/shard_map/all_to_all | solution.py:75
  234.0 9.3 %collective-permute-start.9 = (bf16[128,64]{1,0:T(8,128)(2,1)S(1)}, bf16[128,64]{1,0:T(8,128)(2,1)S(1)}, u32[]{:S(2)}, u32[]{:S(2)}) collective-permute-start(bf16[128,64]{1,0:T(8,128)(2,1)S(1)} %copy-done.18), channel_id=1, source_target_pairs={{0,2},{2,0},{1,3},{3,1},{4,6},{6,4},{5,7},{7,5},{8,10},{10,8},{9,1... | collective-permute-start | bytes 49160 | tf_op jit(solution)/shard_map/ppermute | solution.py:71
  243.3 0.9 collective-permute-done.9
  244.2 9.5 %first_backward.1 = f32[8,72,128]{2,1,0:T(8,128)} custom-call(s32[4]{0:T(128)S(1)} %pad_add_fusion.where_ref, s32[16]{0:T(128)S(1)} %copy-done.20, bf16[128,2432]{1,0:T(8,128)(2,1)S(1)} %bitcast.48, bf16[128,64]{1,0:T(8,128)(2,1)S(1)} %copy-done.16, f32[128,128]{1,0:T(8,128)S(1)} %copy-done.11, f32[128,128]{1,0:T(8,128)S(1)} %copy-done.13, ...), custom_call_target="tpu_custom_call" | custom-call | tf_op jit(solution)/shard_map/first_backward/pallas_call | solution.py:581
  253.7 10.6 %all-to-all-start.12 = ((f32[8,72,128]{2,1,0:T(8,128)}), f32[8,72,128]{2,1,0:T(8,128)S(1)}, u32[]{:S(2)}, u32[]{:S(2)}) async-start(f32[8,72,128]{2,1,0:T(8,128)} %first_backward.1), calls=%async_computation.12 | async-start | bytes 589824 | tf_op jit(solution)/shard_map/all_to_all | solution.py:919
  264.3 0.7 copy.25
  265.0 6.1 %all-to-all-done.12.parts_ref = f32[8,72,128]{2,1,0:T(8,128)S(1)} async-done(((f32[8,72,128]{2,1,0:T(8,128)}), f32[8,72,128]{2,1,0:T(8,128)S(1)}, u32[]{:S(2)}, u32[]{:S(2)}) %all-to-all-start.12) | async-done | bytes 294944 | tf_op jit(solution)/shard_map/all_to_all | solution.py:919
  271.1 0.6 output.1
  (68 shorter events, 1.2 us)
Async XLA Ops:
  2.0 1.1 copy-start
  3.1 1.0 copy-start.3
  4.1 0.9 copy-start.9
  6.5 33.2 %copy-start.1 = (bf16[152,1216]{1,0:T(8,128)(2,1)S(1)}, bf16[152,1216]{1,0:T(8,128)(2,1)}, u32[]{:S(2)}) copy-start(bf16[152,1216]{1,0:T(8,128)(2,1)} %w1_ref.1) | copy-start | bytes 1108996
  6.5 33.2 %copy-start.2 = (bf16[1216,152]{0,1:T(8,128)(2,1)S(1)}, bf16[1216,152]{0,1:T(8,128)(2,1)}, u32[]{:S(2)}) copy-start(bf16[1216,152]{0,1:T(8,128)(2,1)} %param.26) | copy-start | bytes 1108996
  6.5 16.3 %all-to-all-start = ((bf16[16,8,1024]{2,1,0:T(8,128)(2,1)}), bf16[16,8,1024]{2,1,0:T(8,128)(2,1)S(1)}, u32[]{:S(2)}, u32[]{:S(2)}) async-start(bf16[16,8,1024]{2,1,0:T(8,128)(2,1)} %bitcast.67), calls=%async_computation | async-start | bytes 524288 | tf_op jit(solution)/shard_map/all_to_all | solution.py:674
  15.1 2.0 collective-permute-start
  17.1 25.7 %copy-start.23 = (bf16[152,768]{1,0:T(8,128)(2,1)}, bf16[152,768]{1,0:T(8,128)(2,1)S(1)}, u32[]{:S(2)}) copy-start(bf16[152,768]{1,0:T(8,128)(2,1)S(1)} %constant_dynamic-update-slice_fusion) | copy-start | bytes 700420
  17.1 22.6 %collective-permute-start.1 = (bf16[152,768]{1,0:T(8,128)(2,1)S(1)}, bf16[152,768]{1,0:T(8,128)(2,1)S(1)}, u32[]{:S(2)}, u32[]{:S(2)}) collective-permute-start(bf16[152,768]{1,0:T(8,128)(2,1)S(1)} %constant_dynamic-update-slice_fusion), channel_id=1, source_target_pairs={{0,1},{1,0},{2,3},{3,2},{4,5},{5,4},{6,7},{7,6},{8,9},{9,8},{10,11... | collective-permute-start | bytes 700424 | tf_op jit(solution)/shard_map/ppermute | solution.py:679
  39.7 3.7 %copy-start.24 = (bf16[152,768]{1,0:T(8,128)(2,1)}, bf16[152,768]{1,0:T(8,128)(2,1)S(1)}, u32[]{:S(2)}) copy-start(bf16[152,768]{1,0:T(8,128)(2,1)S(1)} %collective-permute-done.1) | copy-start | bytes 700420
  42.8 64.0 %collective-permute-start.2 = (bf16[2,1216,2432]{2,1,0:T(8,128)(2,1)}, bf16[2,1216,2432]{2,1,0:T(8,128)(2,1)}, u32[]{:S(2)}, u32[]{:S(2)}) collective-permute-start(bf16[2,1216,2432]{2,1,0:T(8,128)(2,1)} %bitcast.56), channel_id=1, source_target_pairs={{0,2},{2,0},{1,3},{3,1},{4,6},{6,4},{5,7},{7,5},{8,10},{10,8},{9,1... | collective-permute-start | bytes 35487752 | tf_op jit(solution)/shard_map/ppermute | solution.py:71
  43.1 63.8 %collective-permute-start.3 = (bf16[2,1216,2432]{2,1,0:T(8,128)(2,1)}, bf16[2,1216,2432]{2,1,0:T(8,128)(2,1)}, u32[]{:S(2)}, u32[]{:S(2)}) collective-permute-start(bf16[2,1216,2432]{2,1,0:T(8,128)(2,1)} %own.1), channel_id=1, source_target_pairs={{0,2},{2,0},{1,3},{3,1},{4,6},{6,4},{5,7},{7,5},{8,10},{10,8},{9,1... | collective-permute-start | bytes 35487752 | tf_op jit(solution)/shard_map/ppermute | solution.py:71
  43.4 25.0 %all-to-all-start.1 = ((bf16[16,16,2560]{2,1,0:T(8,128)(2,1)}), bf16[16,16,2560]{2,1,0:T(8,128)(2,1)S(1)}, u32[]{:S(2)}, u32[]{:S(2)}) async-start(bf16[16,16,2560]{2,1,0:T(8,128)(2,1)} %bitcast.62), calls=%async_computation.1 | async-start | bytes 2621440 | tf_op jit(solution)/shard_map/all_to_all | solution.py:704
  47.1 21.3 %copy-start.21 = (s32[16]{0:T(128)S(1)}, s32[16]{0:T(128)}, u32[]{:S(2)}) copy-start(s32[16]{0:T(128)} %student_ref.1) | copy-start | bytes 196
  70.4 16.1 %copy-start.8 = (bf16[1,256,64]{1,2,0:T(8,128)(2,1)S(1)}, bf16[1,256,64]{1,2,0:T(8,128)(2,1)}, u32[]{:S(2)}) copy-start(bf16[1,256,64]{1,2,0:T(8,128)(2,1)} %param.16) | copy-start | bytes 98308
  70.4 15.6 %all-to-all-start.2 = ((bf16[16,8,2560]{2,1,0:T(8,128)(2,1)}), bf16[16,8,2560]{2,1,0:T(8,128)(2,1)S(1)}, u32[]{:S(2)}, u32[]{:S(2)}) async-start(bf16[16,8,2560]{2,1,0:T(8,128)(2,1)} %bitcast.60), calls=%async_computation.2 | async-start | bytes 1310720 | tf_op jit(solution)/shard_map/all_to_all | solution.py:738
  86.0 16.1 %collective-permute-start.6 = (bf16[304,768]{1,0:T(8,128)(2,1)}, bf16[304,768]{1,0:T(8,128)(2,1)}, u32[]{:S(2)}, u32[]{:S(2)}) collective-permute-start(bf16[304,768]{1,0:T(8,128)(2,1)} %pad_maximum_fusion.2), channel_id=1, source_target_pairs={{0,64},{16,80},{32,96},{48,112},{64,0},{80,16},{96,32},{112,48},{1... | collective-permute-start | bytes 1400840 | tf_op jit(solution)/shard_map/ppermute | solution.py:751
  88.6 17.0 %copy-start.19 = (f32[2,304]{1,0:T(2,128)S(1)}, f32[2,304]{1,0:T(2,128)}, u32[]{:S(2)}) copy-start(f32[2,304]{1,0:T(2,128)} %out_own.1) | copy-start | bytes 7300
  88.6 18.5 %copy-start.14 = (bf16[1,256,64]{1,2,0:T(8,128)(2,1)S(1)}, bf16[1,256,64]{1,2,0:T(8,128)(2,1)}, u32[]{:S(2)}) copy-start(bf16[1,256,64]{1,2,0:T(8,128)(2,1)} %param.19) | copy-start | bytes 98308
  88.6 18.5 %copy-start.20 = (s32[16]{0:T(128)S(1)}, s32[16]{0:T(128)}, u32[]{:S(2)}) copy-start(s32[16]{0:T(128)} %teacher_ref.3) | copy-start | bytes 196
  104.4 21.5 %collective-permute-start.7 = (bf16[608,768]{1,0:T(8,128)(2,1)}, bf16[608,768]{1,0:T(8,128)(2,1)}, u32[]{:S(2)}, u32[]{:S(2)}) collective-permute-start(bf16[608,768]{1,0:T(8,128)(2,1)} %pad_maximum_fusion.1), channel_id=1, source_target_pairs={{0,16},{16,0},{32,48},{48,32},{64,80},{80,64},{96,112},{112,96},{1... | collective-permute-start | bytes 2801672 | tf_op jit(solution)/shard_map/ppermute | solution.py:522
  104.4 2.6 collective-permute-start.5
  105.5 1.3 collective-permute-start.4
  114.7 0.6 copy-start.10
  115.4 0.6 copy-start.17
  116.0 12.8 %copy-start.15 = (bf16[128,64]{1,0:T(8,128)(2,1)}, bf16[128,64]{1,0:T(8,128)(2,1)S(1)}, u32[]{:S(2)}) copy-start(bf16[128,64]{1,0:T(8,128)(2,1)S(1)} %get-tuple-element.113.x_ref) | copy-start | bytes 49156
  116.0 14.1 %all-to-all-start.4 = ((bf16[4,32,2432]{2,1,0:T(8,128)(2,1)}), bf16[4,32,2432]{2,1,0:T(8,128)(2,1)S(1)}, u32[]{:S(2)}, u32[]{:S(2)}) async-start(bf16[4,32,2432]{2,1,0:T(8,128)(2,1)} %bitcast.63), calls=%async_computation.4 | async-start | bytes 1245184 | tf_op jit(solution)/shard_map/all_to_all | solution.py:75
  128.8 41.9 %collective-permute-start.8 = (bf16[1216,768]{1,0:T(8,128)(2,1)}, bf16[1216,768]{1,0:T(8,128)(2,1)}, u32[]{:S(2)}, u32[]{:S(2)}) collective-permute-start(bf16[1216,768]{1,0:T(8,128)(2,1)} %pad_maximum_fusion.near), channel_id=1, source_target_pairs={{0,48},{16,32},{32,16},{48,0},{64,112},{80,96},{96,80},{112,64},{1... | collective-permute-start | bytes 5603336 | tf_op jit(solution)/shard_map/ppermute | solution.py:820
  154.3 23.6 %copy-start.22 = (s32[1,2]{1,0:T(1,128)S(1)}, s32[1,2]{1,0:T(1,128)}, u32[]{:S(2)}) copy-start(s32[1,2]{1,0:T(1,128)} %param.20) | copy-start | bytes 28
  166.3 0.7 copy-start.6
  167.0 10.9 %all-to-all-start.7 = ((bf16[4,32,2432]{2,1,0:T(8,128)(2,1)}), bf16[4,32,2432]{2,1,0:T(8,128)(2,1)S(1)}, u32[]{:S(2)}, u32[]{:S(2)}) async-start(bf16[4,32,2432]{2,1,0:T(8,128)(2,1)} %get-tuple-element.92), calls=%async_computation.7 | async-start | bytes 1245184 | tf_op jit(solution)/shard_map/all_to_all | solution.py:75
  177.9 16.6 %copy-start.7 = (bf16[32,2432]{1,0:T(8,128)(2,1)S(1)}, bf16[32,2432]{1,0:T(8,128)(2,1)}, u32[]{:S(2)}) copy-start(bf16[32,2432]{1,0:T(8,128)(2,1)} %copy-done.6) | copy-start | bytes 466948
  195.7 0.7 copy-start.4
  196.4 10.9 %all-to-all-start.9 = ((bf16[4,32,2432]{2,1,0:T(8,128)(2,1)}), bf16[4,32,2432]{2,1,0:T(8,128)(2,1)S(1)}, u32[]{:S(2)}, u32[]{:S(2)}) async-start(bf16[4,32,2432]{2,1,0:T(8,128)(2,1)} %get-tuple-element.103), calls=%async_computation.9 | async-start | bytes 1245184 | tf_op jit(solution)/shard_map/all_to_all | solution.py:75
  205.5 0.6 copy-start.12
  207.3 21.8 %copy-start.5 = (f32[32,2432]{1,0:T(8,128)S(1)}, f32[32,2432]{1,0:T(8,128)}, u32[]{:S(2)}) copy-start(f32[32,2432]{1,0:T(8,128)} %copy-done.4) | copy-start | bytes 933892
  229.1 4.9 %copy-start.18 = (bf16[128,64]{1,0:T(8,128)(2,1)S(1)}, bf16[128,64]{1,0:T(8,128)(2,1)}, u32[]{:S(2)}) copy-start(bf16[128,64]{1,0:T(8,128)(2,1)} %copy-done.17) | copy-start | bytes 49156
  229.1 15.1 %copy-start.11 = (f32[128,128]{1,0:T(8,128)S(1)}, f32[128,128]{1,0:T(8,128)}, u32[]{:S(2)}) copy-start(f32[128,128]{1,0:T(8,128)} %copy-done.10) | copy-start | bytes 196612
  229.1 15.1 %copy-start.13 = (f32[128,128]{1,0:T(8,128)S(1)}, f32[128,128]{1,0:T(8,128)}, u32[]{:S(2)}) copy-start(f32[128,128]{1,0:T(8,128)} %copy-done.12) | copy-start | bytes 196612
  229.1 15.1 %copy-start.16 = (bf16[128,64]{1,0:T(8,128)(2,1)S(1)}, bf16[128,64]{1,0:T(8,128)(2,1)}, u32[]{:S(2)}) copy-start(bf16[128,64]{1,0:T(8,128)(2,1)} %copy-done.15) | copy-start | bytes 49156
  230.5 13.7 %all-to-all-start.11 = ((bf16[4,32,2432]{2,1,0:T(8,128)(2,1)}), bf16[4,32,2432]{2,1,0:T(8,128)(2,1)S(1)}, u32[]{:S(2)}, u32[]{:S(2)}) async-start(bf16[4,32,2432]{2,1,0:T(8,128)(2,1)} %get-tuple-element.109), calls=%async_computation.11 | async-start | bytes 1245184 | tf_op jit(solution)/shard_map/all_to_all | solution.py:75
  234.0 10.1 %collective-permute-start.9 = (bf16[128,64]{1,0:T(8,128)(2,1)S(1)}, bf16[128,64]{1,0:T(8,128)(2,1)S(1)}, u32[]{:S(2)}, u32[]{:S(2)}) collective-permute-start(bf16[128,64]{1,0:T(8,128)(2,1)S(1)} %copy-done.18), channel_id=1, source_target_pairs={{0,2},{2,0},{1,3},{3,1},{4,6},{6,4},{5,7},{7,5},{8,10},{10,8},{9,1... | collective-permute-start | bytes 49160 | tf_op jit(solution)/shard_map/ppermute | solution.py:71
  253.7 17.4 %all-to-all-start.12 = ((f32[8,72,128]{2,1,0:T(8,128)}), f32[8,72,128]{2,1,0:T(8,128)S(1)}, u32[]{:S(2)}, u32[]{:S(2)}) async-start(f32[8,72,128]{2,1,0:T(8,128)} %first_backward.1), calls=%async_computation.12 | async-start | bytes 589824 | tf_op jit(solution)/shard_map/all_to_all | solution.py:919

commit v6 on v4

--- a/solution.py
+++ b/solution.py
@@ -898,7 +898,7 @@
         far_out=(1,),
         scratch=(quarter_rows, four),
     )
-    dy_0, latents = lax.optimization_barrier((swap_y(dy_0).reshape(half, width), latents))
+    dy_0, latents = lax.optimization_barrier((swap_y(dy_0).reshape(half, width), latents.T))
     final = here(
         first_backward_kernel,
         "first_backward",
@@ -929,7 +929,7 @@
         (array((cells, seq), F32), array((heads, seq), F32)),
         (lax.all_to_all(final, TP, 0, 0),),
     )
-    return (latents[None], scores[None], grad.T[None])
+    return (latents.T[None], scores[None], grad.T[None])
 
 
 def solution(mesh):

time: 271 us -> 271 us (level)
  no operation moved by 1% of the time
where the time goes in v6:
time: 271 us; the launch traced here: 270 us
  blocking collectives  74.4 us (27%)
  Pallas kernels  71.6 us (26%)
  starting transfers between devices  56.8 us (21%)
  waiting for transfers between devices  51.9 us (19%)
  other arithmetic  8.27 us (3%)
  local copies, waits for them, and re-layouts  5.65 us (2%)
    pallas_call x16, Pallas kernels, here(): pl.pallas_call(kernel, name=name, out_shape=shapes if many else shapes[0]...  71.6 us
    all_to_all x4, blocking collectives, swap_y(): return lax.all_to_all(values, 'y', 0, 0)  44.5 us
    all_gather x1, blocking collectives, body(): gathered = lax.all_gather(packed, TP, axis=0, tiled=False)  16.5 us
    all_to_all x1, waiting for transfers between devices, body(): lax.all_to_all(parts.reshape(samples, piece, both_wide), SAMPLE, 0, 0)  15.5 us
    all_to_all x4, starting transfers between devices, swap_y(): return lax.all_to_all(values, 'y', 0, 0)  14.1 us
    all_to_all x1, blocking collectives, body(): velocity = lax.all_to_all(velocity, TP, 0, 0)  13.4 us
    ppermute x6, starting transfers between devices, sibling(): return lax.ppermute(values, 'core', [(0, 1), (1, 0)])  12.2 us
    all_to_all x1, starting transfers between devices, body(): lax.all_to_all(final, TP, 0, 0)  10.6 us
  transfers between devices with their start and end apart: 18, of which 10 were waited for; matrix products, arithmetic and copies ran while one was open for 4% of the time, Pallas kernels for 14%

profile of v6, /device:TPU:1, one launch (start us, length us, event | category | flops | bytes accessed | tf_op | source)
XLA Modules:
  0.0 270.0 jit_solution(8746831633720355961)
XLA Ops:
  0.8 0.7 convert_element_type.29
  1.6 0.2 fusion.1.cond_t_ref
  2.0 2.6 modulation.1
  4.7 8.6 %all-to-all-start = ((bf16[16,8,1024]{2,1,0:T(8,128)(2,1)}), bf16[16,8,1024]{2,1,0:T(8,128)(2,1)S(1)}, u32[]{:S(2)}, u32[]{:S(2)}) async-start(bf16[16,8,1024]{2,1,0:T(8,128)(2,1)} %bitcast.71), calls=%async_computation | async-start | bytes 524288 | tf_op jit(solution)/shard_map/all_to_all | solution.py:685
  13.3 1.0 collective-permute-start
  14.3 0.9 constant_dynamic-update-slice_fusion.1
  15.2 0.3 collective-permute-done
  15.5 1.6 collective-permute-start.1
  17.2 3.8 %all-to-all-done = bf16[16,8,1024]{2,1,0:T(8,128)(2,1)S(1)} async-done(((bf16[16,8,1024]{2,1,0:T(8,128)(2,1)}), bf16[16,8,1024]{2,1,0:T(8,128)(2,1)S(1)}, u32[]{:S(2)}, u32[]{:S(2)}) %all-to-all-start) | async-done | bytes 262176 | tf_op jit(solution)/shard_map/all_to_all | solution.py:685
  21.4 16.5 %all-gather = bf16[2432,210]{1,0:T(8,128)(2,1)S(1)} all-gather(bf16[304,210]{1,0:T(8,128)(2,1)S(1)} %pad_maximum_fusion.3), channel_id=2, replica_groups=mesh['fsdp'=8,'y'=4,'core'=2,'grp'=2] {'y','core'}, dimensions={0}, use_global_device_ids=true | all-gather | bytes 1149120 | tf_op jit(solution)/shard_map/all_gather | solution.py:691
  37.9 3.1 %product.1 = (bf16[256,2560]{1,0:T(8,128)(2,1)}, bf16[8,1216]{1,0:T(8,128)(2,1)S(1)}) custom-call(s32[8]{0:T(128)S(1)} %stack.55.at_ref, bf16[8,304,210]{2,1,0:T(8,128)(2,1)S(1)} %bitcast.46, bf16[152,1216]{1,0:T(8,128)(2,1)S(1)} %copy-done, bf16[152,1216]{1,0:T(8,128)(2,1)S(1)} %bitcast.54), custom_call_target="tpu_custom_call" | custom-call | tf_op jit(solution)/shard_map/product/pallas_call | solution.py:588
  41.1 0.2 collective-permute-start.2
  41.3 0.4 collective-permute-start.3
  41.7 3.7 %all-to-all-start.1 = ((bf16[16,16,2560]{2,1,0:T(8,128)(2,1)}), bf16[16,16,2560]{2,1,0:T(8,128)(2,1)S(1)}, u32[]{:S(2)}, u32[]{:S(2)}) async-start(bf16[16,16,2560]{2,1,0:T(8,128)(2,1)} %bitcast.66), calls=%async_computation.1 | async-start | bytes 2621440 | tf_op jit(solution)/shard_map/all_to_all | solution.py:715
  45.4 5.8 %first_product.1 = (f32[72,1216]{1,0:T(8,128)S(1)}, f32[8,2432]{1,0:T(8,128)S(1)}) custom-call(bf16[8,304,210]{2,1,0:T(8,128)(2,1)S(1)} %bitcast.47, bf16[2,1216,2432]{2,1,0:T(8,128)(2,1)} %bitcast.61), custom_call_target="tpu_custom_call" | custom-call | tf_op jit(solution)/shard_map/first_product/pallas_call | solution.py:588
  51.2 15.5 %all-to-all-done.1.parts_ref = bf16[16,16,2560]{2,1,0:T(8,128)(2,1)S(1)} async-done(((bf16[16,16,2560]{2,1,0:T(8,128)(2,1)}), bf16[16,16,2560]{2,1,0:T(8,128)(2,1)S(1)}, u32[]{:S(2)}, u32[]{:S(2)}) %all-to-all-start.1) | async-done | bytes 1310752 | tf_op jit(solution)/shard_map/all_to_all | solution.py:715
  66.7 1.9 select.4
  68.6 4.2 %all-to-all-start.2 = ((bf16[16,8,2560]{2,1,0:T(8,128)(2,1)}), bf16[16,8,2560]{2,1,0:T(8,128)(2,1)S(1)}, u32[]{:S(2)}, u32[]{:S(2)}) async-start(bf16[16,8,2560]{2,1,0:T(8,128)(2,1)} %bitcast.64), calls=%async_computation.2 | async-start | bytes 1310720 | tf_op jit(solution)/shard_map/all_to_all | solution.py:749
  72.9 1.1 broadcast_select_fusion.1
  74.0 0.8 pad_maximum_fusion.2
  74.8 9.4 %all-to-all-done.2 = bf16[16,8,2560]{2,1,0:T(8,128)(2,1)S(1)} async-done(((bf16[16,8,2560]{2,1,0:T(8,128)(2,1)}), bf16[16,8,2560]{2,1,0:T(8,128)(2,1)S(1)}, u32[]{:S(2)}, u32[]{:S(2)}) %all-to-all-start.2) | async-done | bytes 655392 | tf_op jit(solution)/shard_map/all_to_all | solution.py:749
  84.2 0.4 collective-permute-start.6
  84.7 2.1 student.1
  86.8 0.2 copy.23
  87.0 13.4 %all_to_all.65 = f32[8,128,64]{1,2,0:T(8,128)S(1)} all-to-all(f32[8,128,64]{1,2,0:T(8,128)S(1)} %copy.23), channel_id=1, replica_groups=mesh['fsdp'=8,'y'=4,'core'=2,'grp'=2] {'y','core'}, dimensions={0} | all-to-all | bytes 524288 | tf_op jit(solution)/shard_map/all_to_all | solution.py:763
  100.4 2.2 pad_maximum_fusion.1
  102.6 1.1 collective-permute-start.5
  103.7 0.2 collective-permute-start.4
  103.9 1.1 collective-permute-done.4.out_sib
  105.0 0.2 copy.24.velocity_ref
  105.3 7.6 %first_forward.1 = (bf16[128,2432]{1,0:T(8,128)(2,1)}, bf16[2,128,1216]{2,1,0:T(8,128)(2,1)}, bf16[128,64]{1,0:T(8,128)(2,1)S(1)}, bf16[128,64]{1,0:T(8,128)(2,1...) custom-call(s32[4]{0:T(128)S(1)} %pad_add_fusion.where_ref, s32[16]{0:T(128)S(1)} %copy-done.18, ...), custom_call_target="tpu_custom_call" | custom-call | tf_op jit(solution)/shard_map/first_forward/pallas_call | solution.py:588
  112.9 0.6 copy-done.7
  113.6 0.6 copy-done.14
  114.2 3.5 %all-to-all-start.4 = ((bf16[4,32,2432]{2,1,0:T(8,128)(2,1)}), bf16[4,32,2432]{2,1,0:T(8,128)(2,1)S(1)}, u32[]{:S(2)}, u32[]{:S(2)}) async-start(bf16[4,32,2432]{2,1,0:T(8,128)(2,1)} %bitcast.67), calls=%async_computation.4 | async-start | bytes 1245184 | tf_op jit(solution)/shard_map/all_to_all | solution.py:75
  117.7 6.4 %collective-permute-done.7 = bf16[608,768]{1,0:T(8,128)(2,1)} collective-permute-done((bf16[608,768]{1,0:T(8,128)(2,1)}, bf16[608,768]{1,0:T(8,128)(2,1)}, u32[]{:S(2)}, u32[]{:S(2)}) %collective-permute-start.7) | collective-permute-done | bytes 933920 | tf_op jit(solution)/shard_map/ppermute | solution.py:529
  124.1 2.9 %pad_maximum_fusion.near = bf16[1216,768]{1,0:T(8,128)(2,1)} fusion(bf16[608,768]{1,0:T(8,128)(2,1)} %collective-permute-done.7, bf16[304,768]{1,0:T(8,128)(2,1)} %collective-permute-done.6, bf16[304,768]{1,0:T(8,128)(2,1)} %pad_maximum_fusion.2), kind=kLoop, calls=%fused_computation | loop fusion | flops 5603328 | bytes 3735552 | tf_op jit(solution)/shard_map/concatenate | solution.py:530
  127.0 1.3 collective-permute-start.8
  128.2 1.5 first_middle.1
  129.8 11.8 %all_to_all.66 = bf16[4,32,2432]{2,1,0:T(8,128)(2,1)S(1)} all-to-all(bf16[4,32,2432]{2,1,0:T(8,128)(2,1)} %get-tuple-element.88), channel_id=1, replica_groups=mesh['fsdp'=8,'y'=4,'core'=2,'grp'=2] {'y'}, dimensions={0} | all-to-all | bytes 1245184 | tf_op jit(solution)/shard_map/all_to_all | solution.py:75
  141.5 11.0 %forward.1 = (bf16[128,2432]{1,0:T(8,128)(2,1)}, bf16[2,128,1216]{2,1,0:T(8,128)(2,1)}) custom-call(bf16[128,2432]{1,0:T(8,128)(2,1)S(1)} %bitcast.48, f32[8,2432]{1,0:T(8,128)S(1)} %get-tuple-element.87.vector_ref, bf16[2,1216,2432]{2,1,0:T(8,128)(2,1)} %bitcast.62, bf16[2,1216,2432]{2,1,0:T(8,128)(2,1)} %collective-permute-done.2.up_sib, ...), custom_call_target="tpu_custom_call" | custom-call | tf_op jit(solution)/shard_map/forward/pallas_call | solution.py:588
  152.5 10.9 %all_to_all.67.parts_ref = bf16[4,32,2432]{2,1,0:T(8,128)(2,1)S(1)} all-to-all(bf16[4,32,2432]{2,1,0:T(8,128)(2,1)} %bitcast.69), channel_id=1, replica_groups=mesh['fsdp'=8,'y'=4,'core'=2,'grp'=2] {'y'}, dimensions={0} | all-to-all | bytes 1245184 | tf_op jit(solution)/shard_map/all_to_all | solution.py:75
  163.4 1.1 last_middle.1
  164.5 0.6 copy-done.4
  165.2 3.7 %all-to-all-start.7 = ((bf16[4,32,2432]{2,1,0:T(8,128)(2,1)}), bf16[4,32,2432]{2,1,0:T(8,128)(2,1)S(1)}, u32[]{:S(2)}, u32[]{:S(2)}) async-start(bf16[4,32,2432]{2,1,0:T(8,128)(2,1)} %get-tuple-element.92), calls=%async_computation.7 | async-start | bytes 1245184 | tf_op jit(solution)/shard_map/all_to_all | solution.py:75
  168.9 7.2 %all-to-all-done.7 = bf16[4,32,2432]{2,1,0:T(8,128)(2,1)S(1)} async-done(((bf16[4,32,2432]{2,1,0:T(8,128)(2,1)}), bf16[4,32,2432]{2,1,0:T(8,128)(2,1)S(1)}, u32[]{:S(2)}, u32[]{:S(2)}) %all-to-all-start.7) | async-done | bytes 622624 | tf_op jit(solution)/shard_map/all_to_all | solution.py:75
  176.1 5.7 %head_last.1 = (bf16[128,2432]{1,0:T(8,128)(2,1)}, f32[128,128]{1,0:T(8,128)S(1)}) custom-call(s32[2]{0:T(128)S(1)} %bitcast.58, s32[4]{0:T(128)S(1)} %pad_add_fusion.where_ref, bf16[128,2432]{1,0:T(8,128)(2,1)S(1)} %bitcast.53, f32[2,304]{1,0:T(2,128)S(1)} %copy-done.16, f32[2,304]{1,0:T(2,128)S(1)} %collective-permute-done.4.out_sib, ...), custom_call_target="tpu_custom_call" | custom-call | tf_op jit(solution)/shard_map/head_last/pallas_call | solution.py:588
  181.8 10.9 %all_to_all.68.parts_ref = bf16[4,32,2432]{2,1,0:T(8,128)(2,1)S(1)} all-to-all(bf16[4,32,2432]{2,1,0:T(8,128)(2,1)} %bitcast.68), channel_id=1, replica_groups=mesh['fsdp'=8,'y'=4,'core'=2,'grp'=2] {'y'}, dimensions={0} | all-to-all | bytes 1245184 | tf_op jit(solution)/shard_map/all_to_all | solution.py:75
  192.7 1.2 last_back.1
  193.9 0.7 copy-done.2
  194.6 3.5 %all-to-all-start.9 = ((bf16[4,32,2432]{2,1,0:T(8,128)(2,1)}), bf16[4,32,2432]{2,1,0:T(8,128)(2,1)S(1)}, u32[]{:S(2)}, u32[]{:S(2)}) async-start(bf16[4,32,2432]{2,1,0:T(8,128)(2,1)} %get-tuple-element.103), calls=%async_computation.9 | async-start | bytes 1245184 | tf_op jit(solution)/shard_map/all_to_all | solution.py:75
  198.1 5.7 %head_first.1 = (bf16[128,2432]{1,0:T(8,128)(2,1)}, f32[128,128]{1,0:T(8,128)S(1)}) custom-call(s32[2]{0:T(128)S(1)} %bitcast.59, s32[4]{0:T(128)S(1)} %pad_add_fusion.where_ref, bf16[128,2432]{1,0:T(8,128)(2,1)S(1)} %bitcast.49, f32[2,304]{1,0:T(2,128)S(1)} %copy-done.16, f32[2,304]{1,0:T(2,128)S(1)} %collective-permute-done.4.out_sib, ...), custom_call_target="tpu_custom_call" | custom-call | tf_op jit(solution)/shard_map/head_first/pallas_call | solution.py:588
  203.8 0.6 copy-done.9
  204.4 1.1 all-to-all-done.9
  205.6 10.9 %backward.1 = bf16[128,2432]{1,0:T(8,128)(2,1)} custom-call(bf16[128,2432]{1,0:T(8,128)(2,1)S(1)} %bitcast.51, f32[8,2432]{1,0:T(8,128)S(1)} %get-tuple-element.87.vector_ref, bf16[2,128,1216]{2,1,0:T(8,128)(2,1)} %get-tuple-element.104.slope, bf16[128,2432]{1,0:T(8,128)(2,1)} %get-tuple-element.108.head, bf16[2,1216,2432]{2,1,0:T(8,128)(2,1)} %bitcast.63, ...), custom_call_target="tpu_custom_call" | custom-call | tf_op jit(solution)/shard_map/backward/pallas_call | solution.py:588
  216.4 10.9 %all_to_all.69.parts_ref = bf16[4,32,2432]{2,1,0:T(8,128)(2,1)S(1)} all-to-all(bf16[4,32,2432]{2,1,0:T(8,128)(2,1)} %bitcast.65), channel_id=1, replica_groups=mesh['fsdp'=8,'y'=4,'core'=2,'grp'=2] {'y'}, dimensions={0} | all-to-all | bytes 1245184 | tf_op jit(solution)/shard_map/all_to_all | solution.py:75
  227.4 1.4 first_back.1
  228.7 3.5 %all-to-all-start.11 = ((bf16[4,32,2432]{2,1,0:T(8,128)(2,1)}), bf16[4,32,2432]{2,1,0:T(8,128)(2,1)S(1)}, u32[]{:S(2)}, u32[]{:S(2)}) async-start(bf16[4,32,2432]{2,1,0:T(8,128)(2,1)} %get-tuple-element.109), calls=%async_computation.11 | async-start | bytes 1245184 | tf_op jit(solution)/shard_map/all_to_all | solution.py:75
  232.2 9.3 %collective-permute-start.9 = (bf16[128,64]{1,0:T(8,128)(2,1)S(1)}, bf16[128,64]{1,0:T(8,128)(2,1)S(1)}, u32[]{:S(2)}, u32[]{:S(2)}) collective-permute-start(bf16[128,64]{1,0:T(8,128)(2,1)S(1)} %copy-done.15), channel_id=1, source_target_pairs={{0,2},{2,0},{1,3},{3,1},{4,6},{6,4},{5,7},{7,5},{8,10},{10,8},{9,1... | collective-permute-start | bytes 49160 | tf_op jit(solution)/shard_map/ppermute | solution.py:71
  241.5 0.9 collective-permute-done.9
  242.4 9.5 %first_backward.1 = f32[8,72,128]{2,1,0:T(8,128)} custom-call(s32[4]{0:T(128)S(1)} %pad_add_fusion.where_ref, s32[16]{0:T(128)S(1)} %copy-done.17, bf16[128,2432]{1,0:T(8,128)(2,1)S(1)} %bitcast.52, bf16[128,64]{1,0:T(8,128)(2,1)S(1)} %copy-done.13, f32[128,128]{1,0:T(8,128)S(1)} %copy-done.8, f32[128,128]{1,0:T(8,128)S(1)} %copy-done.10, ...), custom_call_target="tpu_custom_call" | custom-call | tf_op jit(solution)/shard_map/first_backward/pallas_call | solution.py:588
  251.9 10.6 %all-to-all-start.12 = ((f32[8,72,128]{2,1,0:T(8,128)}), f32[8,72,128]{2,1,0:T(8,128)S(1)}, u32[]{:S(2)}, u32[]{:S(2)}) async-start(f32[8,72,128]{2,1,0:T(8,128)} %first_backward.1), calls=%async_computation.12 | async-start | bytes 589824 | tf_op jit(solution)/shard_map/all_to_all | solution.py:930
  262.6 0.7 copy.25
  263.3 6.1 %all-to-all-done.12.parts_ref = f32[8,72,128]{2,1,0:T(8,128)S(1)} async-done(((f32[8,72,128]{2,1,0:T(8,128)}), f32[8,72,128]{2,1,0:T(8,128)S(1)}, u32[]{:S(2)}, u32[]{:S(2)}) %all-to-all-start.12) | async-done | bytes 294944 | tf_op jit(solution)/shard_map/all_to_all | solution.py:930
  269.4 0.6 output.1
  (62 shorter events, 0.9 us)
Async XLA Ops:
  4.7 33.3 %copy-start = (bf16[152,1216]{1,0:T(8,128)(2,1)S(1)}, bf16[152,1216]{1,0:T(8,128)(2,1)}, u32[]{:S(2)}) copy-start(bf16[152,1216]{1,0:T(8,128)(2,1)} %w1_ref.1) | copy-start | bytes 1108996
  4.7 33.2 %copy-start.1 = (bf16[1216,152]{0,1:T(8,128)(2,1)S(1)}, bf16[1216,152]{0,1:T(8,128)(2,1)}, u32[]{:S(2)}) copy-start(bf16[1216,152]{0,1:T(8,128)(2,1)} %param.26) | copy-start | bytes 1108996
  4.7 16.3 %all-to-all-start = ((bf16[16,8,1024]{2,1,0:T(8,128)(2,1)}), bf16[16,8,1024]{2,1,0:T(8,128)(2,1)S(1)}, u32[]{:S(2)}, u32[]{:S(2)}) async-start(bf16[16,8,1024]{2,1,0:T(8,128)(2,1)} %bitcast.71), calls=%async_computation | async-start | bytes 524288 | tf_op jit(solution)/shard_map/all_to_all | solution.py:685
  13.3 2.2 collective-permute-start
  15.5 25.5 %copy-start.20 = (bf16[152,768]{1,0:T(8,128)(2,1)}, bf16[152,768]{1,0:T(8,128)(2,1)S(1)}, u32[]{:S(2)}) copy-start(bf16[152,768]{1,0:T(8,128)(2,1)S(1)} %constant_dynamic-update-slice_fusion) | copy-start | bytes 700420
  15.5 22.4 %collective-permute-start.1 = (bf16[152,768]{1,0:T(8,128)(2,1)S(1)}, bf16[152,768]{1,0:T(8,128)(2,1)S(1)}, u32[]{:S(2)}, u32[]{:S(2)}) collective-permute-start(bf16[152,768]{1,0:T(8,128)(2,1)S(1)} %constant_dynamic-update-slice_fusion), channel_id=1, source_target_pairs={{0,1},{1,0},{2,3},{3,2},{4,5},{5,4},{6,7},{7,6},{8,9},{9,8},{10,11... | collective-permute-start | bytes 700424 | tf_op jit(solution)/shard_map/ppermute | solution.py:690
  37.9 3.7 %copy-start.21 = (bf16[152,768]{1,0:T(8,128)(2,1)}, bf16[152,768]{1,0:T(8,128)(2,1)S(1)}, u32[]{:S(2)}) copy-start(bf16[152,768]{1,0:T(8,128)(2,1)S(1)} %collective-permute-done.1) | copy-start | bytes 700420
  41.1 64.0 %collective-permute-start.2 = (bf16[2,1216,2432]{2,1,0:T(8,128)(2,1)}, bf16[2,1216,2432]{2,1,0:T(8,128)(2,1)}, u32[]{:S(2)}, u32[]{:S(2)}) collective-permute-start(bf16[2,1216,2432]{2,1,0:T(8,128)(2,1)} %bitcast.60), channel_id=1, source_target_pairs={{0,2},{2,0},{1,3},{3,1},{4,6},{6,4},{5,7},{7,5},{8,10},{10,8},{9,1... | collective-permute-start | bytes 35487752 | tf_op jit(solution)/shard_map/ppermute | solution.py:71
  41.3 63.8 %collective-permute-start.3 = (bf16[2,1216,2432]{2,1,0:T(8,128)(2,1)}, bf16[2,1216,2432]{2,1,0:T(8,128)(2,1)}, u32[]{:S(2)}, u32[]{:S(2)}) collective-permute-start(bf16[2,1216,2432]{2,1,0:T(8,128)(2,1)} %own.1), channel_id=1, source_target_pairs={{0,2},{2,0},{1,3},{3,1},{4,6},{6,4},{5,7},{7,5},{8,10},{10,8},{9,1... | collective-permute-start | bytes 35487752 | tf_op jit(solution)/shard_map/ppermute | solution.py:71
  41.7 25.0 %all-to-all-start.1 = ((bf16[16,16,2560]{2,1,0:T(8,128)(2,1)}), bf16[16,16,2560]{2,1,0:T(8,128)(2,1)S(1)}, u32[]{:S(2)}, u32[]{:S(2)}) async-start(bf16[16,16,2560]{2,1,0:T(8,128)(2,1)} %bitcast.66), calls=%async_computation.1 | async-start | bytes 2621440 | tf_op jit(solution)/shard_map/all_to_all | solution.py:715
  45.4 21.3 %copy-start.18 = (s32[16]{0:T(128)S(1)}, s32[16]{0:T(128)}, u32[]{:S(2)}) copy-start(s32[16]{0:T(128)} %student_ref.1) | copy-start | bytes 196
  68.6 16.1 %copy-start.6 = (bf16[1,256,64]{1,2,0:T(8,128)(2,1)S(1)}, bf16[1,256,64]{1,2,0:T(8,128)(2,1)}, u32[]{:S(2)}) copy-start(bf16[1,256,64]{1,2,0:T(8,128)(2,1)} %param.16) | copy-start | bytes 98308
  68.6 15.6 %all-to-all-start.2 = ((bf16[16,8,2560]{2,1,0:T(8,128)(2,1)}), bf16[16,8,2560]{2,1,0:T(8,128)(2,1)S(1)}, u32[]{:S(2)}, u32[]{:S(2)}) async-start(bf16[16,8,2560]{2,1,0:T(8,128)(2,1)} %bitcast.64), calls=%async_computation.2 | async-start | bytes 1310720 | tf_op jit(solution)/shard_map/all_to_all | solution.py:749
  84.2 16.1 %collective-permute-start.6 = (bf16[304,768]{1,0:T(8,128)(2,1)}, bf16[304,768]{1,0:T(8,128)(2,1)}, u32[]{:S(2)}, u32[]{:S(2)}) collective-permute-start(bf16[304,768]{1,0:T(8,128)(2,1)} %pad_maximum_fusion.2), channel_id=1, source_target_pairs={{0,64},{16,80},{32,96},{48,112},{64,0},{80,16},{96,32},{112,48},{1... | collective-permute-start | bytes 1400840 | tf_op jit(solution)/shard_map/ppermute | solution.py:762
  86.8 16.9 %copy-start.16 = (f32[2,304]{1,0:T(2,128)S(1)}, f32[2,304]{1,0:T(2,128)}, u32[]{:S(2)}) copy-start(f32[2,304]{1,0:T(2,128)} %out_own.1) | copy-start | bytes 7300
  86.8 18.5 %copy-start.11 = (bf16[1,256,64]{1,2,0:T(8,128)(2,1)S(1)}, bf16[1,256,64]{1,2,0:T(8,128)(2,1)}, u32[]{:S(2)}) copy-start(bf16[1,256,64]{1,2,0:T(8,128)(2,1)} %param.19) | copy-start | bytes 98308
  86.8 18.5 %copy-start.17 = (s32[16]{0:T(128)S(1)}, s32[16]{0:T(128)}, u32[]{:S(2)}) copy-start(s32[16]{0:T(128)} %teacher_ref.3) | copy-start | bytes 196
  102.6 21.5 %collective-permute-start.7 = (bf16[608,768]{1,0:T(8,128)(2,1)}, bf16[608,768]{1,0:T(8,128)(2,1)}, u32[]{:S(2)}, u32[]{:S(2)}) collective-permute-start(bf16[608,768]{1,0:T(8,128)(2,1)} %pad_maximum_fusion.1), channel_id=1, source_target_pairs={{0,16},{16,0},{32,48},{48,32},{64,80},{80,64},{96,112},{112,96},{1... | collective-permute-start | bytes 2801672 | tf_op jit(solution)/shard_map/ppermute | solution.py:529
  102.6 2.6 collective-permute-start.5
  103.7 1.3 collective-permute-start.4
  112.9 0.6 copy-start.7
  113.6 0.6 copy-start.14
  114.2 12.8 %copy-start.12 = (bf16[128,64]{1,0:T(8,128)(2,1)}, bf16[128,64]{1,0:T(8,128)(2,1)S(1)}, u32[]{:S(2)}) copy-start(bf16[128,64]{1,0:T(8,128)(2,1)S(1)} %get-tuple-element.113.x_ref) | copy-start | bytes 49156
  114.2 14.1 %all-to-all-start.4 = ((bf16[4,32,2432]{2,1,0:T(8,128)(2,1)}), bf16[4,32,2432]{2,1,0:T(8,128)(2,1)S(1)}, u32[]{:S(2)}, u32[]{:S(2)}) async-start(bf16[4,32,2432]{2,1,0:T(8,128)(2,1)} %bitcast.67), calls=%async_computation.4 | async-start | bytes 1245184 | tf_op jit(solution)/shard_map/all_to_all | solution.py:75
  127.0 41.9 %collective-permute-start.8 = (bf16[1216,768]{1,0:T(8,128)(2,1)}, bf16[1216,768]{1,0:T(8,128)(2,1)}, u32[]{:S(2)}, u32[]{:S(2)}) collective-permute-start(bf16[1216,768]{1,0:T(8,128)(2,1)} %pad_maximum_fusion.near), channel_id=1, source_target_pairs={{0,48},{16,32},{32,16},{48,0},{64,112},{80,96},{96,80},{112,64},{1... | collective-permute-start | bytes 5603336 | tf_op jit(solution)/shard_map/ppermute | solution.py:831
  152.5 23.6 %copy-start.19 = (s32[1,2]{1,0:T(1,128)S(1)}, s32[1,2]{1,0:T(1,128)}, u32[]{:S(2)}) copy-start(s32[1,2]{1,0:T(1,128)} %param.20) | copy-start | bytes 28
  164.5 0.7 copy-start.4
  165.2 10.9 %all-to-all-start.7 = ((bf16[4,32,2432]{2,1,0:T(8,128)(2,1)}), bf16[4,32,2432]{2,1,0:T(8,128)(2,1)S(1)}, u32[]{:S(2)}, u32[]{:S(2)}) async-start(bf16[4,32,2432]{2,1,0:T(8,128)(2,1)} %get-tuple-element.92), calls=%async_computation.7 | async-start | bytes 1245184 | tf_op jit(solution)/shard_map/all_to_all | solution.py:75
  176.1 16.6 %copy-start.5 = (bf16[32,2432]{1,0:T(8,128)(2,1)S(1)}, bf16[32,2432]{1,0:T(8,128)(2,1)}, u32[]{:S(2)}) copy-start(bf16[32,2432]{1,0:T(8,128)(2,1)} %copy-done.4) | copy-start | bytes 466948
  193.9 0.7 copy-start.2
  194.6 10.9 %all-to-all-start.9 = ((bf16[4,32,2432]{2,1,0:T(8,128)(2,1)}), bf16[4,32,2432]{2,1,0:T(8,128)(2,1)S(1)}, u32[]{:S(2)}, u32[]{:S(2)}) async-start(bf16[4,32,2432]{2,1,0:T(8,128)(2,1)} %get-tuple-element.103), calls=%async_computation.9 | async-start | bytes 1245184 | tf_op jit(solution)/shard_map/all_to_all | solution.py:75
  203.8 0.6 copy-start.9
  205.5 21.8 %copy-start.3 = (f32[32,2432]{1,0:T(8,128)S(1)}, f32[32,2432]{1,0:T(8,128)}, u32[]{:S(2)}) copy-start(f32[32,2432]{1,0:T(8,128)} %copy-done.2) | copy-start | bytes 933892
  227.3 4.9 %copy-start.15 = (bf16[128,64]{1,0:T(8,128)(2,1)S(1)}, bf16[128,64]{1,0:T(8,128)(2,1)}, u32[]{:S(2)}) copy-start(bf16[128,64]{1,0:T(8,128)(2,1)} %copy-done.14) | copy-start | bytes 49156
  227.3 15.1 %copy-start.8 = (f32[128,128]{1,0:T(8,128)S(1)}, f32[128,128]{1,0:T(8,128)}, u32[]{:S(2)}) copy-start(f32[128,128]{1,0:T(8,128)} %copy-done.7) | copy-start | bytes 196612
  227.3 15.1 %copy-start.10 = (f32[128,128]{1,0:T(8,128)S(1)}, f32[128,128]{1,0:T(8,128)}, u32[]{:S(2)}) copy-start(f32[128,128]{1,0:T(8,128)} %copy-done.9) | copy-start | bytes 196612
  227.4 15.1 %copy-start.13 = (bf16[128,64]{1,0:T(8,128)(2,1)S(1)}, bf16[128,64]{1,0:T(8,128)(2,1)}, u32[]{:S(2)}) copy-start(bf16[128,64]{1,0:T(8,128)(2,1)} %copy-done.12) | copy-start | bytes 49156
  228.7 13.7 %all-to-all-start.11 = ((bf16[4,32,2432]{2,1,0:T(8,128)(2,1)}), bf16[4,32,2432]{2,1,0:T(8,128)(2,1)S(1)}, u32[]{:S(2)}, u32[]{:S(2)}) async-start(bf16[4,32,2432]{2,1,0:T(8,128)(2,1)} %get-tuple-element.109), calls=%async_computation.11 | async-start | bytes 1245184 | tf_op jit(solution)/shard_map/all_to_all | solution.py:75
  232.2 10.1 %collective-permute-start.9 = (bf16[128,64]{1,0:T(8,128)(2,1)S(1)}, bf16[128,64]{1,0:T(8,128)(2,1)S(1)}, u32[]{:S(2)}, u32[]{:S(2)}) collective-permute-start(bf16[128,64]{1,0:T(8,128)(2,1)S(1)} %copy-done.15), channel_id=1, source_target_pairs={{0,2},{2,0},{1,3},{3,1},{4,6},{6,4},{5,7},{7,5},{8,10},{10,8},{9,1... | collective-permute-start | bytes 49160 | tf_op jit(solution)/shard_map/ppermute | solution.py:71
  251.9 17.5 %all-to-all-start.12 = ((f32[8,72,128]{2,1,0:T(8,128)}), f32[8,72,128]{2,1,0:T(8,128)S(1)}, u32[]{:S(2)}, u32[]{:S(2)}) async-start(f32[8,72,128]{2,1,0:T(8,128)} %first_backward.1), calls=%async_computation.12 | async-start | bytes 589824 | tf_op jit(solution)/shard_map/all_to_all | solution.py:930
